TPU v7x, 128 devices: a whole 4x4x4 slice. The times are simulated.
128 devices in a mesh: group: 64 (over z, y, x), local: 2 (over core).
Axes of the slice: x: 4, y: 4, z: 4, core: 2. Of those that a mesh axis runs over, the one named last changes fastest.
Arguments:
- tokens: bfloat16 [65536, 2048], P(('group', 'local')), may hold values from -6 to 6
- cotangent: bfloat16 [65536, 2048], P(('group', 'local')), may hold values from -6 to 6
- row_slot: int32 [65536], P(('group', 'local')), may hold values from 0 to 1
- placement: int32 [64, 2], replicated, may hold values from 0 to 7, as said below
- master: float32 [8, 3, 384, 2048], P(None, None, 'group', 'local'), may hold values from -0.125 to 0.125
- first_moment: float32 [8, 3, 384, 2048], P(None, None, 'group', 'local'), may hold values from -2 to 2
- second_moment: float32 [8, 3, 384, 2048], P(None, None, 'group', 'local'), may hold values from 1 to 1000
Outputs:
- layer_out: bfloat16 [65536, 2048], P(('group', 'local'))
- input_grad: bfloat16 [65536, 2048], P(('group', 'local'))
- new_master: float32 [8, 3, 384, 2048], P(None, None, 'group', 'local')
- new_first: float32 [8, 3, 384, 2048], P(None, None, 'group', 'local')
- new_second: float32 [8, 3, 384, 2048], P(None, None, 'group', 'local')
Inputs may be any that keep to these rules, and one draw needn't show every extreme that they name: `placement`: the 2 slots of a group name different experts; every expert is named by at least one slot.
All inputs are finite; a program needn't handle non-finite values.
Results may differ from a plain program's by a relative error of at most 0.0071.
Values may be sent and summed in bfloat16 or wider, within the bound.
No kernel may reach another device: no remote copies, remote signals or barrier semaphores. Data moves between devices by JAX's collectives and lax.ppermute only.
A program may use at most 128 MiB of HBM per device.

v0:
```python
import functools
import jax
import jax.numpy as jnp
import numpy as np
from jax import lax
from jax.experimental import pallas as pl
from jax.experimental.pallas import tpu as pltpu
from jax.sharding import PartitionSpec as P

loss_scale = 4.0
beta_first = 0.9
beta_second = 0.95
learn_rate = 0.001
adam_epsilon = 1e-08
bias_first = 1.0 - 0.9**10
bias_second = 1.0 - 0.95**10

SIDE = 4
CHAINS = 3
BOTH = ("group", "local")
SHIFTS = (4, 2, 0)
AXES = ((2, 1, 0), (1, 0, 2), (0, 2, 1))


def place(coords, core):
    return ((coords[0] * SIDE + coords[1]) * SIDE + coords[2]) * 2 + core


def step_pairs(axis, offsets):
    pairs = []
    for group in range(SIDE**3):
        for core in range(2):
            coords = [group // 16, group // 4 % 4, group % 4]
            here = place(coords, core)
            coords[axis] ^= offsets[core]
            pairs.append((here, place(coords, core)))
    return pairs


CORE_PAIRS = [(i, i ^ 1) for i in range(2 * SIDE**3)]
ONE, BACK, ACROSS = (1, 3), (3, 1), (2, 2)
STEPS = ((0, 0), ONE, BACK, ACROSS)


def hop(value, axis, offsets):
    return lax.ppermute(value, BOTH, step_pairs(axis, offsets))


def swap(value):
    return lax.ppermute(value, BOTH, CORE_PAIRS)


def contract_last(left, right):
    return lax.dot_general(
        left, right, (((1,), (1,)), ((), ())), preferred_element_type=jnp.float32
    )


def contract_first(left, right):
    return lax.dot_general(
        left, right, (((0,), (0,)), ((), ())), preferred_element_type=jnp.float32
    )


def matmul(left, right):
    return jnp.dot(left, right, preferred_element_type=jnp.float32)


VMEM = pl.BlockSpec(memory_space=pltpu.VMEM)
SMEM = pl.BlockSpec(memory_space=pltpu.SMEM)
LIMIT = pltpu.CompilerParams(vmem_limit_bytes=16 * 1024 * 1024)


def shape_of(*dims):
    return jax.ShapeDtypeStruct(dims, jnp.bfloat16)


def spots(core):
    return (0, 1 + core, 2 - core, 3)


def weave_kernel(table_ref, own, one, rest, out, turned):
    first = table_ref[8] == 0
    for m in range(3):
        for r in range(2):
            near = one[m, r].astype(jnp.float32)
            back = rest[0, m, r].astype(jnp.float32)
            turned[m, :, r] = own[m, r].astype(jnp.float32)
            turned[m, :, 2 + r] = jnp.where(first, near, back)
            turned[m, :, 4 + r] = jnp.where(first, back, near)
            turned[m, :, 6 + r] = rest[1, m, r].astype(jnp.float32)
    out[...] = turned[...].astype(jnp.bfloat16)


def weave(table, own, one, rest):
    _, _, experts, columns = own.shape
    return pl.pallas_call(
        weave_kernel,
        out_shape=shape_of(3, experts, 8, columns),
        in_specs=[SMEM] + [VMEM] * 3,
        out_specs=VMEM,
        scratch_shapes=[pltpu.VMEM((3, experts, 8, columns), jnp.float32)],
        compiler_params=LIMIT,
        name="weave",
    )(table, own, one, rest)


def unweave_kernel(table_ref, own, came, last, out, one, rest):
    first = table_ref[8] == 0
    for m in range(3):
        total = own[m].astype(jnp.float32) + came[0, m].astype(jnp.float32)
        turned = jnp.swapaxes(total + last[m].astype(jnp.float32), 0, 1)
        left = turned[2:4]
        right = turned[4:6]
        out[m] = turned[0:2]
        one[m] = jnp.where(first, left, right).astype(jnp.bfloat16)
        rest[0, m] = jnp.where(first, right, left).astype(jnp.bfloat16)
        rest[1, m] = turned[6:8].astype(jnp.bfloat16)


def unweave(table, own, came, last):
    _, experts, _, columns = own.shape
    return pl.pallas_call(
        unweave_kernel,
        out_shape=[
            jax.ShapeDtypeStruct((3, 2, experts, columns), jnp.float32),
            shape_of(3, 2, experts, columns),
            shape_of(2, 3, 2, experts, columns),
        ],
        in_specs=[SMEM] + [VMEM] * 3,
        out_specs=[VMEM] * 3,
        compiler_params=LIMIT,
        name="unweave",
    )(table, own, came, last)


def pick_kernel(table_ref, kept, one, rest, own, ahead, back):
    spot = spots(table_ref[8])
    for index, out in enumerate((own, ahead.at[0], back, ahead.at[1])):
        for k in range(2):
            e = table_ref[2 * index + k]
            for b, p in enumerate((kept, one, rest.at[0], rest.at[1])):
                out[k, :, spot[b]] = p[:, e]


def pick(table, *plane):
    columns = plane[0].shape[-1]
    return pl.pallas_call(
        pick_kernel,
        out_shape=[shape_of(*lead, 2, 3, 4, 8, columns) for lead in ((), (2,), ())],
        in_specs=[SMEM] + [VMEM] * 3,
        out_specs=[VMEM] * 3,
        compiler_params=LIMIT,
        name="pick",
    )(table, *plane)


def first_kernel(table_ref, tok0, tok1, cot0, cot1, mask, own, came, rest, sums, weights):
    core = table_ref[8]
    columns = own.shape[-1]
    rows = tok0.shape[0]
    for spot, a in zip(spots(core), (own, came.at[0], rest.at[0], rest.at[1])):
        weights[:, :, spot] = a[...]
    half = pl.ds(pl.multiple_of(core * columns, columns), columns)
    w_pair = jnp.concatenate([weights[k, 0:2].reshape(256, columns) for k in range(2)], 0)
    w_down = jnp.concatenate([weights[k, 2].reshape(128, columns) for k in range(2)], 0)
    parts = ((tok0[:, half], cot0[:, half]), (tok1[...], cot1[...]))
    for b, (tok, cot) in enumerate(parts):
        here = slice(rows * b, rows * b + rows)
        chosen = mask[here] > 0.0
        pre = contract_last(tok, w_pair)
        d_hidden = contract_last(cot, w_down)
        sums[0, here] = jnp.where(chosen, pre[:, :128], pre[:, 256:384])
        sums[1, here] = jnp.where(chosen, pre[:, 128:256], pre[:, 384:])
        sums[2, here] = jnp.where(chosen, d_hidden[:, :128], d_hidden[:, 128:])


def first(table, rows_in, mask, arrived):
    columns = arrived[0].shape[-1]
    rows = mask.shape[0]
    return pl.pallas_call(
        first_kernel,
        out_shape=[
            jax.ShapeDtypeStruct((3, rows, 128), jnp.float32),
            shape_of(2, 3, 4, 32, columns),
        ],
        in_specs=[SMEM] + [VMEM] * 8,
        out_specs=[VMEM] * 2,
        compiler_params=pltpu.CompilerParams(vmem_limit_bytes=24 * 1024 * 1024),
        name="first",
    )(table, *rows_in, mask, *arrived)


def second_kernel(
    table_ref, tok0, tok1, cot0, cot1, mask, sums, got, own, ahead, back, hidden, pair, turned
):
    core = table_ref[8]
    columns = own.shape[-1]
    rows = tok0.shape[0]
    step = 256
    for r in range(0, 2 * rows, step):
        here = slice(r, r + step)
        there = slice((r + rows) % (2 * rows), (r + rows) % (2 * rows) + step)
        gate_pre = sums[0, here] + got[0, there]
        up_pre = sums[1, here] + got[1, there]
        d_hidden = sums[2, here] + got[2, there]
        sigmoid_gate = jax.nn.sigmoid(gate_pre)
        act = gate_pre * sigmoid_gate
        d_gate = d_hidden * up_pre * sigmoid_gate * (1.0 + gate_pre * (1.0 - sigmoid_gate))
        three = (d_gate, d_hidden * act, act * up_pre)
        chosen = mask[here] > 0.0
        for k in range(2):
            for m in range(3):
                part = jnp.where(chosen, three[m], 0.0) if k == 0 else jnp.where(chosen, 0.0, three[m])
                part = part.astype(jnp.bfloat16)
                if m < 2:
                    pair[here, 256 * k + 128 * m : 256 * k + 128 * m + 128] = part
                else:
                    hidden[here, 128 * k : 128 * k + 128] = part
                line = 256 * k + 128 * m if m < 2 else 512 + 128 * k
                turned[line : line + 128, here] = part.T
    start = pl.multiple_of(core * columns, columns)
    swapped = core == 1
    for c in range(0, columns, step):
        cols = pl.ds(start + c, step)
        out_cols = slice(c, c + step)
        both = matmul(turned[:512, :rows], tok0[:, cols]) + matmul(
            turned[:512, rows:], tok1[:, out_cols]
        )
        down = matmul(turned[512:, :rows], cot0[:, cols]) + matmul(
            turned[512:, rows:], cot1[:, out_cols]
        )
        for k in range(2):
            for m in range(3):
                line = both[256 * k + 128 * m :][:128] if m < 2 else down[128 * k :][:128]
                line = line.astype(jnp.bfloat16)
                q = [line[32 * i : 32 * i + 32] for i in range(4)]
                own[k, m, :, out_cols] = q[0]
                ahead[0, k, m, :, out_cols] = jnp.where(swapped, q[2], q[1])
                back[k, m, :, out_cols] = jnp.where(swapped, q[1], q[2])
                ahead[1, k, m, :, out_cols] = q[3]


def second(table, rows_in, mask, sums, got, columns):
    rows = mask.shape[0]
    return pl.pallas_call(
        second_kernel,
        out_shape=[shape_of(*lead, 2, 3, 32, columns) for lead in ((), (2,), ())]
        + [shape_of(rows, 256), shape_of(rows, 512)],
        in_specs=[SMEM] + [VMEM] * 7,
        out_specs=[VMEM] * 5,
        scratch_shapes=[pltpu.VMEM((768, rows), jnp.bfloat16)],
        compiler_params=pltpu.CompilerParams(vmem_limit_bytes=24 * 1024 * 1024),
        name="second",
    )(table, *rows_in, mask, sums, got)


def rows_kernel(start, table_ref, *refs):
    hidden, pair, weights = refs[0:3], refs[3:6], refs[6:9]
    added, (layer_out, grad_out) = refs[9:-2], refs[-2:]
    columns = weights[0].shape[-1]
    rows = slice(start, start + layer_out.shape[0])
    step = 512
    if added:
        core = table_ref[8]
        near = pl.multiple_of(core * columns, columns)
        far = pl.ds(pl.multiple_of((1 - core) * columns, columns), columns)
        layer_out[:, far] = added[0][...]
        grad_out[:, far] = added[1][...]
    for c in range(0, columns, step):
        part = slice(c, c + step)
        cols = pl.ds(near + c, step) if added else part
        layer = 0.0
        grad = 0.0
        for chain in range(CHAINS):
            w = weights[chain]
            down = jnp.concatenate([w[k, 2, :, :, part].reshape(128, step) for k in range(2)], 0)
            layer = layer + matmul(hidden[chain][rows], down)
            for k in range(2):
                both = w[k, 0:2, :, :, part].reshape(256, step)
                grad = grad + matmul(pair[chain][rows, 256 * k : 256 * k + 256], both)
        layer_out[:, cols] = layer.astype(jnp.bfloat16)
        grad_out[:, cols] = grad.astype(jnp.bfloat16)


def rows_out(table, hidden, pair, weights, added, start):
    columns = weights[0].shape[-1]
    rows = hidden[0].shape[0] // 2
    return pl.pallas_call(
        functools.partial(rows_kernel, start),
        out_shape=[shape_of(rows, 2 * columns if added else columns)] * 2,
        in_specs=[SMEM] + [VMEM] * (9 + len(added)),
        out_specs=[VMEM] * 2,
        compiler_params=pltpu.CompilerParams(vmem_limit_bytes=24 * 1024 * 1024),
        name="rows_out",
    )(table, *hidden, *pair, *weights, *added)


def merge_kernel(table_ref, kept, came, passed, own, one, rest, total):
    spot = spots(table_ref[8])
    total[...] = jnp.zeros_like(total)
    for index, block in enumerate((kept, came.at[0], passed.at[0], passed.at[1])):
        for k in range(2):
            e = table_ref[2 * index + k]
            for p in range(4):
                total[p, :, e] += block[k, :, p].astype(jnp.float32)
    own[...] = total[0].astype(jnp.bfloat16)
    one[...] = total[spot[1]].astype(jnp.bfloat16)
    rest[0] = total[spot[2]].astype(jnp.bfloat16)
    rest[1] = total[3].astype(jnp.bfloat16)


def merge(table, came, experts):
    columns = came[0].shape[-1]
    return pl.pallas_call(
        merge_kernel,
        out_shape=[shape_of(*lead, 3, experts, 8, columns) for lead in ((), (), (2,))],
        in_specs=[SMEM] + [VMEM] * 3,
        out_specs=[VMEM] * 3,
        scratch_shapes=[pltpu.VMEM((4, 3, experts, 8, columns), jnp.float32)],
        compiler_params=LIMIT,
        name="merge",
    )(table, *[c.reshape(*c.shape[:-2], 4, 8, columns) for c in came])


def shards(tokens, cotangent, row_slot, placement, master, first_moment, second_moment):
    group = lax.axis_index("group")
    core = lax.axis_index("local")
    experts = master.shape[0]
    columns = master.shape[3]
    rows = tokens.shape[0]

    steps = np.array(
        [[[step[c] << SHIFTS[axes[2]] for step in STEPS] for axes in AXES] for c in range(2)], np.int32
    ).reshape(2, -1)
    there = group ^ jnp.where(core == 0, jnp.asarray(steps[0]), jnp.asarray(steps[1]))
    seen = there[:, None] == jnp.arange(SIDE**3)[None]
    pairs = jnp.sum(jnp.where(seen[:, :, None], placement[None], 0), 1)
    pairs = pairs.reshape(CHAINS, 2 * SIDE)
    table = jnp.concatenate([pairs, jnp.full((CHAINS, 1), core)], 1)

    narrow = master.astype(jnp.bfloat16).transpose(1, 2, 0, 3)
    near = [axes[0] for axes in AXES]
    mid = [axes[1] for axes in AXES]
    last = [axes[2] for axes in AXES]
    each = range(CHAINS)
    blocks = [narrow[:, 2 * c : 2 * c + 2] for c in each]
    ones = [hop(blocks[c], near[c], ONE) for c in each]
    both = [jnp.stack([blocks[c], ones[c]], 0) for c in each]
    rests = [hop(both[c], near[c], BACK) for c in each]
    lines = [weave(table[c], blocks[c], ones[c], rests[c]) for c in each]

    def other_rows(*rows):
        far = (1 - core) * columns
        return [lax.dynamic_slice_in_dim(v, far, columns, 1) for v in rows]

    lines[2], tokens, cotangent, row_slot = lax.optimization_barrier(
        (lines[2], tokens, cotangent, row_slot)
    )
    far_tokens, far_cotangent = other_rows(tokens, cotangent)
    rows_in = [tokens, swap(far_tokens), cotangent, swap(far_cotangent)]
    slots = jnp.concatenate([row_slot, swap(row_slot)], 0)
    chosen = jnp.broadcast_to((slots == 0)[:, None], (2 * rows, 128)).astype(jnp.float32)

    ones = [hop(lines[c], mid[c], ONE) for c in each]
    both = [jnp.stack([lines[c], ones[c]], 0) for c in each]
    rests = [hop(both[c], mid[c], BACK) for c in each]
    rests[0], rows_in, chosen = lax.optimization_barrier((rests[0], rows_in, chosen))
    packed = [pick(table[c], lines[c], ones[c], rests[c]) for c in each]

    def exchange(packed):
        came = [hop(packed[c][1], last[c], ONE) for c in each]
        both = [jnp.stack([packed[c][2], came[c][1]], 0) for c in each]
        return [(packed[c][0], came[c], hop(both[c], last[c], BACK)) for c in each]

    arrived = exchange(packed)
    blocks = [[a.reshape(*a.shape[:-3], 32, columns) for a in arrived[c]] for c in each]
    firsts = [first(table[c], rows_in, chosen, blocks[c]) for c in each]
    got = [swap(f[0]) for f in firsts]
    seconds = [
        second(table[c], rows_in, chosen, firsts[c][0], got[c], columns)
        for c in each
    ]
    weights = [f[1] for f in firsts]
    hidden = [v[3] for v in seconds]
    pair = [v[4] for v in seconds]
    sent = exchange(seconds)
    merged = [merge(table[c], sent[c], experts) for c in each]

    def add(one, came):
        return (one.astype(jnp.float32) + came[1].astype(jnp.float32)).astype(jnp.bfloat16)

    def scatter(parts, axes):
        came = [hop(parts[c][2], axes[c], BACK) for c in each]
        ones = [add(parts[c][1], came[c]) for c in each]
        return [(parts[c][0], came[c], hop(ones[c], axes[c], ONE)) for c in each]

    far_rows = rows_out(table[0], hidden, pair, weights, [], rows)
    layer_out, input_grad = rows_out(
        table[0], hidden, pair, weights, [swap(r) for r in far_rows], 0
    )
    merged = scatter(merged, mid)
    sums = [unweave(table[c], *merged[c]) for c in each]
    parts = [
        own + came[0].astype(jnp.float32) + one.astype(jnp.float32)
        for own, came, one in scatter(sums, near)
    ]

    grads = jnp.concatenate(parts, 1).transpose(2, 0, 1, 3)
    scaled = grads / loss_scale
    new_first = beta_first * first_moment + (1.0 - beta_first) * scaled
    new_second = beta_second * second_moment + (1.0 - beta_second) * scaled * scaled
    new_master = master - learn_rate * (new_first / bias_first) / (
        jnp.sqrt(new_second / bias_second) + adam_epsilon
    )

    return layer_out, input_grad, new_master, new_first, new_second


def solution(mesh):
    state = P(None, None, "group", "local")
    rows = P(("group", "local"), None)
    return jax.shard_map(
        shards,
        mesh=mesh,
        in_specs=(rows, rows, P(("group", "local")), P(), state, state, state),
        out_specs=(rows, rows, state, state, state),
        check_vma=False,
    )
```

profile of v0, /device:TPU:0, one launch (start us, length us, event | category | flops | bytes accessed | tf_op | source)
XLA Modules:
  0.0 170.5 jit_solution(8893253128437261735)
XLA Ops:
  2.5 1.7 collective-permute-start.12
  4.2 1.9 %collective-permute-start.4 = (bf16[3,2,8,1024]{3,2,1,0:T(8,128)(2,1)S(1)}, bf16[3,2,8,1024]{3,2,1,0:T(8,128)(2,1)S(1)}, u32[]{:S(2)}, u32[]{:S(2)}) collective-permute-start(bf16[3,2,8,1024]{3,2,1,0:T(8,128)(2,1)S(1)} %get-tuple-element.136.own), channel_id=1, source_target_pairs={{0,32},{1,97},{2,34},{3,99},{4,36},{5,101},{6,38},{7,103},{8,40},{... | collective-permute-start | bytes 294920 | tf_op jit(solution)/shard_map/ppermute | solution.py:46
  6.1 1.5 collective-permute-start
  8.1 2.3 %collective-permute-start.13 = (bf16[2,3,2,8,1024]{4,3,2,1,0:T(8,128)(2,1)S(1)}, bf16[2,3,2,8,1024]{4,3,2,1,0:T(8,128)(2,1)S(1)}, u32[]{:S(2)}, u32[]{:S(2)}) collective-permute-start(bf16[2,3,2,8,1024]{4,3,2,1,0:T(8,128)(2,1)S(1)} %pad_maximum_fusion.12), channel_id=1, source_target_pairs={{0,24},{1,9},{2,26},{3,11},{4,28},{5,13},{6,30},{7,15},{8,16},{9,1... | collective-permute-start | bytes 589832 | tf_op jit(solution)/shard_map/ppermute | solution.py:46
  11.0 4.0 %collective-permute-start.5 = (bf16[2,3,2,8,1024]{4,3,2,1,0:T(8,128)(2,1)}, bf16[2,3,2,8,1024]{4,3,2,1,0:T(8,128)(2,1)S(1)}, u32[]{:S(2)}, u32[]{:S(2)}) collective-permute-start(bf16[2,3,2,8,1024]{4,3,2,1,0:T(8,128)(2,1)} %pad_maximum_fusion.11), channel_id=1, source_target_pairs={{0,96},{1,33},{2,98},{3,35},{4,100},{5,37},{6,102},{7,39},{8,104},... | collective-permute-start | bytes 589832 | tf_op jit(solution)/shard_map/ppermute | solution.py:46
  17.7 2.8 %collective-permute-start.1 = (bf16[2,3,2,8,1024]{4,3,2,1,0:T(8,128)(2,1)}, bf16[2,3,2,8,1024]{4,3,2,1,0:T(8,128)(2,1)}, u32[]{:S(2)}, u32[]{:S(2)}) collective-permute-start(bf16[2,3,2,8,1024]{4,3,2,1,0:T(8,128)(2,1)} %pad_maximum_fusion.10), channel_id=1, source_target_pairs={{0,6},{1,3},{2,4},{3,1},{4,2},{5,7},{6,0},{7,5},{8,14},{9,11},{10,... | collective-permute-start | bytes 589832 | tf_op jit(solution)/shard_map/ppermute | solution.py:46
  21.3 1.4 collective-permute-start.19
  22.7 4.0 %collective-permute-done.1.rest = bf16[2,3,2,8,1024]{4,3,2,1,0:T(8,128)(2,1)} collective-permute-done((bf16[2,3,2,8,1024]{4,3,2,1,0:T(8,128)(2,1)}, bf16[2,3,2,8,1024]{4,3,2,1,0:T(8,128)(2,1)}, u32[]{:S(2)}, u32[]{:S(2)}) %collective-permute-start.1) | collective-permute-done | bytes 196640 | tf_op jit(solution)/shard_map/ppermute | solution.py:46
  28.3 3.5 %collective-permute-start.15 = (bf16[2,3,8,8,1024]{4,3,2,1,0:T(8,128)(2,1)S(1)}, bf16[2,3,8,8,1024]{4,3,2,1,0:T(8,128)(2,1)S(1)}, u32[]{:S(2)}, u32[]{:S(2)}) collective-permute-start(bf16[2,3,8,8,1024]{4,3,2,1,0:T(8,128)(2,1)S(1)} %pad_maximum_fusion.2), channel_id=1, source_target_pairs={{0,96},{1,33},{2,98},{3,35},{4,100},{5,37},{6,102},{7,39},{8,104},... | collective-permute-start | bytes 2359304 | tf_op jit(solution)/shard_map/ppermute | solution.py:46
  32.0 2.6 %collective-permute-start.20 = (bf16[2,3,8,8,1024]{4,3,2,1,0:T(8,128)(2,1)S(1)}, bf16[2,3,8,8,1024]{4,3,2,1,0:T(8,128)(2,1)S(1)}, u32[]{:S(2)}, u32[]{:S(2)}) collective-permute-start(bf16[2,3,8,8,1024]{4,3,2,1,0:T(8,128)(2,1)S(1)} %pad_maximum_fusion.4), channel_id=1, source_target_pairs={{0,6},{1,3},{2,4},{3,1},{4,2},{5,7},{6,0},{7,5},{8,14},{9,11},{10,... | collective-permute-start | bytes 2359304 | tf_op jit(solution)/shard_map/ppermute | solution.py:46
  35.9 3.6 %collective-permute-start.3 = (bf16[2,3,8,8,1024]{4,3,2,1,0:T(8,128)(2,1)S(1)}, bf16[2,3,8,8,1024]{4,3,2,1,0:T(8,128)(2,1)S(1)}, u32[]{:S(2)}, u32[]{:S(2)}) collective-permute-start(bf16[2,3,8,8,1024]{4,3,2,1,0:T(8,128)(2,1)S(1)} %pad_maximum_fusion), channel_id=1, source_target_pairs={{0,24},{1,9},{2,26},{3,11},{4,28},{5,13},{6,30},{7,15},{8,16},{9,1... | collective-permute-start | bytes 2359304 | tf_op jit(solution)/shard_map/ppermute | solution.py:46
  39.5 2.3 %collective-permute-done.15.rest = bf16[2,3,8,8,1024]{4,3,2,1,0:T(8,128)(2,1)S(1)} collective-permute-done((bf16[2,3,8,8,1024]{4,3,2,1,0:T(8,128)(2,1)S(1)}, bf16[2,3,8,8,1024]{4,3,2,1,0:T(8,128)(2,1)S(1)}, u32[]{:S(2)}, u32[]{:S(2)}) %collective-permute-start.15) | collective-permute-done | bytes 786464 | tf_op jit(solution)/shard_map/ppermute | solution.py:46
  42.8 2.9 %collective-permute-done.20.rest = bf16[2,3,8,8,1024]{4,3,2,1,0:T(8,128)(2,1)S(1)} collective-permute-done((bf16[2,3,8,8,1024]{4,3,2,1,0:T(8,128)(2,1)S(1)}, bf16[2,3,8,8,1024]{4,3,2,1,0:T(8,128)(2,1)S(1)}, u32[]{:S(2)}, u32[]{:S(2)}) %collective-permute-start.20) | collective-permute-done | bytes 786464 | tf_op jit(solution)/shard_map/ppermute | solution.py:46
  46.8 2.2 %collective-permute-start.21 = (bf16[2,2,3,4,8,1024]{5,4,3,2,1,0:T(8,128)(2,1)S(1)}, bf16[2,2,3,4,8,1024]{5,4,3,2,1,0:T(8,128)(2,1)S(1)}, u32[]{:S(2)}, u32[]{:S(2)}) collective-permute-start(bf16[2,2,3,4,8,1024]{5,4,3,2,1,0:T(8,128)(2,1)S(1)} %get-tuple-element.88), channel_id=1, source_target_pairs={{0,8},{1,25},{2,10},{3,27},{4,12},{5,29},{6,14},{7,31},{8,0},{9,17... | collective-permute-start | bytes 2359304 | tf_op jit(solution)/shard_map/ppermute | solution.py:46
  50.3 1.7 %collective-permute-start.9 = (bf16[2,2,3,4,8,1024]{5,4,3,2,1,0:T(8,128)(2,1)S(1)}, bf16[2,2,3,4,8,1024]{5,4,3,2,1,0:T(8,128)(2,1)S(1)}, u32[]{:S(2)}, u32[]{:S(2)}) collective-permute-start(bf16[2,2,3,4,8,1024]{5,4,3,2,1,0:T(8,128)(2,1)S(1)} %get-tuple-element.77), channel_id=1, source_target_pairs={{0,32},{1,97},{2,34},{3,99},{4,36},{5,101},{6,38},{7,103},{8,40},{... | collective-permute-start | bytes 2359304 | tf_op jit(solution)/shard_map/ppermute | solution.py:46
  52.0 2.4 %collective-permute-done.16 = bf16[2,2,3,4,8,1024]{5,4,3,2,1,0:T(8,128)(2,1)S(1)} collective-permute-done((bf16[2,2,3,4,8,1024]{5,4,3,2,1,0:T(8,128)(2,1)S(1)}, bf16[2,2,3,4,8,1024]{5,4,3,2,1,0:T(8,128)(2,1)S(1)}, u32[]{:S(2)}, u32[]{:S(2)}) %collective-permute-start.16) | collective-permute-done | bytes 786464 | tf_op jit(solution)/shard_map/ppermute | solution.py:46
  54.6 3.2 %collective-permute-start.17 = (bf16[2,2,3,4,8,1024]{5,4,3,2,1,0:T(8,128)(2,1)S(1)}, bf16[2,2,3,4,8,1024]{5,4,3,2,1,0:T(8,128)(2,1)S(1)}, u32[]{:S(2)}, u32[]{:S(2)}) collective-permute-start(bf16[2,2,3,4,8,1024]{5,4,3,2,1,0:T(8,128)(2,1)S(1)} %pad_maximum_fusion.3), channel_id=1, source_target_pairs={{0,6},{1,3},{2,4},{3,1},{4,2},{5,7},{6,0},{7,5},{8,14},{9,11},{10,... | collective-permute-start | bytes 2359304 | tf_op jit(solution)/shard_map/ppermute | solution.py:46
  57.8 1.2 collective-permute-done.21
  59.2 2.3 %collective-permute-start.22 = (bf16[2,2,3,4,8,1024]{5,4,3,2,1,0:T(8,128)(2,1)S(1)}, bf16[2,2,3,4,8,1024]{5,4,3,2,1,0:T(8,128)(2,1)S(1)}, u32[]{:S(2)}, u32[]{:S(2)}) collective-permute-start(bf16[2,2,3,4,8,1024]{5,4,3,2,1,0:T(8,128)(2,1)S(1)} %pad_maximum_fusion.5), channel_id=1, source_target_pairs={{0,24},{1,9},{2,26},{3,11},{4,28},{5,13},{6,30},{7,15},{8,16},{9,1... | collective-permute-start | bytes 2359304 | tf_op jit(solution)/shard_map/ppermute | solution.py:46
  62.5 12.8 %collective-permute-start.10 = (bf16[2,2,3,4,8,1024]{5,4,3,2,1,0:T(8,128)(2,1)S(1)}, bf16[2,2,3,4,8,1024]{5,4,3,2,1,0:T(8,128)(2,1)S(1)}, u32[]{:S(2)}, u32[]{:S(2)}) collective-permute-start(bf16[2,2,3,4,8,1024]{5,4,3,2,1,0:T(8,128)(2,1)S(1)} %pad_maximum_fusion.1), channel_id=1, source_target_pairs={{0,96},{1,33},{2,98},{3,35},{4,100},{5,37},{6,102},{7,39},{8,104},... | collective-permute-start | bytes 2359304 | tf_op jit(solution)/shard_map/ppermute | solution.py:46
  75.3 2.5 %first.4 = (f32[3,1024,128]{2,1,0:T(8,128)S(1)}, bf16[2,3,4,32,1024]{4,3,2,1,0:T(8,128)(2,1)S(1)}) custom-call(s32[9]{0:T(128)S(1)} %get-tuple-element.138.table_ref, bf16[512,2048]{1,0:T(8,128)(2,1)S(1)} %copy-done, bf16[512,1024]{1,0:T(8,128)(2,1)S(1)} %collective-permute-done.6.tok1, bf16[512,2048]{1,0:T(8,128)(2,1)S(1)} %copy-done.1, ...), custom_call_target="tpu_custom_call" | custom-call | tf_op jit(solution)/shard_map/first/pallas_call | solution.py:181
  77.9 2.5 %first.5 = (f32[3,1024,128]{2,1,0:T(8,128)S(1)}, bf16[2,3,4,32,1024]{4,3,2,1,0:T(8,128)(2,1)S(1)}) custom-call(s32[9]{0:T(128)S(1)} %get-tuple-element.139.table_ref, bf16[512,2048]{1,0:T(8,128)(2,1)S(1)} %copy-done, bf16[512,1024]{1,0:T(8,128)(2,1)S(1)} %collective-permute-done.6.tok1, bf16[512,2048]{1,0:T(8,128)(2,1)S(1)} %copy-done.1, ...), custom_call_target="tpu_custom_call" | custom-call | tf_op jit(solution)/shard_map/first/pallas_call | solution.py:181
  81.1 4.2 %collective-permute-done.10 = bf16[2,2,3,4,8,1024]{5,4,3,2,1,0:T(8,128)(2,1)S(1)} collective-permute-done((bf16[2,2,3,4,8,1024]{5,4,3,2,1,0:T(8,128)(2,1)S(1)}, bf16[2,2,3,4,8,1024]{5,4,3,2,1,0:T(8,128)(2,1)S(1)}, u32[]{:S(2)}, u32[]{:S(2)}) %collective-permute-start.10) | collective-permute-done | bytes 786464 | tf_op jit(solution)/shard_map/ppermute | solution.py:46
  85.3 2.5 %first.3 = (f32[3,1024,128]{2,1,0:T(8,128)S(1)}, bf16[2,3,4,32,1024]{4,3,2,1,0:T(8,128)(2,1)S(1)}) custom-call(s32[9]{0:T(128)S(1)} %get-tuple-element.140.table_ref, bf16[512,2048]{1,0:T(8,128)(2,1)S(1)} %copy-done, bf16[512,1024]{1,0:T(8,128)(2,1)S(1)} %collective-permute-done.6.tok1, bf16[512,2048]{1,0:T(8,128)(2,1)S(1)} %copy-done.1, ...), custom_call_target="tpu_custom_call" | custom-call | tf_op jit(solution)/shard_map/first/pallas_call | solution.py:181
  87.8 2.8 %second.4 = (bf16[2,3,32,1024]{3,2,1,0:T(8,128)(2,1)S(1)}, bf16[2,2,3,32,1024]{4,3,2,1,0:T(8,128)(2,1)S(1)}, bf16[2,3,32,1024]{3,2,1,0:T(8,128)(2,1)S(1)}, bf16[...) custom-call(s32[9]{0:T(128)S(1)} %get-tuple-element.138.table_ref, bf16[512,2048]{1,0:T(8,128)(2,1)S(1)} %copy-done, ...), custom_call_target="tpu_custom_call" | custom-call | tf_op jit(solution)/shard_map/second/pallas_call | solution.py:246
  90.8 2.8 %second.5 = (bf16[2,3,32,1024]{3,2,1,0:T(8,128)(2,1)S(1)}, bf16[2,2,3,32,1024]{4,3,2,1,0:T(8,128)(2,1)S(1)}, bf16[2,3,32,1024]{3,2,1,0:T(8,128)(2,1)S(1)}, bf16[...) custom-call(s32[9]{0:T(128)S(1)} %get-tuple-element.139.table_ref, bf16[512,2048]{1,0:T(8,128)(2,1)S(1)} %copy-done, ...), custom_call_target="tpu_custom_call" | custom-call | tf_op jit(solution)/shard_map/second/pallas_call | solution.py:246
  93.7 2.8 %second.3 = (bf16[2,3,32,1024]{3,2,1,0:T(8,128)(2,1)S(1)}, bf16[2,2,3,32,1024]{4,3,2,1,0:T(8,128)(2,1)S(1)}, bf16[2,3,32,1024]{3,2,1,0:T(8,128)(2,1)S(1)}, bf16[...) custom-call(s32[9]{0:T(128)S(1)} %get-tuple-element.140.table_ref, bf16[512,2048]{1,0:T(8,128)(2,1)S(1)} %copy-done, ...), custom_call_target="tpu_custom_call" | custom-call | tf_op jit(solution)/shard_map/second/pallas_call | solution.py:246
  96.5 2.0 %collective-permute-start.26 = (bf16[2,2,3,32,1024]{4,3,2,1,0:T(8,128)(2,1)S(1)}, bf16[2,2,3,32,1024]{4,3,2,1,0:T(8,128)(2,1)S(1)}, u32[]{:S(2)}, u32[]{:S(2)}) collective-permute-start(bf16[2,2,3,32,1024]{4,3,2,1,0:T(8,128)(2,1)S(1)} %get-tuple-element.103), channel_id=1, source_target_pairs={{0,32},{1,97},{2,34},{3,99},{4,36},{5,101},{6,38},{7,103},{8,40},{... | collective-permute-start | bytes 2359304 | tf_op jit(solution)/shard_map/ppermute | solution.py:46
  98.5 4.3 %collective-permute-done.32 = bf16[2,2,3,32,1024]{4,3,2,1,0:T(8,128)(2,1)S(1)} collective-permute-done((bf16[2,2,3,32,1024]{4,3,2,1,0:T(8,128)(2,1)S(1)}, bf16[2,2,3,32,1024]{4,3,2,1,0:T(8,128)(2,1)S(1)}, u32[]{:S(2)}, u32[]{:S(2)}) %collective-permute-start.32) | collective-permute-done | bytes 786464 | tf_op jit(solution)/shard_map/ppermute | solution.py:46
  102.9 2.8 %collective-permute-start.33 = (bf16[2,2,3,32,1024]{4,3,2,1,0:T(8,128)(2,1)S(1)}, bf16[2,2,3,32,1024]{4,3,2,1,0:T(8,128)(2,1)S(1)}, u32[]{:S(2)}, u32[]{:S(2)}) collective-permute-start(bf16[2,2,3,32,1024]{4,3,2,1,0:T(8,128)(2,1)S(1)} %pad_maximum_fusion.7), channel_id=1, source_target_pairs={{0,6},{1,3},{2,4},{3,1},{4,2},{5,7},{6,0},{7,5},{8,14},{9,11},{10,... | collective-permute-start | bytes 2359304 | tf_op jit(solution)/shard_map/ppermute | solution.py:46
  105.8 3.7 %collective-permute-start.39 = (bf16[2,2,3,32,1024]{4,3,2,1,0:T(8,128)(2,1)S(1)}, bf16[2,2,3,32,1024]{4,3,2,1,0:T(8,128)(2,1)S(1)}, u32[]{:S(2)}, u32[]{:S(2)}) collective-permute-start(bf16[2,2,3,32,1024]{4,3,2,1,0:T(8,128)(2,1)S(1)} %pad_maximum_fusion.8), channel_id=1, source_target_pairs={{0,24},{1,9},{2,26},{3,11},{4,28},{5,13},{6,30},{7,15},{8,16},{9,1... | collective-permute-start | bytes 2359304 | tf_op jit(solution)/shard_map/ppermute | solution.py:46
  109.6 3.3 %collective-permute-start.27 = (bf16[2,2,3,32,1024]{4,3,2,1,0:T(8,128)(2,1)S(1)}, bf16[2,2,3,32,1024]{4,3,2,1,0:T(8,128)(2,1)S(1)}, u32[]{:S(2)}, u32[]{:S(2)}) collective-permute-start(bf16[2,2,3,32,1024]{4,3,2,1,0:T(8,128)(2,1)S(1)} %pad_maximum_fusion.6), channel_id=1, source_target_pairs={{0,96},{1,33},{2,98},{3,35},{4,100},{5,37},{6,102},{7,39},{8,104},... | collective-permute-start | bytes 2359304 | tf_op jit(solution)/shard_map/ppermute | solution.py:46
  112.9 3.3 %collective-permute-done.33 = bf16[2,2,3,32,1024]{4,3,2,1,0:T(8,128)(2,1)S(1)} collective-permute-done((bf16[2,2,3,32,1024]{4,3,2,1,0:T(8,128)(2,1)S(1)}, bf16[2,2,3,32,1024]{4,3,2,1,0:T(8,128)(2,1)S(1)}, u32[]{:S(2)}, u32[]{:S(2)}) %collective-permute-start.33) | collective-permute-done | bytes 786464 | tf_op jit(solution)/shard_map/ppermute | solution.py:46
  117.3 3.3 %collective-permute-start.34 = (bf16[2,3,8,8,1024]{4,3,2,1,0:T(8,128)(2,1)S(1)}, bf16[2,3,8,8,1024]{4,3,2,1,0:T(8,128)(2,1)S(1)}, u32[]{:S(2)}, u32[]{:S(2)}) collective-permute-start(bf16[2,3,8,8,1024]{4,3,2,1,0:T(8,128)(2,1)S(1)} %get-tuple-element.115), channel_id=1, source_target_pairs={{0,96},{1,33},{2,98},{3,35},{4,100},{5,37},{6,102},{7,39},{8,104},... | collective-permute-start | bytes 2359304 | tf_op jit(solution)/shard_map/ppermute | solution.py:46
  121.8 3.0 %collective-permute-start.40 = (bf16[2,3,8,8,1024]{4,3,2,1,0:T(8,128)(2,1)S(1)}, bf16[2,3,8,8,1024]{4,3,2,1,0:T(8,128)(2,1)S(1)}, u32[]{:S(2)}, u32[]{:S(2)}) collective-permute-start(bf16[2,3,8,8,1024]{4,3,2,1,0:T(8,128)(2,1)S(1)} %get-tuple-element.124), channel_id=1, source_target_pairs={{0,6},{1,3},{2,4},{3,1},{4,2},{5,7},{6,0},{7,5},{8,14},{9,11},{10,... | collective-permute-start | bytes 2359304 | tf_op jit(solution)/shard_map/ppermute | solution.py:46
  126.0 2.3 %collective-permute-start.28 = (bf16[2,3,8,8,1024]{4,3,2,1,0:T(8,128)(2,1)S(1)}, bf16[2,3,8,8,1024]{4,3,2,1,0:T(8,128)(2,1)S(1)}, u32[]{:S(2)}, u32[]{:S(2)}) collective-permute-start(bf16[2,3,8,8,1024]{4,3,2,1,0:T(8,128)(2,1)S(1)} %get-tuple-element.106), channel_id=1, source_target_pairs={{0,24},{1,9},{2,26},{3,11},{4,28},{5,13},{6,30},{7,15},{8,16},{9,1... | collective-permute-start | bytes 2359304 | tf_op jit(solution)/shard_map/ppermute | solution.py:46
  128.3 3.1 %rows_out.2 = (bf16[512,1024]{1,0:T(8,128)(2,1)S(1)}, bf16[512,1024]{1,0:T(8,128)(2,1)S(1)}) custom-call(s32[9]{0:T(128)S(1)} %get-tuple-element.140.table_ref, bf16[1024,256]{1,0:T(8,128)(2,1)S(1)} %get-tuple-element.80.refs_0_, bf16[1024,256]{1,0:T(8,128)(2,1)S(1)} %get-tuple-element.85.refs_1_, bf16[1024,256]{1,0:T(8,128)(2,1)S(1)} %get-tuple-element.91.refs_2_, ...), custom_call_target="tpu_custom_call" | custom-call | tf_op jit(solution)/shard_map/rows_out/pallas_call | solution.py:289
  132.2 3.1 %collective-permute-done.40.came = bf16[2,3,8,8,1024]{4,3,2,1,0:T(8,128)(2,1)S(1)} collective-permute-done((bf16[2,3,8,8,1024]{4,3,2,1,0:T(8,128)(2,1)S(1)}, bf16[2,3,8,8,1024]{4,3,2,1,0:T(8,128)(2,1)S(1)}, u32[]{:S(2)}, u32[]{:S(2)}) %collective-permute-start.40) | collective-permute-done | bytes 786464 | tf_op jit(solution)/shard_map/ppermute | solution.py:46
  135.8 3.5 %collective-permute-done.28.came = bf16[2,3,8,8,1024]{4,3,2,1,0:T(8,128)(2,1)S(1)} collective-permute-done((bf16[2,3,8,8,1024]{4,3,2,1,0:T(8,128)(2,1)S(1)}, bf16[2,3,8,8,1024]{4,3,2,1,0:T(8,128)(2,1)S(1)}, u32[]{:S(2)}, u32[]{:S(2)}) %collective-permute-start.28) | collective-permute-done | bytes 786464 | tf_op jit(solution)/shard_map/ppermute | solution.py:46
  140.8 2.2 %collective-permute-start.36 = (bf16[2,3,2,8,1024]{4,3,2,1,0:T(8,128)(2,1)S(1)}, bf16[2,3,2,8,1024]{4,3,2,1,0:T(8,128)(2,1)S(1)}, u32[]{:S(2)}, u32[]{:S(2)}) collective-permute-start(bf16[2,3,2,8,1024]{4,3,2,1,0:T(8,128)(2,1)S(1)} %get-tuple-element.118), channel_id=1, source_target_pairs={{0,24},{1,9},{2,26},{3,11},{4,28},{5,13},{6,30},{7,15},{8,16},{9,1... | collective-permute-start | bytes 589832 | tf_op jit(solution)/shard_map/ppermute | solution.py:46
  143.1 5.0 %rows_out.3 = (bf16[512,2048]{1,0:T(8,128)(2,1)}, bf16[512,2048]{1,0:T(8,128)(2,1)}) custom-call(s32[9]{0:T(128)S(1)} %get-tuple-element.140.table_ref, bf16[1024,256]{1,0:T(8,128)(2,1)S(1)} %get-tuple-element.80.refs_0_, bf16[1024,256]{1,0:T(8,128)(2,1)S(1)} %get-tuple-element.85.refs_1_, bf16[1024,256]{1,0:T(8,128)(2,1)S(1)} %get-tuple-element.91.refs_2_, ...), custom_call_target="tpu_custom_call" | custom-call | tf_op jit(solution)/shard_map/rows_out/pallas_call | solution.py:289
  149.0 3.3 %collective-permute-start.42 = (bf16[2,3,2,8,1024]{4,3,2,1,0:T(8,128)(2,1)S(1)}, bf16[2,3,2,8,1024]{4,3,2,1,0:T(8,128)(2,1)S(1)}, u32[]{:S(2)}, u32[]{:S(2)}) collective-permute-start(bf16[2,3,2,8,1024]{4,3,2,1,0:T(8,128)(2,1)S(1)} %get-tuple-element.127), channel_id=1, source_target_pairs={{0,96},{1,33},{2,98},{3,35},{4,100},{5,37},{6,102},{7,39},{8,104},... | collective-permute-start | bytes 589832 | tf_op jit(solution)/shard_map/ppermute | solution.py:46
  153.2 1.4 collective-permute-start.30
  154.6 1.3 collective-permute-start.37
  156.5 3.7 %collective-permute-done.30 = bf16[2,3,2,8,1024]{4,3,2,1,0:T(8,128)(2,1)S(1)} collective-permute-done((bf16[2,3,2,8,1024]{4,3,2,1,0:T(8,128)(2,1)S(1)}, bf16[2,3,2,8,1024]{4,3,2,1,0:T(8,128)(2,1)S(1)}, u32[]{:S(2)}, u32[]{:S(2)}) %collective-permute-start.30) | collective-permute-done | bytes 196640 | tf_op jit(solution)/shard_map/ppermute | solution.py:46
  160.3 6.1 %collective-permute-start.31 = (bf16[3,2,8,1024]{3,2,1,0:T(8,128)(2,1)S(1)}, bf16[3,2,8,1024]{3,2,1,0:T(8,128)(2,1)S(1)}, u32[]{:S(2)}, u32[]{:S(2)}) collective-permute-start(bf16[3,2,8,1024]{3,2,1,0:T(8,128)(2,1)S(1)} %fusion.7), channel_id=1, source_target_pairs={{0,2},{1,7},{2,0},{3,5},{4,6},{5,3},{6,4},{7,1},{8,10},{9,15},{10,... | collective-permute-start | bytes 294920 | tf_op jit(solution)/shard_map/ppermute | solution.py:46
  166.5 2.5 %collective-permute-done.31 = bf16[3,2,8,1024]{3,2,1,0:T(8,128)(2,1)S(1)} collective-permute-done((bf16[3,2,8,1024]{3,2,1,0:T(8,128)(2,1)S(1)}, bf16[3,2,8,1024]{3,2,1,0:T(8,128)(2,1)S(1)}, u32[]{:S(2)}, u32[]{:S(2)}) %collective-permute-start.31) | collective-permute-done | bytes 98336 | tf_op jit(solution)/shard_map/ppermute | solution.py:46
  169.1 1.5 divide_subtract_fusion
  (119 shorter events, 24.4 us)
Async XLA Ops:
  2.5 5.5 %collective-permute-start.12 = (bf16[3,2,8,1024]{3,2,1,0:T(8,128)(2,1)S(1)}, bf16[3,2,8,1024]{3,2,1,0:T(8,128)(2,1)S(1)}, u32[]{:S(2)}, u32[]{:S(2)}) collective-permute-start(bf16[3,2,8,1024]{3,2,1,0:T(8,128)(2,1)S(1)} %get-tuple-element.135.own), channel_id=1, source_target_pairs={{0,8},{1,25},{2,10},{3,27},{4,12},{5,29},{6,14},{7,31},{8,0},{9,17... | collective-permute-start | bytes 294920 | tf_op jit(solution)/shard_map/ppermute | solution.py:46
  4.2 6.2 %collective-permute-start.4 = (bf16[3,2,8,1024]{3,2,1,0:T(8,128)(2,1)S(1)}, bf16[3,2,8,1024]{3,2,1,0:T(8,128)(2,1)S(1)}, u32[]{:S(2)}, u32[]{:S(2)}) collective-permute-start(bf16[3,2,8,1024]{3,2,1,0:T(8,128)(2,1)S(1)} %get-tuple-element.136.own), channel_id=1, source_target_pairs={{0,32},{1,97},{2,34},{3,99},{4,36},{5,101},{6,38},{7,103},{8,40},{... | collective-permute-start | bytes 294920 | tf_op jit(solution)/shard_map/ppermute | solution.py:46
  6.1 10.9 %collective-permute-start = (bf16[3,2,8,1024]{3,2,1,0:T(8,128)(2,1)S(1)}, bf16[3,2,8,1024]{3,2,1,0:T(8,128)(2,1)S(1)}, u32[]{:S(2)}, u32[]{:S(2)}) collective-permute-start(bf16[3,2,8,1024]{3,2,1,0:T(8,128)(2,1)S(1)} %get-tuple-element.137.own), channel_id=1, source_target_pairs={{0,2},{1,7},{2,0},{3,5},{4,6},{5,3},{6,4},{7,1},{8,10},{9,15},{10,... | collective-permute-start | bytes 294920 | tf_op jit(solution)/shard_map/ppermute | solution.py:46
  8.1 7.0 %collective-permute-start.13 = (bf16[2,3,2,8,1024]{4,3,2,1,0:T(8,128)(2,1)S(1)}, bf16[2,3,2,8,1024]{4,3,2,1,0:T(8,128)(2,1)S(1)}, u32[]{:S(2)}, u32[]{:S(2)}) collective-permute-start(bf16[2,3,2,8,1024]{4,3,2,1,0:T(8,128)(2,1)S(1)} %pad_maximum_fusion.12), channel_id=1, source_target_pairs={{0,24},{1,9},{2,26},{3,11},{4,28},{5,13},{6,30},{7,15},{8,16},{9,1... | collective-permute-start | bytes 589832 | tf_op jit(solution)/shard_map/ppermute | solution.py:46
  10.3 17.7 %copy-start.1 = (bf16[512,2048]{1,0:T(8,128)(2,1)S(1)}, bf16[512,2048]{1,0:T(8,128)(2,1)}, u32[]{:S(2)}) copy-start(bf16[512,2048]{1,0:T(8,128)(2,1)} %cot0.5) | copy-start | bytes 6291460
  11.0 9.4 %collective-permute-start.5 = (bf16[2,3,2,8,1024]{4,3,2,1,0:T(8,128)(2,1)}, bf16[2,3,2,8,1024]{4,3,2,1,0:T(8,128)(2,1)S(1)}, u32[]{:S(2)}, u32[]{:S(2)}) collective-permute-start(bf16[2,3,2,8,1024]{4,3,2,1,0:T(8,128)(2,1)} %pad_maximum_fusion.11), channel_id=1, source_target_pairs={{0,96},{1,33},{2,98},{3,35},{4,100},{5,37},{6,102},{7,39},{8,104},... | collective-permute-start | bytes 589832 | tf_op jit(solution)/shard_map/ppermute | solution.py:46
  15.9 12.3 %collective-permute-start.14 = (bf16[3,8,8,1024]{3,2,1,0:T(8,128)(2,1)S(1)}, bf16[3,8,8,1024]{3,2,1,0:T(8,128)(2,1)S(1)}, u32[]{:S(2)}, u32[]{:S(2)}) collective-permute-start(bf16[3,8,8,1024]{3,2,1,0:T(8,128)(2,1)S(1)} %weave.5.kept), channel_id=1, source_target_pairs={{0,32},{1,97},{2,34},{3,99},{4,36},{5,101},{6,38},{7,103},{8,40},{... | collective-permute-start | bytes 1179656 | tf_op jit(solution)/shard_map/ppermute | solution.py:46
  17.7 9.0 %collective-permute-start.1 = (bf16[2,3,2,8,1024]{4,3,2,1,0:T(8,128)(2,1)}, bf16[2,3,2,8,1024]{4,3,2,1,0:T(8,128)(2,1)}, u32[]{:S(2)}, u32[]{:S(2)}) collective-permute-start(bf16[2,3,2,8,1024]{4,3,2,1,0:T(8,128)(2,1)} %pad_maximum_fusion.10), channel_id=1, source_target_pairs={{0,6},{1,3},{2,4},{3,1},{4,2},{5,7},{6,0},{7,5},{8,14},{9,11},{10,... | collective-permute-start | bytes 589832 | tf_op jit(solution)/shard_map/ppermute | solution.py:46
  21.3 10.7 %collective-permute-start.19 = (bf16[3,8,8,1024]{3,2,1,0:T(8,128)(2,1)S(1)}, bf16[3,8,8,1024]{3,2,1,0:T(8,128)(2,1)S(1)}, u32[]{:S(2)}, u32[]{:S(2)}) collective-permute-start(bf16[3,8,8,1024]{3,2,1,0:T(8,128)(2,1)S(1)} %weave.4.kept), channel_id=1, source_target_pairs={{0,2},{1,7},{2,0},{3,5},{4,6},{5,3},{6,4},{7,1},{8,10},{9,15},{10,... | collective-permute-start | bytes 1179656 | tf_op jit(solution)/shard_map/ppermute | solution.py:46
  27.9 7.9 %collective-permute-start.2 = (bf16[3,8,8,1024]{3,2,1,0:T(8,128)(2,1)S(1)}, bf16[3,8,8,1024]{3,2,1,0:T(8,128)(2,1)S(1)}, u32[]{:S(2)}, u32[]{:S(2)}) collective-permute-start(bf16[3,8,8,1024]{3,2,1,0:T(8,128)(2,1)S(1)} %weave.3.kept), channel_id=1, source_target_pairs={{0,8},{1,25},{2,10},{3,27},{4,12},{5,29},{6,14},{7,31},{8,0},{9,17... | collective-permute-start | bytes 1179656 | tf_op jit(solution)/shard_map/ppermute | solution.py:46
  28.1 21.0 %collective-permute-start.7 = (bf16[512,1024]{1,0:T(8,128)(2,1)S(1)}, bf16[512,1024]{1,0:T(8,128)(2,1)S(1)}, u32[]{:S(2)}, u32[]{:S(2)}) collective-permute-start(bf16[512,1024]{1,0:T(8,128)(2,1)S(1)} %constant_dynamic-slice_fusion), channel_id=1, source_target_pairs={{0,1},{1,0},{2,3},{3,2},{4,5},{5,4},{6,7},{7,6},{8,9},{9,8},{10,11... | collective-permute-start | bytes 3145736 | tf_op jit(solution)/shard_map/ppermute | solution.py:50
  28.3 13.4 %collective-permute-start.15 = (bf16[2,3,8,8,1024]{4,3,2,1,0:T(8,128)(2,1)S(1)}, bf16[2,3,8,8,1024]{4,3,2,1,0:T(8,128)(2,1)S(1)}, u32[]{:S(2)}, u32[]{:S(2)}) collective-permute-start(bf16[2,3,8,8,1024]{4,3,2,1,0:T(8,128)(2,1)S(1)} %pad_maximum_fusion.2), channel_id=1, source_target_pairs={{0,96},{1,33},{2,98},{3,35},{4,100},{5,37},{6,102},{7,39},{8,104},... | collective-permute-start | bytes 2359304 | tf_op jit(solution)/shard_map/ppermute | solution.py:46
  31.9 17.2 %collective-permute-start.6 = (bf16[512,1024]{1,0:T(8,128)(2,1)S(1)}, bf16[512,1024]{1,0:T(8,128)(2,1)S(1)}, u32[]{:S(2)}, u32[]{:S(2)}) collective-permute-start(bf16[512,1024]{1,0:T(8,128)(2,1)S(1)} %constant_dynamic-slice_fusion.1), channel_id=1, source_target_pairs={{0,1},{1,0},{2,3},{3,2},{4,5},{5,4},{6,7},{7,6},{8,9},{9,8},{10,11... | collective-permute-start | bytes 3145736 | tf_op jit(solution)/shard_map/ppermute | solution.py:50
  32.0 13.6 %collective-permute-start.20 = (bf16[2,3,8,8,1024]{4,3,2,1,0:T(8,128)(2,1)S(1)}, bf16[2,3,8,8,1024]{4,3,2,1,0:T(8,128)(2,1)S(1)}, u32[]{:S(2)}, u32[]{:S(2)}) collective-permute-start(bf16[2,3,8,8,1024]{4,3,2,1,0:T(8,128)(2,1)S(1)} %pad_maximum_fusion.4), channel_id=1, source_target_pairs={{0,6},{1,3},{2,4},{3,1},{4,2},{5,7},{6,0},{7,5},{8,14},{9,11},{10,... | collective-permute-start | bytes 2359304 | tf_op jit(solution)/shard_map/ppermute | solution.py:46
  35.9 13.6 %collective-permute-start.3 = (bf16[2,3,8,8,1024]{4,3,2,1,0:T(8,128)(2,1)S(1)}, bf16[2,3,8,8,1024]{4,3,2,1,0:T(8,128)(2,1)S(1)}, u32[]{:S(2)}, u32[]{:S(2)}) collective-permute-start(bf16[2,3,8,8,1024]{4,3,2,1,0:T(8,128)(2,1)S(1)} %pad_maximum_fusion), channel_id=1, source_target_pairs={{0,24},{1,9},{2,26},{3,11},{4,28},{5,13},{6,30},{7,15},{8,16},{9,1... | collective-permute-start | bytes 2359304 | tf_op jit(solution)/shard_map/ppermute | solution.py:46
  42.4 12.1 %collective-permute-start.16 = (bf16[2,2,3,4,8,1024]{5,4,3,2,1,0:T(8,128)(2,1)S(1)}, bf16[2,2,3,4,8,1024]{5,4,3,2,1,0:T(8,128)(2,1)S(1)}, u32[]{:S(2)}, u32[]{:S(2)}) collective-permute-start(bf16[2,2,3,4,8,1024]{5,4,3,2,1,0:T(8,128)(2,1)S(1)} %get-tuple-element.82), channel_id=1, source_target_pairs={{0,2},{1,7},{2,0},{3,5},{4,6},{5,3},{6,4},{7,1},{8,10},{9,15},{10,... | collective-permute-start | bytes 2359304 | tf_op jit(solution)/shard_map/ppermute | solution.py:46
  45.7 1.2 collective-permute-start.8
  46.8 12.2 %collective-permute-start.21 = (bf16[2,2,3,4,8,1024]{5,4,3,2,1,0:T(8,128)(2,1)S(1)}, bf16[2,2,3,4,8,1024]{5,4,3,2,1,0:T(8,128)(2,1)S(1)}, u32[]{:S(2)}, u32[]{:S(2)}) collective-permute-start(bf16[2,2,3,4,8,1024]{5,4,3,2,1,0:T(8,128)(2,1)S(1)} %get-tuple-element.88), channel_id=1, source_target_pairs={{0,8},{1,25},{2,10},{3,27},{4,12},{5,29},{6,14},{7,31},{8,0},{9,17... | collective-permute-start | bytes 2359304 | tf_op jit(solution)/shard_map/ppermute | solution.py:46
  50.3 12.1 %collective-permute-start.9 = (bf16[2,2,3,4,8,1024]{5,4,3,2,1,0:T(8,128)(2,1)S(1)}, bf16[2,2,3,4,8,1024]{5,4,3,2,1,0:T(8,128)(2,1)S(1)}, u32[]{:S(2)}, u32[]{:S(2)}) collective-permute-start(bf16[2,2,3,4,8,1024]{5,4,3,2,1,0:T(8,128)(2,1)S(1)} %get-tuple-element.77), channel_id=1, source_target_pairs={{0,32},{1,97},{2,34},{3,99},{4,36},{5,101},{6,38},{7,103},{8,40},{... | collective-permute-start | bytes 2359304 | tf_op jit(solution)/shard_map/ppermute | solution.py:46
  54.6 20.7 %collective-permute-start.17 = (bf16[2,2,3,4,8,1024]{5,4,3,2,1,0:T(8,128)(2,1)S(1)}, bf16[2,2,3,4,8,1024]{5,4,3,2,1,0:T(8,128)(2,1)S(1)}, u32[]{:S(2)}, u32[]{:S(2)}) collective-permute-start(bf16[2,2,3,4,8,1024]{5,4,3,2,1,0:T(8,128)(2,1)S(1)} %pad_maximum_fusion.3), channel_id=1, source_target_pairs={{0,6},{1,3},{2,4},{3,1},{4,2},{5,7},{6,0},{7,5},{8,14},{9,11},{10,... | collective-permute-start | bytes 2359304 | tf_op jit(solution)/shard_map/ppermute | solution.py:46
  59.2 18.7 %collective-permute-start.22 = (bf16[2,2,3,4,8,1024]{5,4,3,2,1,0:T(8,128)(2,1)S(1)}, bf16[2,2,3,4,8,1024]{5,4,3,2,1,0:T(8,128)(2,1)S(1)}, u32[]{:S(2)}, u32[]{:S(2)}) collective-permute-start(bf16[2,2,3,4,8,1024]{5,4,3,2,1,0:T(8,128)(2,1)S(1)} %pad_maximum_fusion.5), channel_id=1, source_target_pairs={{0,24},{1,9},{2,26},{3,11},{4,28},{5,13},{6,30},{7,15},{8,16},{9,1... | collective-permute-start | bytes 2359304 | tf_op jit(solution)/shard_map/ppermute | solution.py:46
  62.5 22.8 %collective-permute-start.10 = (bf16[2,2,3,4,8,1024]{5,4,3,2,1,0:T(8,128)(2,1)S(1)}, bf16[2,2,3,4,8,1024]{5,4,3,2,1,0:T(8,128)(2,1)S(1)}, u32[]{:S(2)}, u32[]{:S(2)}) collective-permute-start(bf16[2,2,3,4,8,1024]{5,4,3,2,1,0:T(8,128)(2,1)S(1)} %pad_maximum_fusion.1), channel_id=1, source_target_pairs={{0,96},{1,33},{2,98},{3,35},{4,100},{5,37},{6,102},{7,39},{8,104},... | collective-permute-start | bytes 2359304 | tf_op jit(solution)/shard_map/ppermute | solution.py:46
  77.8 10.1 %collective-permute-start.18 = (f32[3,1024,128]{2,1,0:T(8,128)S(1)}, f32[3,1024,128]{2,1,0:T(8,128)S(1)}, u32[]{:S(2)}, u32[]{:S(2)}) collective-permute-start(f32[3,1024,128]{2,1,0:T(8,128)S(1)} %get-tuple-element.84.sums), channel_id=1, source_target_pairs={{0,1},{1,0},{2,3},{3,2},{4,5},{5,4},{6,7},{7,6},{8,9},{9,8},{10,11... | collective-permute-start | bytes 4718600 | tf_op jit(solution)/shard_map/ppermute | solution.py:50
  80.3 10.4 %collective-permute-start.23 = (f32[3,1024,128]{2,1,0:T(8,128)S(1)}, f32[3,1024,128]{2,1,0:T(8,128)S(1)}, u32[]{:S(2)}, u32[]{:S(2)}) collective-permute-start(f32[3,1024,128]{2,1,0:T(8,128)S(1)} %get-tuple-element.90.sums), channel_id=1, source_target_pairs={{0,1},{1,0},{2,3},{3,2},{4,5},{5,4},{6,7},{7,6},{8,9},{9,8},{10,11... | collective-permute-start | bytes 4718600 | tf_op jit(solution)/shard_map/ppermute | solution.py:50
  87.7 6.0 %collective-permute-start.11 = (f32[3,1024,128]{2,1,0:T(8,128)S(1)}, f32[3,1024,128]{2,1,0:T(8,128)S(1)}, u32[]{:S(2)}, u32[]{:S(2)}) collective-permute-start(f32[3,1024,128]{2,1,0:T(8,128)S(1)} %get-tuple-element.79.sums), channel_id=1, source_target_pairs={{0,1},{1,0},{2,3},{3,2},{4,5},{5,4},{6,7},{7,6},{8,9},{9,8},{10,11... | collective-permute-start | bytes 4718600 | tf_op jit(solution)/shard_map/ppermute | solution.py:50
  90.7 12.1 %collective-permute-start.32 = (bf16[2,2,3,32,1024]{4,3,2,1,0:T(8,128)(2,1)S(1)}, bf16[2,2,3,32,1024]{4,3,2,1,0:T(8,128)(2,1)S(1)}, u32[]{:S(2)}, u32[]{:S(2)}) collective-permute-start(bf16[2,2,3,32,1024]{4,3,2,1,0:T(8,128)(2,1)S(1)} %get-tuple-element.112), channel_id=1, source_target_pairs={{0,2},{1,7},{2,0},{3,5},{4,6},{5,3},{6,4},{7,1},{8,10},{9,15},{10,... | collective-permute-start | bytes 2359304 | tf_op jit(solution)/shard_map/ppermute | solution.py:46
  93.6 12.1 %collective-permute-start.38 = (bf16[2,2,3,32,1024]{4,3,2,1,0:T(8,128)(2,1)S(1)}, bf16[2,2,3,32,1024]{4,3,2,1,0:T(8,128)(2,1)S(1)}, u32[]{:S(2)}, u32[]{:S(2)}) collective-permute-start(bf16[2,2,3,32,1024]{4,3,2,1,0:T(8,128)(2,1)S(1)} %get-tuple-element.121), channel_id=1, source_target_pairs={{0,8},{1,25},{2,10},{3,27},{4,12},{5,29},{6,14},{7,31},{8,0},{9,17... | collective-permute-start | bytes 2359304 | tf_op jit(solution)/shard_map/ppermute | solution.py:46
  96.5 12.9 %collective-permute-start.26 = (bf16[2,2,3,32,1024]{4,3,2,1,0:T(8,128)(2,1)S(1)}, bf16[2,2,3,32,1024]{4,3,2,1,0:T(8,128)(2,1)S(1)}, u32[]{:S(2)}, u32[]{:S(2)}) collective-permute-start(bf16[2,2,3,32,1024]{4,3,2,1,0:T(8,128)(2,1)S(1)} %get-tuple-element.103), channel_id=1, source_target_pairs={{0,32},{1,97},{2,34},{3,99},{4,36},{5,101},{6,38},{7,103},{8,40},{... | collective-permute-start | bytes 2359304 | tf_op jit(solution)/shard_map/ppermute | solution.py:46
  102.9 13.3 %collective-permute-start.33 = (bf16[2,2,3,32,1024]{4,3,2,1,0:T(8,128)(2,1)S(1)}, bf16[2,2,3,32,1024]{4,3,2,1,0:T(8,128)(2,1)S(1)}, u32[]{:S(2)}, u32[]{:S(2)}) collective-permute-start(bf16[2,2,3,32,1024]{4,3,2,1,0:T(8,128)(2,1)S(1)} %pad_maximum_fusion.7), channel_id=1, source_target_pairs={{0,6},{1,3},{2,4},{3,1},{4,2},{5,7},{6,0},{7,5},{8,14},{9,11},{10,... | collective-permute-start | bytes 2359304 | tf_op jit(solution)/shard_map/ppermute | solution.py:46
  105.8 14.9 %collective-permute-start.39 = (bf16[2,2,3,32,1024]{4,3,2,1,0:T(8,128)(2,1)S(1)}, bf16[2,2,3,32,1024]{4,3,2,1,0:T(8,128)(2,1)S(1)}, u32[]{:S(2)}, u32[]{:S(2)}) collective-permute-start(bf16[2,2,3,32,1024]{4,3,2,1,0:T(8,128)(2,1)S(1)} %pad_maximum_fusion.8), channel_id=1, source_target_pairs={{0,24},{1,9},{2,26},{3,11},{4,28},{5,13},{6,30},{7,15},{8,16},{9,1... | collective-permute-start | bytes 2359304 | tf_op jit(solution)/shard_map/ppermute | solution.py:46
  109.6 15.3 %collective-permute-start.27 = (bf16[2,2,3,32,1024]{4,3,2,1,0:T(8,128)(2,1)S(1)}, bf16[2,2,3,32,1024]{4,3,2,1,0:T(8,128)(2,1)S(1)}, u32[]{:S(2)}, u32[]{:S(2)}) collective-permute-start(bf16[2,2,3,32,1024]{4,3,2,1,0:T(8,128)(2,1)S(1)} %pad_maximum_fusion.6), channel_id=1, source_target_pairs={{0,96},{1,33},{2,98},{3,35},{4,100},{5,37},{6,102},{7,39},{8,104},... | collective-permute-start | bytes 2359304 | tf_op jit(solution)/shard_map/ppermute | solution.py:46
  117.3 14.7 %collective-permute-start.34 = (bf16[2,3,8,8,1024]{4,3,2,1,0:T(8,128)(2,1)S(1)}, bf16[2,3,8,8,1024]{4,3,2,1,0:T(8,128)(2,1)S(1)}, u32[]{:S(2)}, u32[]{:S(2)}) collective-permute-start(bf16[2,3,8,8,1024]{4,3,2,1,0:T(8,128)(2,1)S(1)} %get-tuple-element.115), channel_id=1, source_target_pairs={{0,96},{1,33},{2,98},{3,35},{4,100},{5,37},{6,102},{7,39},{8,104},... | collective-permute-start | bytes 2359304 | tf_op jit(solution)/shard_map/ppermute | solution.py:46
  121.8 13.5 %collective-permute-start.40 = (bf16[2,3,8,8,1024]{4,3,2,1,0:T(8,128)(2,1)S(1)}, bf16[2,3,8,8,1024]{4,3,2,1,0:T(8,128)(2,1)S(1)}, u32[]{:S(2)}, u32[]{:S(2)}) collective-permute-start(bf16[2,3,8,8,1024]{4,3,2,1,0:T(8,128)(2,1)S(1)} %get-tuple-element.124), channel_id=1, source_target_pairs={{0,6},{1,3},{2,4},{3,1},{4,2},{5,7},{6,0},{7,5},{8,14},{9,11},{10,... | collective-permute-start | bytes 2359304 | tf_op jit(solution)/shard_map/ppermute | solution.py:46
  126.0 13.3 %collective-permute-start.28 = (bf16[2,3,8,8,1024]{4,3,2,1,0:T(8,128)(2,1)S(1)}, bf16[2,3,8,8,1024]{4,3,2,1,0:T(8,128)(2,1)S(1)}, u32[]{:S(2)}, u32[]{:S(2)}) collective-permute-start(bf16[2,3,8,8,1024]{4,3,2,1,0:T(8,128)(2,1)S(1)} %get-tuple-element.106), channel_id=1, source_target_pairs={{0,24},{1,9},{2,26},{3,11},{4,28},{5,13},{6,30},{7,15},{8,16},{9,1... | collective-permute-start | bytes 2359304 | tf_op jit(solution)/shard_map/ppermute | solution.py:46
  131.4 11.7 %collective-permute-start.24 = (bf16[512,1024]{1,0:T(8,128)(2,1)S(1)}, bf16[512,1024]{1,0:T(8,128)(2,1)S(1)}, u32[]{:S(2)}, u32[]{:S(2)}) collective-permute-start(bf16[512,1024]{1,0:T(8,128)(2,1)S(1)} %get-tuple-element.98), channel_id=1, source_target_pairs={{0,1},{1,0},{2,3},{3,2},{4,5},{5,4},{6,7},{7,6},{8,9},{9,8},{10,11... | collective-permute-start | bytes 3145736 | tf_op jit(solution)/shard_map/ppermute | solution.py:50
  131.5 11.6 %collective-permute-start.25 = (bf16[512,1024]{1,0:T(8,128)(2,1)S(1)}, bf16[512,1024]{1,0:T(8,128)(2,1)S(1)}, u32[]{:S(2)}, u32[]{:S(2)}) collective-permute-start(bf16[512,1024]{1,0:T(8,128)(2,1)S(1)} %get-tuple-element.99), channel_id=1, source_target_pairs={{0,1},{1,0},{2,3},{3,2},{4,5},{5,4},{6,7},{7,6},{8,9},{9,8},{10,11... | collective-permute-start | bytes 3145736 | tf_op jit(solution)/shard_map/ppermute | solution.py:50
  132.1 7.9 %collective-permute-start.35 = (bf16[3,8,8,1024]{3,2,1,0:T(8,128)(2,1)S(1)}, bf16[3,8,8,1024]{3,2,1,0:T(8,128)(2,1)S(1)}, u32[]{:S(2)}, u32[]{:S(2)}) collective-permute-start(bf16[3,8,8,1024]{3,2,1,0:T(8,128)(2,1)S(1)} %fusion.1), channel_id=1, source_target_pairs={{0,32},{1,97},{2,34},{3,99},{4,36},{5,101},{6,38},{7,103},{8,40},{... | collective-permute-start | bytes 1179656 | tf_op jit(solution)/shard_map/ppermute | solution.py:46
  135.5 12.7 %collective-permute-start.41 = (bf16[3,8,8,1024]{3,2,1,0:T(8,128)(2,1)S(1)}, bf16[3,8,8,1024]{3,2,1,0:T(8,128)(2,1)S(1)}, u32[]{:S(2)}, u32[]{:S(2)}) collective-permute-start(bf16[3,8,8,1024]{3,2,1,0:T(8,128)(2,1)S(1)} %fusion), channel_id=1, source_target_pairs={{0,2},{1,7},{2,0},{3,5},{4,6},{5,3},{6,4},{7,1},{8,10},{9,15},{10,... | collective-permute-start | bytes 1179656 | tf_op jit(solution)/shard_map/ppermute | solution.py:46
  139.4 12.9 %collective-permute-start.29 = (bf16[3,8,8,1024]{3,2,1,0:T(8,128)(2,1)S(1)}, bf16[3,8,8,1024]{3,2,1,0:T(8,128)(2,1)S(1)}, u32[]{:S(2)}, u32[]{:S(2)}) collective-permute-start(bf16[3,8,8,1024]{3,2,1,0:T(8,128)(2,1)S(1)} %fusion.2), channel_id=1, source_target_pairs={{0,8},{1,25},{2,10},{3,27},{4,12},{5,29},{6,14},{7,31},{8,0},{9,17... | collective-permute-start | bytes 1179656 | tf_op jit(solution)/shard_map/ppermute | solution.py:46
  140.8 13.7 %collective-permute-start.36 = (bf16[2,3,2,8,1024]{4,3,2,1,0:T(8,128)(2,1)S(1)}, bf16[2,3,2,8,1024]{4,3,2,1,0:T(8,128)(2,1)S(1)}, u32[]{:S(2)}, u32[]{:S(2)}) collective-permute-start(bf16[2,3,2,8,1024]{4,3,2,1,0:T(8,128)(2,1)S(1)} %get-tuple-element.118), channel_id=1, source_target_pairs={{0,24},{1,9},{2,26},{3,11},{4,28},{5,13},{6,30},{7,15},{8,16},{9,1... | collective-permute-start | bytes 589832 | tf_op jit(solution)/shard_map/ppermute | solution.py:46
  149.0 7.0 %collective-permute-start.42 = (bf16[2,3,2,8,1024]{4,3,2,1,0:T(8,128)(2,1)S(1)}, bf16[2,3,2,8,1024]{4,3,2,1,0:T(8,128)(2,1)S(1)}, u32[]{:S(2)}, u32[]{:S(2)}) collective-permute-start(bf16[2,3,2,8,1024]{4,3,2,1,0:T(8,128)(2,1)S(1)} %get-tuple-element.127), channel_id=1, source_target_pairs={{0,96},{1,33},{2,98},{3,35},{4,100},{5,37},{6,102},{7,39},{8,104},... | collective-permute-start | bytes 589832 | tf_op jit(solution)/shard_map/ppermute | solution.py:46
  153.1 15.9 %copy-start.2 = (f32[8,3,6,1024]{3,0,2,1:T(8,128)S(1)}, f32[8,3,6,1024]{3,0,2,1:T(8,128)}, u32[]{:S(2)}) copy-start(f32[8,3,6,1024]{3,0,2,1:T(8,128)} %param.13) | copy-start | bytes 1769476
  153.1 15.9 %copy-start.3 = (f32[8,3,6,1024]{3,0,2,1:T(8,128)S(1)}, f32[8,3,6,1024]{3,0,2,1:T(8,128)}, u32[]{:S(2)}) copy-start(f32[8,3,6,1024]{3,0,2,1:T(8,128)} %param.14) | copy-start | bytes 1769476
  153.2 15.9 %copy-start.4 = (f32[8,3,6,1024]{3,0,2,1:T(8,128)S(1)}, f32[8,3,6,1024]{3,0,2,1:T(8,128)}, u32[]{:S(2)}) copy-start(f32[8,3,6,1024]{3,0,2,1:T(8,128)} %param.15) | copy-start | bytes 1769476
  153.2 7.1 %collective-permute-start.30 = (bf16[2,3,2,8,1024]{4,3,2,1,0:T(8,128)(2,1)S(1)}, bf16[2,3,2,8,1024]{4,3,2,1,0:T(8,128)(2,1)S(1)}, u32[]{:S(2)}, u32[]{:S(2)}) collective-permute-start(bf16[2,3,2,8,1024]{4,3,2,1,0:T(8,128)(2,1)S(1)} %get-tuple-element.109), channel_id=1, source_target_pairs={{0,6},{1,3},{2,4},{3,1},{4,2},{5,7},{6,0},{7,5},{8,14},{9,11},{10,... | collective-permute-start | bytes 589832 | tf_op jit(solution)/shard_map/ppermute | solution.py:46
  154.6 11.8 %collective-permute-start.37 = (bf16[3,2,8,1024]{3,2,1,0:T(8,128)(2,1)S(1)}, bf16[3,2,8,1024]{3,2,1,0:T(8,128)(2,1)S(1)}, u32[]{:S(2)}, u32[]{:S(2)}) collective-permute-start(bf16[3,2,8,1024]{3,2,1,0:T(8,128)(2,1)S(1)} %fusion.5), channel_id=1, source_target_pairs={{0,8},{1,25},{2,10},{3,27},{4,12},{5,29},{6,14},{7,31},{8,0},{9,17... | collective-permute-start | bytes 294920 | tf_op jit(solution)/shard_map/ppermute | solution.py:46
  156.0 10.5 %collective-permute-start.43 = (bf16[3,2,8,1024]{3,2,1,0:T(8,128)(2,1)S(1)}, bf16[3,2,8,1024]{3,2,1,0:T(8,128)(2,1)S(1)}, u32[]{:S(2)}, u32[]{:S(2)}) collective-permute-start(bf16[3,2,8,1024]{3,2,1,0:T(8,128)(2,1)S(1)} %fusion.3), channel_id=1, source_target_pairs={{0,32},{1,97},{2,34},{3,99},{4,36},{5,101},{6,38},{7,103},{8,40},{... | collective-permute-start | bytes 294920 | tf_op jit(solution)/shard_map/ppermute | solution.py:46
  160.3 8.7 %collective-permute-start.31 = (bf16[3,2,8,1024]{3,2,1,0:T(8,128)(2,1)S(1)}, bf16[3,2,8,1024]{3,2,1,0:T(8,128)(2,1)S(1)}, u32[]{:S(2)}, u32[]{:S(2)}) collective-permute-start(bf16[3,2,8,1024]{3,2,1,0:T(8,128)(2,1)S(1)} %fusion.7), channel_id=1, source_target_pairs={{0,2},{1,7},{2,0},{3,5},{4,6},{5,3},{6,4},{7,1},{8,10},{9,15},{10,... | collective-permute-start | bytes 294920 | tf_op jit(solution)/shard_map/ppermute | solution.py:46
  (6 other events, 43.6 us)
where the time goes:
time: 171 us
  starting transfers between devices  86.6 us (51%)
  waiting for transfers between devices  40.8 us (24%)
  Pallas kernels  34.8 us (20%)
  other arithmetic  5.6 us (3%)
    ppermute x36, starting transfers between devices, hop(): return lax.ppermute(value, BOTH, step_pairs(axis, offsets))  84.9 us
    ppermute x36, waiting for transfers between devices, hop(): return lax.ppermute(value, BOTH, step_pairs(axis, offsets))  40.3 us
    pallas_call x3, Pallas kernels, second(): pl.pallas_call(second_kernel, out_shape=[shape_of(*lead, 2, 3, 32, column...  8.46 us
    pallas_call x2, Pallas kernels, rows_out(): pl.pallas_call(functools.partial(rows_kernel, start), out_shape=[shape_of...  8.16 us
    pallas_call x3, Pallas kernels, first(): pl.pallas_call(first_kernel, out_shape=[jax.ShapeDtypeStruct((3, rows, 12...  7.38 us
    pallas_call x3, Pallas kernels, merge(): pl.pallas_call(merge_kernel, out_shape=[shape_of(*lead, 3, experts, 8, co...  3.54 us
  transfers between devices with their start and end apart: 44, of which 17 were waited for; matrix products, arithmetic and copies ran while one was open for 2% of the time, Pallas kernels for 20%

commit v1 on v0

--- a/solution.py
+++ b/solution.py
@@ -19,7 +19,7 @@
 CHAINS = 3
 BOTH = ("group", "local")
 SHIFTS = (4, 2, 0)
-AXES = ((2, 1, 0), (1, 0, 2), (0, 2, 1))
+AXES = ((2, 1, 0), (0, 2, 1), (1, 0, 2))
 
 
 def place(coords, core):
@@ -132,6 +132,23 @@
         compiler_params=LIMIT,
         name="unweave",
     )(table, own, came, last)
+
+
+def split_kernel(master, *outs):
+    for c, out in enumerate(outs):
+        out[...] = master[:, 2 * c : 2 * c + 2].astype(jnp.bfloat16)
+
+
+def split(master):
+    parts, _, experts, columns = master.shape
+    return pl.pallas_call(
+        split_kernel,
+        out_shape=[shape_of(parts, 2, experts, columns)] * CHAINS,
+        in_specs=[VMEM],
+        out_specs=[VMEM] * CHAINS,
+        compiler_params=LIMIT,
+        name="split",
+    )(master)
 
 
 def pick_kernel(table_ref, kept, one, rest, own, ahead, back):
@@ -339,12 +356,11 @@
     pairs = pairs.reshape(CHAINS, 2 * SIDE)
     table = jnp.concatenate([pairs, jnp.full((CHAINS, 1), core)], 1)
 
-    narrow = master.astype(jnp.bfloat16).transpose(1, 2, 0, 3)
     near = [axes[0] for axes in AXES]
     mid = [axes[1] for axes in AXES]
     last = [axes[2] for axes in AXES]
     each = range(CHAINS)
-    blocks = [narrow[:, 2 * c : 2 * c + 2] for c in each]
+    blocks = split(master.transpose(1, 2, 0, 3))
     ones = [hop(blocks[c], near[c], ONE) for c in each]
     both = [jnp.stack([blocks[c], ones[c]], 0) for c in each]
     rests = [hop(both[c], near[c], BACK) for c in each]
@@ -385,6 +401,8 @@
     hidden = [v[3] for v in seconds]
     pair = [v[4] for v in seconds]
     sent = exchange(seconds)
+    far_rows = rows_out(table[0], hidden, pair, weights, [], rows)
+    sent[1], far_rows = lax.optimization_barrier((sent[1], far_rows))
     merged = [merge(table[c], sent[c], experts) for c in each]
 
     def add(one, came):
@@ -395,7 +413,6 @@
         ones = [add(parts[c][1], came[c]) for c in each]
         return [(parts[c][0], came[c], hop(ones[c], axes[c], ONE)) for c in each]
 
-    far_rows = rows_out(table[0], hidden, pair, weights, [], rows)
     layer_out, input_grad = rows_out(
         table[0], hidden, pair, weights, [swap(r) for r in far_rows], 0
     )

time: 171 us -> 166 us (0.971)
  starting transfers between devices: 86.6 us -> 64.7 us
  waiting for transfers between devices: 40.8 us -> 58.8 us
    ppermute x36, starting transfers between devices: 84.9 us -> 62.2 us  [hop(): return lax.ppermute(value, BOTH, step_pairs(axis, offsets))]
    ppermute x36, waiting for transfers between devices: 40.3 us -> 58 us  [hop(): return lax.ppermute(value, BOTH, step_pairs(axis, offsets))]
  transfers between devices with their start and end apart: 44 -> 44, of which waited for: 17 -> 18; matrix products, arithmetic and copies ran while one was open for 2% -> 2% of each run, Pallas kernels for 20% -> 21%
where the time goes in v1:
time: 166 us; the launch traced here: 165 us
  starting transfers between devices  64.7 us (39%)
  waiting for transfers between devices  58.8 us (35%)
  Pallas kernels  34.4 us (21%)
  other arithmetic  4.46 us (3%)
  local copies, waits for them, and re-layouts  1.71 us (1%)
    ppermute x36, starting transfers between devices, hop(): return lax.ppermute(value, BOTH, step_pairs(axis, offsets))  62.2 us
    ppermute x36, waiting for transfers between devices, hop(): return lax.ppermute(value, BOTH, step_pairs(axis, offsets))  58 us
    pallas_call x3, Pallas kernels, second(): pl.pallas_call(second_kernel, out_shape=[shape_of(*lead, 2, 3, 32, column...  8.4 us
    pallas_call x2, Pallas kernels, rows_out(): pl.pallas_call(functools.partial(rows_kernel, start), out_shape=[shape_of...  8.16 us
    pallas_call x3, Pallas kernels, first(): pl.pallas_call(first_kernel, out_shape=[jax.ShapeDtypeStruct((3, rows, 12...  7.38 us
    pallas_call x3, Pallas kernels, merge(): pl.pallas_call(merge_kernel, out_shape=[shape_of(*lead, 3, experts, 8, co...  3.54 us
  transfers between devices with their start and end apart: 44, of which 18 were waited for; matrix products, arithmetic and copies ran while one was open for 2% of the time, Pallas kernels for 21%

profile of v1, /device:TPU:0, one launch (start us, length us, event | category | flops | bytes accessed | tf_op | source)
XLA Modules:
  0.0 165.3 jit_solution(3738543122587052345)
XLA Ops:
  1.7 1.7 %collective-permute-start = (bf16[3,2,8,1024]{3,2,1,0:T(8,128)(2,1)S(1)}, bf16[3,2,8,1024]{3,2,1,0:T(8,128)(2,1)S(1)}, u32[]{:S(2)}, u32[]{:S(2)}) collective-permute-start(bf16[3,2,8,1024]{3,2,1,0:T(8,128)(2,1)S(1)} %get-tuple-element.75.own), channel_id=1, source_target_pairs={{0,2},{1,7},{2,0},{3,5},{4,6},{5,3},{6,4},{7,1},{8,10},{9,15},{10,... | collective-permute-start | bytes 294920 | tf_op jit(solution)/shard_map/ppermute | solution.py:46
  3.4 1.6 collective-permute-start.4
  5.0 1.9 %collective-permute-start.12 = (bf16[3,2,8,1024]{3,2,1,0:T(8,128)(2,1)S(1)}, bf16[3,2,8,1024]{3,2,1,0:T(8,128)(2,1)S(1)}, u32[]{:S(2)}, u32[]{:S(2)}) collective-permute-start(bf16[3,2,8,1024]{3,2,1,0:T(8,128)(2,1)S(1)} %get-tuple-element.91.own), channel_id=1, source_target_pairs={{0,32},{1,97},{2,34},{3,99},{4,36},{5,101},{6,38},{7,103},{8,40},{... | collective-permute-start | bytes 294920 | tf_op jit(solution)/shard_map/ppermute | solution.py:46
  8.7 2.2 %collective-permute-start.1 = (bf16[2,3,2,8,1024]{4,3,2,1,0:T(8,128)(2,1)S(1)}, bf16[2,3,2,8,1024]{4,3,2,1,0:T(8,128)(2,1)S(1)}, u32[]{:S(2)}, u32[]{:S(2)}) collective-permute-start(bf16[2,3,2,8,1024]{4,3,2,1,0:T(8,128)(2,1)S(1)} %pad_maximum_fusion.10), channel_id=1, source_target_pairs={{0,6},{1,3},{2,4},{3,1},{4,2},{5,7},{6,0},{7,5},{8,14},{9,11},{10,... | collective-permute-start | bytes 589832 | tf_op jit(solution)/shard_map/ppermute | solution.py:46
  10.9 2.3 %collective-permute-start.5 = (bf16[2,3,2,8,1024]{4,3,2,1,0:T(8,128)(2,1)S(1)}, bf16[2,3,2,8,1024]{4,3,2,1,0:T(8,128)(2,1)S(1)}, u32[]{:S(2)}, u32[]{:S(2)}) collective-permute-start(bf16[2,3,2,8,1024]{4,3,2,1,0:T(8,128)(2,1)S(1)} %pad_maximum_fusion.11), channel_id=1, source_target_pairs={{0,24},{1,9},{2,26},{3,11},{4,28},{5,13},{6,30},{7,15},{8,16},{9,1... | collective-permute-start | bytes 589832 | tf_op jit(solution)/shard_map/ppermute | solution.py:46
  13.2 3.5 %collective-permute-start.13 = (bf16[2,3,2,8,1024]{4,3,2,1,0:T(8,128)(2,1)S(1)}, bf16[2,3,2,8,1024]{4,3,2,1,0:T(8,128)(2,1)S(1)}, u32[]{:S(2)}, u32[]{:S(2)}) collective-permute-start(bf16[2,3,2,8,1024]{4,3,2,1,0:T(8,128)(2,1)S(1)} %pad_maximum_fusion.12), channel_id=1, source_target_pairs={{0,96},{1,33},{2,98},{3,35},{4,100},{5,37},{6,102},{7,39},{8,104},... | collective-permute-start | bytes 589832 | tf_op jit(solution)/shard_map/ppermute | solution.py:46
  21.8 1.1 collective-permute-start.19
  23.0 2.4 %collective-permute-done.2.one = bf16[3,8,8,1024]{3,2,1,0:T(8,128)(2,1)S(1)} collective-permute-done((bf16[3,8,8,1024]{3,2,1,0:T(8,128)(2,1)S(1)}, bf16[3,8,8,1024]{3,2,1,0:T(8,128)(2,1)S(1)}, u32[]{:S(2)}, u32[]{:S(2)}) %collective-permute-start.2) | collective-permute-done | bytes 393248 | tf_op jit(solution)/shard_map/ppermute | solution.py:46
  25.4 1.3 collective-permute-start.3
  26.7 2.3 %collective-permute-done.14.one = bf16[3,8,8,1024]{3,2,1,0:T(8,128)(2,1)S(1)} collective-permute-done((bf16[3,8,8,1024]{3,2,1,0:T(8,128)(2,1)S(1)}, bf16[3,8,8,1024]{3,2,1,0:T(8,128)(2,1)S(1)}, u32[]{:S(2)}, u32[]{:S(2)}) %collective-permute-start.14) | collective-permute-done | bytes 393248 | tf_op jit(solution)/shard_map/ppermute | solution.py:46
  29.0 1.1 collective-permute-start.15
  31.3 3.0 %collective-permute-start.20 = (bf16[2,3,8,8,1024]{4,3,2,1,0:T(8,128)(2,1)S(1)}, bf16[2,3,8,8,1024]{4,3,2,1,0:T(8,128)(2,1)S(1)}, u32[]{:S(2)}, u32[]{:S(2)}) collective-permute-start(bf16[2,3,8,8,1024]{4,3,2,1,0:T(8,128)(2,1)S(1)} %pad_maximum_fusion.4), channel_id=1, source_target_pairs={{0,96},{1,33},{2,98},{3,35},{4,100},{5,37},{6,102},{7,39},{8,104},... | collective-permute-start | bytes 2359304 | tf_op jit(solution)/shard_map/ppermute | solution.py:46
  34.3 4.4 %collective-permute-done.3.rest = bf16[2,3,8,8,1024]{4,3,2,1,0:T(8,128)(2,1)S(1)} collective-permute-done((bf16[2,3,8,8,1024]{4,3,2,1,0:T(8,128)(2,1)S(1)}, bf16[2,3,8,8,1024]{4,3,2,1,0:T(8,128)(2,1)S(1)}, u32[]{:S(2)}, u32[]{:S(2)}) %collective-permute-start.3) | collective-permute-done | bytes 786464 | tf_op jit(solution)/shard_map/ppermute | solution.py:46
  39.8 2.5 %collective-permute-done.15.rest = bf16[2,3,8,8,1024]{4,3,2,1,0:T(8,128)(2,1)S(1)} collective-permute-done((bf16[2,3,8,8,1024]{4,3,2,1,0:T(8,128)(2,1)S(1)}, bf16[2,3,8,8,1024]{4,3,2,1,0:T(8,128)(2,1)S(1)}, u32[]{:S(2)}, u32[]{:S(2)}) %collective-permute-start.15) | collective-permute-done | bytes 786464 | tf_op jit(solution)/shard_map/ppermute | solution.py:46
  43.6 5.2 %collective-permute-done.20.rest = bf16[2,3,8,8,1024]{4,3,2,1,0:T(8,128)(2,1)S(1)} collective-permute-done((bf16[2,3,8,8,1024]{4,3,2,1,0:T(8,128)(2,1)S(1)}, bf16[2,3,8,8,1024]{4,3,2,1,0:T(8,128)(2,1)S(1)}, u32[]{:S(2)}, u32[]{:S(2)}) %collective-permute-start.20) | collective-permute-done | bytes 786464 | tf_op jit(solution)/shard_map/ppermute | solution.py:46
  49.4 3.0 %collective-permute-start.21 = (bf16[2,2,3,4,8,1024]{5,4,3,2,1,0:T(8,128)(2,1)S(1)}, bf16[2,2,3,4,8,1024]{5,4,3,2,1,0:T(8,128)(2,1)S(1)}, u32[]{:S(2)}, u32[]{:S(2)}) collective-permute-start(bf16[2,2,3,4,8,1024]{5,4,3,2,1,0:T(8,128)(2,1)S(1)} %get-tuple-element.99), channel_id=1, source_target_pairs={{0,2},{1,7},{2,0},{3,5},{4,6},{5,3},{6,4},{7,1},{8,10},{9,15},{10,... | collective-permute-start | bytes 2359304 | tf_op jit(solution)/shard_map/ppermute | solution.py:46
  52.5 3.8 %collective-permute-start.10 = (bf16[2,2,3,4,8,1024]{5,4,3,2,1,0:T(8,128)(2,1)S(1)}, bf16[2,2,3,4,8,1024]{5,4,3,2,1,0:T(8,128)(2,1)S(1)}, u32[]{:S(2)}, u32[]{:S(2)}) collective-permute-start(bf16[2,2,3,4,8,1024]{5,4,3,2,1,0:T(8,128)(2,1)S(1)} %pad_maximum_fusion.1), channel_id=1, source_target_pairs={{0,96},{1,33},{2,98},{3,35},{4,100},{5,37},{6,102},{7,39},{8,104},... | collective-permute-start | bytes 2359304 | tf_op jit(solution)/shard_map/ppermute | solution.py:46
  56.4 1.4 collective-permute-start.17
  57.8 8.3 %collective-permute-done.21 = bf16[2,2,3,4,8,1024]{5,4,3,2,1,0:T(8,128)(2,1)S(1)} collective-permute-done((bf16[2,2,3,4,8,1024]{5,4,3,2,1,0:T(8,128)(2,1)S(1)}, bf16[2,2,3,4,8,1024]{5,4,3,2,1,0:T(8,128)(2,1)S(1)}, u32[]{:S(2)}, u32[]{:S(2)}) %collective-permute-start.21) | collective-permute-done | bytes 786464 | tf_op jit(solution)/shard_map/ppermute | solution.py:46
  66.2 4.8 %collective-permute-start.22 = (bf16[2,2,3,4,8,1024]{5,4,3,2,1,0:T(8,128)(2,1)S(1)}, bf16[2,2,3,4,8,1024]{5,4,3,2,1,0:T(8,128)(2,1)S(1)}, u32[]{:S(2)}, u32[]{:S(2)}) collective-permute-start(bf16[2,2,3,4,8,1024]{5,4,3,2,1,0:T(8,128)(2,1)S(1)} %pad_maximum_fusion.5), channel_id=1, source_target_pairs={{0,6},{1,3},{2,4},{3,1},{4,2},{5,7},{6,0},{7,5},{8,14},{9,11},{10,... | collective-permute-start | bytes 2359304 | tf_op jit(solution)/shard_map/ppermute | solution.py:46
  70.9 2.5 %first.3 = (f32[3,1024,128]{2,1,0:T(8,128)S(1)}, bf16[2,3,4,32,1024]{4,3,2,1,0:T(8,128)(2,1)S(1)}) custom-call(s32[9]{0:T(128)S(1)} %get-tuple-element.150.table_ref, bf16[512,2048]{1,0:T(8,128)(2,1)S(1)} %copy-done, bf16[512,1024]{1,0:T(8,128)(2,1)S(1)} %collective-permute-done.6.tok1, bf16[512,2048]{1,0:T(8,128)(2,1)S(1)} %copy-done.1, ...), custom_call_target="tpu_custom_call" | custom-call | tf_op jit(solution)/shard_map/first/pallas_call | solution.py:198
  73.5 2.5 %first.4 = (f32[3,1024,128]{2,1,0:T(8,128)S(1)}, bf16[2,3,4,32,1024]{4,3,2,1,0:T(8,128)(2,1)S(1)}) custom-call(s32[9]{0:T(128)S(1)} %get-tuple-element.148.table_ref, bf16[512,2048]{1,0:T(8,128)(2,1)S(1)} %copy-done, bf16[512,1024]{1,0:T(8,128)(2,1)S(1)} %collective-permute-done.6.tok1, bf16[512,2048]{1,0:T(8,128)(2,1)S(1)} %copy-done.1, ...), custom_call_target="tpu_custom_call" | custom-call | tf_op jit(solution)/shard_map/first/pallas_call | solution.py:198
  76.7 4.2 %collective-permute-done.22 = bf16[2,2,3,4,8,1024]{5,4,3,2,1,0:T(8,128)(2,1)S(1)} collective-permute-done((bf16[2,2,3,4,8,1024]{5,4,3,2,1,0:T(8,128)(2,1)S(1)}, bf16[2,2,3,4,8,1024]{5,4,3,2,1,0:T(8,128)(2,1)S(1)}, u32[]{:S(2)}, u32[]{:S(2)}) %collective-permute-start.22) | collective-permute-done | bytes 786464 | tf_op jit(solution)/shard_map/ppermute | solution.py:46
  80.9 2.5 %first.5 = (f32[3,1024,128]{2,1,0:T(8,128)S(1)}, bf16[2,3,4,32,1024]{4,3,2,1,0:T(8,128)(2,1)S(1)}) custom-call(s32[9]{0:T(128)S(1)} %get-tuple-element.149.table_ref, bf16[512,2048]{1,0:T(8,128)(2,1)S(1)} %copy-done, bf16[512,1024]{1,0:T(8,128)(2,1)S(1)} %collective-permute-done.6.tok1, bf16[512,2048]{1,0:T(8,128)(2,1)S(1)} %copy-done.1, ...), custom_call_target="tpu_custom_call" | custom-call | tf_op jit(solution)/shard_map/first/pallas_call | solution.py:198
  83.5 2.8 %second.3 = (bf16[2,3,32,1024]{3,2,1,0:T(8,128)(2,1)S(1)}, bf16[2,2,3,32,1024]{4,3,2,1,0:T(8,128)(2,1)S(1)}, bf16[2,3,32,1024]{3,2,1,0:T(8,128)(2,1)S(1)}, bf16[...) custom-call(s32[9]{0:T(128)S(1)} %get-tuple-element.150.table_ref, bf16[512,2048]{1,0:T(8,128)(2,1)S(1)} %copy-done, ...), custom_call_target="tpu_custom_call" | custom-call | tf_op jit(solution)/shard_map/second/pallas_call | solution.py:263
  86.4 2.8 %second.4 = (bf16[2,3,32,1024]{3,2,1,0:T(8,128)(2,1)S(1)}, bf16[2,2,3,32,1024]{4,3,2,1,0:T(8,128)(2,1)S(1)}, bf16[2,3,32,1024]{3,2,1,0:T(8,128)(2,1)S(1)}, bf16[...) custom-call(s32[9]{0:T(128)S(1)} %get-tuple-element.148.table_ref, bf16[512,2048]{1,0:T(8,128)(2,1)S(1)} %copy-done, ...), custom_call_target="tpu_custom_call" | custom-call | tf_op jit(solution)/shard_map/second/pallas_call | solution.py:263
  89.3 2.8 %second.5 = (bf16[2,3,32,1024]{3,2,1,0:T(8,128)(2,1)S(1)}, bf16[2,2,3,32,1024]{4,3,2,1,0:T(8,128)(2,1)S(1)}, bf16[2,3,32,1024]{3,2,1,0:T(8,128)(2,1)S(1)}, bf16[...) custom-call(s32[9]{0:T(128)S(1)} %get-tuple-element.149.table_ref, bf16[512,2048]{1,0:T(8,128)(2,1)S(1)} %copy-done, ...), custom_call_target="tpu_custom_call" | custom-call | tf_op jit(solution)/shard_map/second/pallas_call | solution.py:263
  92.2 6.2 %collective-permute-done.28 = bf16[2,2,3,32,1024]{4,3,2,1,0:T(8,128)(2,1)S(1)} collective-permute-done((bf16[2,2,3,32,1024]{4,3,2,1,0:T(8,128)(2,1)S(1)}, bf16[2,2,3,32,1024]{4,3,2,1,0:T(8,128)(2,1)S(1)}, u32[]{:S(2)}, u32[]{:S(2)}) %collective-permute-start.28) | collective-permute-done | bytes 786464 | tf_op jit(solution)/shard_map/ppermute | solution.py:46
  98.5 3.5 %collective-permute-start.29 = (bf16[2,2,3,32,1024]{4,3,2,1,0:T(8,128)(2,1)S(1)}, bf16[2,2,3,32,1024]{4,3,2,1,0:T(8,128)(2,1)S(1)}, u32[]{:S(2)}, u32[]{:S(2)}) collective-permute-start(bf16[2,2,3,32,1024]{4,3,2,1,0:T(8,128)(2,1)S(1)} %pad_maximum_fusion.7), channel_id=1, source_target_pairs={{0,96},{1,33},{2,98},{3,35},{4,100},{5,37},{6,102},{7,39},{8,104},... | collective-permute-start | bytes 2359304 | tf_op jit(solution)/shard_map/ppermute | solution.py:46
  102.1 1.5 collective-permute-start.25
  104.3 3.3 %collective-permute-start.39 = (bf16[2,2,3,32,1024]{4,3,2,1,0:T(8,128)(2,1)S(1)}, bf16[2,2,3,32,1024]{4,3,2,1,0:T(8,128)(2,1)S(1)}, u32[]{:S(2)}, u32[]{:S(2)}) collective-permute-start(bf16[2,2,3,32,1024]{4,3,2,1,0:T(8,128)(2,1)S(1)} %pad_maximum_fusion.8), channel_id=1, source_target_pairs={{0,6},{1,3},{2,4},{3,1},{4,2},{5,7},{6,0},{7,5},{8,14},{9,11},{10,... | collective-permute-start | bytes 2359304 | tf_op jit(solution)/shard_map/ppermute | solution.py:46
  107.6 4.4 %collective-permute-done.29 = bf16[2,2,3,32,1024]{4,3,2,1,0:T(8,128)(2,1)S(1)} collective-permute-done((bf16[2,2,3,32,1024]{4,3,2,1,0:T(8,128)(2,1)S(1)}, bf16[2,2,3,32,1024]{4,3,2,1,0:T(8,128)(2,1)S(1)}, u32[]{:S(2)}, u32[]{:S(2)}) %collective-permute-start.29) | collective-permute-done | bytes 786464 | tf_op jit(solution)/shard_map/ppermute | solution.py:46
  112.0 1.2 merge.3
  113.2 1.7 %collective-permute-start.30 = (bf16[2,3,8,8,1024]{4,3,2,1,0:T(8,128)(2,1)S(1)}, bf16[2,3,8,8,1024]{4,3,2,1,0:T(8,128)(2,1)S(1)}, u32[]{:S(2)}, u32[]{:S(2)}) collective-permute-start(bf16[2,3,8,8,1024]{4,3,2,1,0:T(8,128)(2,1)S(1)} %get-tuple-element.122), channel_id=1, source_target_pairs={{0,24},{1,9},{2,26},{3,11},{4,28},{5,13},{6,30},{7,15},{8,16},{9,1... | collective-permute-start | bytes 2359304 | tf_op jit(solution)/shard_map/ppermute | solution.py:46
  114.9 3.1 %rows_out.2 = (bf16[512,1024]{1,0:T(8,128)(2,1)S(1)}, bf16[512,1024]{1,0:T(8,128)(2,1)S(1)}) custom-call(s32[9]{0:T(128)S(1)} %get-tuple-element.150.table_ref, bf16[1024,256]{1,0:T(8,128)(2,1)S(1)} %get-tuple-element.90.refs_0_, bf16[1024,256]{1,0:T(8,128)(2,1)S(1)} %get-tuple-element.96.refs_1_, bf16[1024,256]{1,0:T(8,128)(2,1)S(1)} %get-tuple-element.102.refs_2_, ...), custom_call_target="tpu_custom_call" | custom-call | tf_op jit(solution)/shard_map/rows_out/pallas_call | solution.py:306
  118.0 1.2 merge.4
  119.2 3.0 %collective-permute-start.34 = (bf16[2,3,8,8,1024]{4,3,2,1,0:T(8,128)(2,1)S(1)}, bf16[2,3,8,8,1024]{4,3,2,1,0:T(8,128)(2,1)S(1)}, u32[]{:S(2)}, u32[]{:S(2)}) collective-permute-start(bf16[2,3,8,8,1024]{4,3,2,1,0:T(8,128)(2,1)S(1)} %get-tuple-element.131), channel_id=1, source_target_pairs={{0,6},{1,3},{2,4},{3,1},{4,2},{5,7},{6,0},{7,5},{8,14},{9,11},{10,... | collective-permute-start | bytes 2359304 | tf_op jit(solution)/shard_map/ppermute | solution.py:46
  122.2 1.2 merge.5
  123.4 3.3 %collective-permute-start.40 = (bf16[2,3,8,8,1024]{4,3,2,1,0:T(8,128)(2,1)S(1)}, bf16[2,3,8,8,1024]{4,3,2,1,0:T(8,128)(2,1)S(1)}, u32[]{:S(2)}, u32[]{:S(2)}) collective-permute-start(bf16[2,3,8,8,1024]{4,3,2,1,0:T(8,128)(2,1)S(1)} %get-tuple-element.140), channel_id=1, source_target_pairs={{0,96},{1,33},{2,98},{3,35},{4,100},{5,37},{6,102},{7,39},{8,104},... | collective-permute-start | bytes 2359304 | tf_op jit(solution)/shard_map/ppermute | solution.py:46
  127.5 5.0 %collective-permute-done.34.came = bf16[2,3,8,8,1024]{4,3,2,1,0:T(8,128)(2,1)S(1)} collective-permute-done((bf16[2,3,8,8,1024]{4,3,2,1,0:T(8,128)(2,1)S(1)}, bf16[2,3,8,8,1024]{4,3,2,1,0:T(8,128)(2,1)S(1)}, u32[]{:S(2)}, u32[]{:S(2)}) %collective-permute-start.34) | collective-permute-done | bytes 786464 | tf_op jit(solution)/shard_map/ppermute | solution.py:46
  132.7 5.4 %collective-permute-done.40.came = bf16[2,3,8,8,1024]{4,3,2,1,0:T(8,128)(2,1)S(1)} collective-permute-done((bf16[2,3,8,8,1024]{4,3,2,1,0:T(8,128)(2,1)S(1)}, bf16[2,3,8,8,1024]{4,3,2,1,0:T(8,128)(2,1)S(1)}, u32[]{:S(2)}, u32[]{:S(2)}) %collective-permute-start.40) | collective-permute-done | bytes 786464 | tf_op jit(solution)/shard_map/ppermute | solution.py:46
  139.4 5.0 %rows_out.3 = (bf16[512,2048]{1,0:T(8,128)(2,1)}, bf16[512,2048]{1,0:T(8,128)(2,1)}) custom-call(s32[9]{0:T(128)S(1)} %get-tuple-element.150.table_ref, bf16[1024,256]{1,0:T(8,128)(2,1)S(1)} %get-tuple-element.90.refs_0_, bf16[1024,256]{1,0:T(8,128)(2,1)S(1)} %get-tuple-element.96.refs_1_, bf16[1024,256]{1,0:T(8,128)(2,1)S(1)} %get-tuple-element.102.refs_2_, ...), custom_call_target="tpu_custom_call" | custom-call | tf_op jit(solution)/shard_map/rows_out/pallas_call | solution.py:306
  145.2 3.8 %collective-permute-start.36 = (bf16[2,3,2,8,1024]{4,3,2,1,0:T(8,128)(2,1)S(1)}, bf16[2,3,2,8,1024]{4,3,2,1,0:T(8,128)(2,1)S(1)}, u32[]{:S(2)}, u32[]{:S(2)}) collective-permute-start(bf16[2,3,2,8,1024]{4,3,2,1,0:T(8,128)(2,1)S(1)} %get-tuple-element.134), channel_id=1, source_target_pairs={{0,96},{1,33},{2,98},{3,35},{4,100},{5,37},{6,102},{7,39},{8,104},... | collective-permute-start | bytes 589832 | tf_op jit(solution)/shard_map/ppermute | solution.py:46
  149.9 2.1 %collective-permute-start.42 = (bf16[2,3,2,8,1024]{4,3,2,1,0:T(8,128)(2,1)S(1)}, bf16[2,3,2,8,1024]{4,3,2,1,0:T(8,128)(2,1)S(1)}, u32[]{:S(2)}, u32[]{:S(2)}) collective-permute-start(bf16[2,3,2,8,1024]{4,3,2,1,0:T(8,128)(2,1)S(1)} %get-tuple-element.143), channel_id=1, source_target_pairs={{0,24},{1,9},{2,26},{3,11},{4,28},{5,13},{6,30},{7,15},{8,16},{9,1... | collective-permute-start | bytes 589832 | tf_op jit(solution)/shard_map/ppermute | solution.py:46
  154.3 2.6 %collective-permute-done.42 = bf16[2,3,2,8,1024]{4,3,2,1,0:T(8,128)(2,1)S(1)} collective-permute-done((bf16[2,3,2,8,1024]{4,3,2,1,0:T(8,128)(2,1)S(1)}, bf16[2,3,2,8,1024]{4,3,2,1,0:T(8,128)(2,1)S(1)}, u32[]{:S(2)}, u32[]{:S(2)}) %collective-permute-start.42) | collective-permute-done | bytes 196640 | tf_op jit(solution)/shard_map/ppermute | solution.py:46
  157.0 4.2 %collective-permute-start.43 = (bf16[3,2,8,1024]{3,2,1,0:T(8,128)(2,1)S(1)}, bf16[3,2,8,1024]{3,2,1,0:T(8,128)(2,1)S(1)}, u32[]{:S(2)}, u32[]{:S(2)}) collective-permute-start(bf16[3,2,8,1024]{3,2,1,0:T(8,128)(2,1)S(1)} %fusion.3), channel_id=1, source_target_pairs={{0,8},{1,25},{2,10},{3,27},{4,12},{5,29},{6,14},{7,31},{8,0},{9,17... | collective-permute-start | bytes 294920 | tf_op jit(solution)/shard_map/ppermute | solution.py:46
  161.3 2.5 %collective-permute-done.43 = bf16[3,2,8,1024]{3,2,1,0:T(8,128)(2,1)S(1)} collective-permute-done((bf16[3,2,8,1024]{3,2,1,0:T(8,128)(2,1)S(1)}, bf16[3,2,8,1024]{3,2,1,0:T(8,128)(2,1)S(1)}, u32[]{:S(2)}, u32[]{:S(2)}) %collective-permute-start.43) | collective-permute-done | bytes 98336 | tf_op jit(solution)/shard_map/ppermute | solution.py:46
  163.9 1.5 divide_subtract_fusion
  (112 shorter events, 21.1 us)
Async XLA Ops:
  1.7 17.0 %copy-start = (bf16[512,2048]{1,0:T(8,128)(2,1)S(1)}, bf16[512,2048]{1,0:T(8,128)(2,1)}, u32[]{:S(2)}) copy-start(bf16[512,2048]{1,0:T(8,128)(2,1)} %tok0.5) | copy-start | bytes 6291460
  1.7 6.9 %collective-permute-start = (bf16[3,2,8,1024]{3,2,1,0:T(8,128)(2,1)S(1)}, bf16[3,2,8,1024]{3,2,1,0:T(8,128)(2,1)S(1)}, u32[]{:S(2)}, u32[]{:S(2)}) collective-permute-start(bf16[3,2,8,1024]{3,2,1,0:T(8,128)(2,1)S(1)} %get-tuple-element.75.own), channel_id=1, source_target_pairs={{0,2},{1,7},{2,0},{3,5},{4,6},{5,3},{6,4},{7,1},{8,10},{9,15},{10,... | collective-permute-start | bytes 294920 | tf_op jit(solution)/shard_map/ppermute | solution.py:46
  3.4 7.5 %collective-permute-start.4 = (bf16[3,2,8,1024]{3,2,1,0:T(8,128)(2,1)S(1)}, bf16[3,2,8,1024]{3,2,1,0:T(8,128)(2,1)S(1)}, u32[]{:S(2)}, u32[]{:S(2)}) collective-permute-start(bf16[3,2,8,1024]{3,2,1,0:T(8,128)(2,1)S(1)} %get-tuple-element.76.own), channel_id=1, source_target_pairs={{0,8},{1,25},{2,10},{3,27},{4,12},{5,29},{6,14},{7,31},{8,0},{9,17... | collective-permute-start | bytes 294920 | tf_op jit(solution)/shard_map/ppermute | solution.py:46
  5.0 8.2 %collective-permute-start.12 = (bf16[3,2,8,1024]{3,2,1,0:T(8,128)(2,1)S(1)}, bf16[3,2,8,1024]{3,2,1,0:T(8,128)(2,1)S(1)}, u32[]{:S(2)}, u32[]{:S(2)}) collective-permute-start(bf16[3,2,8,1024]{3,2,1,0:T(8,128)(2,1)S(1)} %get-tuple-element.91.own), channel_id=1, source_target_pairs={{0,32},{1,97},{2,34},{3,99},{4,36},{5,101},{6,38},{7,103},{8,40},{... | collective-permute-start | bytes 294920 | tf_op jit(solution)/shard_map/ppermute | solution.py:46
  8.7 8.0 %collective-permute-start.1 = (bf16[2,3,2,8,1024]{4,3,2,1,0:T(8,128)(2,1)S(1)}, bf16[2,3,2,8,1024]{4,3,2,1,0:T(8,128)(2,1)S(1)}, u32[]{:S(2)}, u32[]{:S(2)}) collective-permute-start(bf16[2,3,2,8,1024]{4,3,2,1,0:T(8,128)(2,1)S(1)} %pad_maximum_fusion.10), channel_id=1, source_target_pairs={{0,6},{1,3},{2,4},{3,1},{4,2},{5,7},{6,0},{7,5},{8,14},{9,11},{10,... | collective-permute-start | bytes 589832 | tf_op jit(solution)/shard_map/ppermute | solution.py:46
  10.9 7.0 %collective-permute-start.5 = (bf16[2,3,2,8,1024]{4,3,2,1,0:T(8,128)(2,1)S(1)}, bf16[2,3,2,8,1024]{4,3,2,1,0:T(8,128)(2,1)S(1)}, u32[]{:S(2)}, u32[]{:S(2)}) collective-permute-start(bf16[2,3,2,8,1024]{4,3,2,1,0:T(8,128)(2,1)S(1)} %pad_maximum_fusion.11), channel_id=1, source_target_pairs={{0,24},{1,9},{2,26},{3,11},{4,28},{5,13},{6,30},{7,15},{8,16},{9,1... | collective-permute-start | bytes 589832 | tf_op jit(solution)/shard_map/ppermute | solution.py:46
  13.2 7.1 %collective-permute-start.13 = (bf16[2,3,2,8,1024]{4,3,2,1,0:T(8,128)(2,1)S(1)}, bf16[2,3,2,8,1024]{4,3,2,1,0:T(8,128)(2,1)S(1)}, u32[]{:S(2)}, u32[]{:S(2)}) collective-permute-start(bf16[2,3,2,8,1024]{4,3,2,1,0:T(8,128)(2,1)S(1)} %pad_maximum_fusion.12), channel_id=1, source_target_pairs={{0,96},{1,33},{2,98},{3,35},{4,100},{5,37},{6,102},{7,39},{8,104},... | collective-permute-start | bytes 589832 | tf_op jit(solution)/shard_map/ppermute | solution.py:46
  17.5 7.9 %collective-permute-start.2 = (bf16[3,8,8,1024]{3,2,1,0:T(8,128)(2,1)S(1)}, bf16[3,8,8,1024]{3,2,1,0:T(8,128)(2,1)S(1)}, u32[]{:S(2)}, u32[]{:S(2)}) collective-permute-start(bf16[3,8,8,1024]{3,2,1,0:T(8,128)(2,1)S(1)} %weave.3.kept), channel_id=1, source_target_pairs={{0,8},{1,25},{2,10},{3,27},{4,12},{5,29},{6,14},{7,31},{8,0},{9,17... | collective-permute-start | bytes 1179656 | tf_op jit(solution)/shard_map/ppermute | solution.py:46
  18.8 15.5 %collective-permute-start.6 = (bf16[512,1024]{1,0:T(8,128)(2,1)S(1)}, bf16[512,1024]{1,0:T(8,128)(2,1)S(1)}, u32[]{:S(2)}, u32[]{:S(2)}) collective-permute-start(bf16[512,1024]{1,0:T(8,128)(2,1)S(1)} %constant_dynamic-slice_fusion.1), channel_id=1, source_target_pairs={{0,1},{1,0},{2,3},{3,2},{4,5},{5,4},{6,7},{7,6},{8,9},{9,8},{10,11... | collective-permute-start | bytes 3145736 | tf_op jit(solution)/shard_map/ppermute | solution.py:50
  21.1 7.9 %collective-permute-start.14 = (bf16[3,8,8,1024]{3,2,1,0:T(8,128)(2,1)S(1)}, bf16[3,8,8,1024]{3,2,1,0:T(8,128)(2,1)S(1)}, u32[]{:S(2)}, u32[]{:S(2)}) collective-permute-start(bf16[3,8,8,1024]{3,2,1,0:T(8,128)(2,1)S(1)} %weave.5.kept), channel_id=1, source_target_pairs={{0,2},{1,7},{2,0},{3,5},{4,6},{5,3},{6,4},{7,1},{8,10},{9,15},{10,... | collective-permute-start | bytes 1179656 | tf_op jit(solution)/shard_map/ppermute | solution.py:46
  21.7 12.6 %collective-permute-start.7 = (bf16[512,1024]{1,0:T(8,128)(2,1)S(1)}, bf16[512,1024]{1,0:T(8,128)(2,1)S(1)}, u32[]{:S(2)}, u32[]{:S(2)}) collective-permute-start(bf16[512,1024]{1,0:T(8,128)(2,1)S(1)} %constant_dynamic-slice_fusion), channel_id=1, source_target_pairs={{0,1},{1,0},{2,3},{3,2},{4,5},{5,4},{6,7},{7,6},{8,9},{9,8},{10,11... | collective-permute-start | bytes 3145736 | tf_op jit(solution)/shard_map/ppermute | solution.py:50
  21.8 8.3 %collective-permute-start.19 = (bf16[3,8,8,1024]{3,2,1,0:T(8,128)(2,1)S(1)}, bf16[3,8,8,1024]{3,2,1,0:T(8,128)(2,1)S(1)}, u32[]{:S(2)}, u32[]{:S(2)}) collective-permute-start(bf16[3,8,8,1024]{3,2,1,0:T(8,128)(2,1)S(1)} %weave.4.kept), channel_id=1, source_target_pairs={{0,32},{1,97},{2,34},{3,99},{4,36},{5,101},{6,38},{7,103},{8,40},{... | collective-permute-start | bytes 1179656 | tf_op jit(solution)/shard_map/ppermute | solution.py:46
  25.4 13.3 %collective-permute-start.3 = (bf16[2,3,8,8,1024]{4,3,2,1,0:T(8,128)(2,1)S(1)}, bf16[2,3,8,8,1024]{4,3,2,1,0:T(8,128)(2,1)S(1)}, u32[]{:S(2)}, u32[]{:S(2)}) collective-permute-start(bf16[2,3,8,8,1024]{4,3,2,1,0:T(8,128)(2,1)S(1)} %pad_maximum_fusion), channel_id=1, source_target_pairs={{0,24},{1,9},{2,26},{3,11},{4,28},{5,13},{6,30},{7,15},{8,16},{9,1... | collective-permute-start | bytes 2359304 | tf_op jit(solution)/shard_map/ppermute | solution.py:46
  29.0 13.3 %collective-permute-start.15 = (bf16[2,3,8,8,1024]{4,3,2,1,0:T(8,128)(2,1)S(1)}, bf16[2,3,8,8,1024]{4,3,2,1,0:T(8,128)(2,1)S(1)}, u32[]{:S(2)}, u32[]{:S(2)}) collective-permute-start(bf16[2,3,8,8,1024]{4,3,2,1,0:T(8,128)(2,1)S(1)} %pad_maximum_fusion.2), channel_id=1, source_target_pairs={{0,6},{1,3},{2,4},{3,1},{4,2},{5,7},{6,0},{7,5},{8,14},{9,11},{10,... | collective-permute-start | bytes 2359304 | tf_op jit(solution)/shard_map/ppermute | solution.py:46
  30.1 1.2 collective-permute-start.8
  31.3 17.4 %collective-permute-start.20 = (bf16[2,3,8,8,1024]{4,3,2,1,0:T(8,128)(2,1)S(1)}, bf16[2,3,8,8,1024]{4,3,2,1,0:T(8,128)(2,1)S(1)}, u32[]{:S(2)}, u32[]{:S(2)}) collective-permute-start(bf16[2,3,8,8,1024]{4,3,2,1,0:T(8,128)(2,1)S(1)} %pad_maximum_fusion.4), channel_id=1, source_target_pairs={{0,96},{1,33},{2,98},{3,35},{4,100},{5,37},{6,102},{7,39},{8,104},... | collective-permute-start | bytes 2359304 | tf_op jit(solution)/shard_map/ppermute | solution.py:46
  39.5 12.8 %collective-permute-start.9 = (bf16[2,2,3,4,8,1024]{5,4,3,2,1,0:T(8,128)(2,1)S(1)}, bf16[2,2,3,4,8,1024]{5,4,3,2,1,0:T(8,128)(2,1)S(1)}, u32[]{:S(2)}, u32[]{:S(2)}) collective-permute-start(bf16[2,2,3,4,8,1024]{5,4,3,2,1,0:T(8,128)(2,1)S(1)} %get-tuple-element.87), channel_id=1, source_target_pairs={{0,32},{1,97},{2,34},{3,99},{4,36},{5,101},{6,38},{7,103},{8,40},{... | collective-permute-start | bytes 2359304 | tf_op jit(solution)/shard_map/ppermute | solution.py:46
  43.0 13.3 %collective-permute-start.16 = (bf16[2,2,3,4,8,1024]{5,4,3,2,1,0:T(8,128)(2,1)S(1)}, bf16[2,2,3,4,8,1024]{5,4,3,2,1,0:T(8,128)(2,1)S(1)}, u32[]{:S(2)}, u32[]{:S(2)}) collective-permute-start(bf16[2,2,3,4,8,1024]{5,4,3,2,1,0:T(8,128)(2,1)S(1)} %get-tuple-element.93), channel_id=1, source_target_pairs={{0,8},{1,25},{2,10},{3,27},{4,12},{5,29},{6,14},{7,31},{8,0},{9,17... | collective-permute-start | bytes 2359304 | tf_op jit(solution)/shard_map/ppermute | solution.py:46
  49.4 16.7 %collective-permute-start.21 = (bf16[2,2,3,4,8,1024]{5,4,3,2,1,0:T(8,128)(2,1)S(1)}, bf16[2,2,3,4,8,1024]{5,4,3,2,1,0:T(8,128)(2,1)S(1)}, u32[]{:S(2)}, u32[]{:S(2)}) collective-permute-start(bf16[2,2,3,4,8,1024]{5,4,3,2,1,0:T(8,128)(2,1)S(1)} %get-tuple-element.99), channel_id=1, source_target_pairs={{0,2},{1,7},{2,0},{3,5},{4,6},{5,3},{6,4},{7,1},{8,10},{9,15},{10,... | collective-permute-start | bytes 2359304 | tf_op jit(solution)/shard_map/ppermute | solution.py:46
  52.5 18.5 %collective-permute-start.10 = (bf16[2,2,3,4,8,1024]{5,4,3,2,1,0:T(8,128)(2,1)S(1)}, bf16[2,2,3,4,8,1024]{5,4,3,2,1,0:T(8,128)(2,1)S(1)}, u32[]{:S(2)}, u32[]{:S(2)}) collective-permute-start(bf16[2,2,3,4,8,1024]{5,4,3,2,1,0:T(8,128)(2,1)S(1)} %pad_maximum_fusion.1), channel_id=1, source_target_pairs={{0,96},{1,33},{2,98},{3,35},{4,100},{5,37},{6,102},{7,39},{8,104},... | collective-permute-start | bytes 2359304 | tf_op jit(solution)/shard_map/ppermute | solution.py:46
  56.4 17.1 %collective-permute-start.17 = (bf16[2,2,3,4,8,1024]{5,4,3,2,1,0:T(8,128)(2,1)S(1)}, bf16[2,2,3,4,8,1024]{5,4,3,2,1,0:T(8,128)(2,1)S(1)}, u32[]{:S(2)}, u32[]{:S(2)}) collective-permute-start(bf16[2,2,3,4,8,1024]{5,4,3,2,1,0:T(8,128)(2,1)S(1)} %pad_maximum_fusion.3), channel_id=1, source_target_pairs={{0,24},{1,9},{2,26},{3,11},{4,28},{5,13},{6,30},{7,15},{8,16},{9,1... | collective-permute-start | bytes 2359304 | tf_op jit(solution)/shard_map/ppermute | solution.py:46
  66.2 14.7 %collective-permute-start.22 = (bf16[2,2,3,4,8,1024]{5,4,3,2,1,0:T(8,128)(2,1)S(1)}, bf16[2,2,3,4,8,1024]{5,4,3,2,1,0:T(8,128)(2,1)S(1)}, u32[]{:S(2)}, u32[]{:S(2)}) collective-permute-start(bf16[2,2,3,4,8,1024]{5,4,3,2,1,0:T(8,128)(2,1)S(1)} %pad_maximum_fusion.5), channel_id=1, source_target_pairs={{0,6},{1,3},{2,4},{3,1},{4,2},{5,7},{6,0},{7,5},{8,14},{9,11},{10,... | collective-permute-start | bytes 2359304 | tf_op jit(solution)/shard_map/ppermute | solution.py:46
  73.4 10.1 %collective-permute-start.11 = (f32[3,1024,128]{2,1,0:T(8,128)S(1)}, f32[3,1024,128]{2,1,0:T(8,128)S(1)}, u32[]{:S(2)}, u32[]{:S(2)}) collective-permute-start(f32[3,1024,128]{2,1,0:T(8,128)S(1)} %get-tuple-element.89.sums), channel_id=1, source_target_pairs={{0,1},{1,0},{2,3},{3,2},{4,5},{5,4},{6,7},{7,6},{8,9},{9,8},{10,11... | collective-permute-start | bytes 4718600 | tf_op jit(solution)/shard_map/ppermute | solution.py:50
  76.0 10.4 %collective-permute-start.18 = (f32[3,1024,128]{2,1,0:T(8,128)S(1)}, f32[3,1024,128]{2,1,0:T(8,128)S(1)}, u32[]{:S(2)}, u32[]{:S(2)}) collective-permute-start(f32[3,1024,128]{2,1,0:T(8,128)S(1)} %get-tuple-element.95.sums), channel_id=1, source_target_pairs={{0,1},{1,0},{2,3},{3,2},{4,5},{5,4},{6,7},{7,6},{8,9},{9,8},{10,11... | collective-permute-start | bytes 4718600 | tf_op jit(solution)/shard_map/ppermute | solution.py:50
  83.4 5.9 %collective-permute-start.23 = (f32[3,1024,128]{2,1,0:T(8,128)S(1)}, f32[3,1024,128]{2,1,0:T(8,128)S(1)}, u32[]{:S(2)}, u32[]{:S(2)}) collective-permute-start(f32[3,1024,128]{2,1,0:T(8,128)S(1)} %get-tuple-element.101.sums), channel_id=1, source_target_pairs={{0,1},{1,0},{2,3},{3,2},{4,5},{5,4},{6,7},{7,6},{8,9},{9,8},{10,11... | collective-permute-start | bytes 4718600 | tf_op jit(solution)/shard_map/ppermute | solution.py:50
  86.3 12.1 %collective-permute-start.28 = (bf16[2,2,3,32,1024]{4,3,2,1,0:T(8,128)(2,1)S(1)}, bf16[2,2,3,32,1024]{4,3,2,1,0:T(8,128)(2,1)S(1)}, u32[]{:S(2)}, u32[]{:S(2)}) collective-permute-start(bf16[2,2,3,32,1024]{4,3,2,1,0:T(8,128)(2,1)S(1)} %get-tuple-element.119), channel_id=1, source_target_pairs={{0,32},{1,97},{2,34},{3,99},{4,36},{5,101},{6,38},{7,103},{8,40},{... | collective-permute-start | bytes 2359304 | tf_op jit(solution)/shard_map/ppermute | solution.py:46
  89.2 12.8 %collective-permute-start.24 = (bf16[2,2,3,32,1024]{4,3,2,1,0:T(8,128)(2,1)S(1)}, bf16[2,2,3,32,1024]{4,3,2,1,0:T(8,128)(2,1)S(1)}, u32[]{:S(2)}, u32[]{:S(2)}) collective-permute-start(bf16[2,2,3,32,1024]{4,3,2,1,0:T(8,128)(2,1)S(1)} %get-tuple-element.110), channel_id=1, source_target_pairs={{0,8},{1,25},{2,10},{3,27},{4,12},{5,29},{6,14},{7,31},{8,0},{9,17... | collective-permute-start | bytes 2359304 | tf_op jit(solution)/shard_map/ppermute | solution.py:46
  92.1 12.1 %collective-permute-start.38 = (bf16[2,2,3,32,1024]{4,3,2,1,0:T(8,128)(2,1)S(1)}, bf16[2,2,3,32,1024]{4,3,2,1,0:T(8,128)(2,1)S(1)}, u32[]{:S(2)}, u32[]{:S(2)}) collective-permute-start(bf16[2,2,3,32,1024]{4,3,2,1,0:T(8,128)(2,1)S(1)} %get-tuple-element.137), channel_id=1, source_target_pairs={{0,2},{1,7},{2,0},{3,5},{4,6},{5,3},{6,4},{7,1},{8,10},{9,15},{10,... | collective-permute-start | bytes 2359304 | tf_op jit(solution)/shard_map/ppermute | solution.py:46
  98.5 13.5 %collective-permute-start.29 = (bf16[2,2,3,32,1024]{4,3,2,1,0:T(8,128)(2,1)S(1)}, bf16[2,2,3,32,1024]{4,3,2,1,0:T(8,128)(2,1)S(1)}, u32[]{:S(2)}, u32[]{:S(2)}) collective-permute-start(bf16[2,2,3,32,1024]{4,3,2,1,0:T(8,128)(2,1)S(1)} %pad_maximum_fusion.7), channel_id=1, source_target_pairs={{0,96},{1,33},{2,98},{3,35},{4,100},{5,37},{6,102},{7,39},{8,104},... | collective-permute-start | bytes 2359304 | tf_op jit(solution)/shard_map/ppermute | solution.py:46
  102.1 15.9 %collective-permute-start.25 = (bf16[2,2,3,32,1024]{4,3,2,1,0:T(8,128)(2,1)S(1)}, bf16[2,2,3,32,1024]{4,3,2,1,0:T(8,128)(2,1)S(1)}, u32[]{:S(2)}, u32[]{:S(2)}) collective-permute-start(bf16[2,2,3,32,1024]{4,3,2,1,0:T(8,128)(2,1)S(1)} %pad_maximum_fusion.6), channel_id=1, source_target_pairs={{0,24},{1,9},{2,26},{3,11},{4,28},{5,13},{6,30},{7,15},{8,16},{9,1... | collective-permute-start | bytes 2359304 | tf_op jit(solution)/shard_map/ppermute | solution.py:46
  104.3 17.9 %collective-permute-start.39 = (bf16[2,2,3,32,1024]{4,3,2,1,0:T(8,128)(2,1)S(1)}, bf16[2,2,3,32,1024]{4,3,2,1,0:T(8,128)(2,1)S(1)}, u32[]{:S(2)}, u32[]{:S(2)}) collective-permute-start(bf16[2,2,3,32,1024]{4,3,2,1,0:T(8,128)(2,1)S(1)} %pad_maximum_fusion.8), channel_id=1, source_target_pairs={{0,6},{1,3},{2,4},{3,1},{4,2},{5,7},{6,0},{7,5},{8,14},{9,11},{10,... | collective-permute-start | bytes 2359304 | tf_op jit(solution)/shard_map/ppermute | solution.py:46
  113.2 14.1 %collective-permute-start.30 = (bf16[2,3,8,8,1024]{4,3,2,1,0:T(8,128)(2,1)S(1)}, bf16[2,3,8,8,1024]{4,3,2,1,0:T(8,128)(2,1)S(1)}, u32[]{:S(2)}, u32[]{:S(2)}) collective-permute-start(bf16[2,3,8,8,1024]{4,3,2,1,0:T(8,128)(2,1)S(1)} %get-tuple-element.122), channel_id=1, source_target_pairs={{0,24},{1,9},{2,26},{3,11},{4,28},{5,13},{6,30},{7,15},{8,16},{9,1... | collective-permute-start | bytes 2359304 | tf_op jit(solution)/shard_map/ppermute | solution.py:46
  119.2 13.3 %collective-permute-start.34 = (bf16[2,3,8,8,1024]{4,3,2,1,0:T(8,128)(2,1)S(1)}, bf16[2,3,8,8,1024]{4,3,2,1,0:T(8,128)(2,1)S(1)}, u32[]{:S(2)}, u32[]{:S(2)}) collective-permute-start(bf16[2,3,8,8,1024]{4,3,2,1,0:T(8,128)(2,1)S(1)} %get-tuple-element.131), channel_id=1, source_target_pairs={{0,6},{1,3},{2,4},{3,1},{4,2},{5,7},{6,0},{7,5},{8,14},{9,11},{10,... | collective-permute-start | bytes 2359304 | tf_op jit(solution)/shard_map/ppermute | solution.py:46
  123.4 14.7 %collective-permute-start.40 = (bf16[2,3,8,8,1024]{4,3,2,1,0:T(8,128)(2,1)S(1)}, bf16[2,3,8,8,1024]{4,3,2,1,0:T(8,128)(2,1)S(1)}, u32[]{:S(2)}, u32[]{:S(2)}) collective-permute-start(bf16[2,3,8,8,1024]{4,3,2,1,0:T(8,128)(2,1)S(1)} %get-tuple-element.140), channel_id=1, source_target_pairs={{0,96},{1,33},{2,98},{3,35},{4,100},{5,37},{6,102},{7,39},{8,104},... | collective-permute-start | bytes 2359304 | tf_op jit(solution)/shard_map/ppermute | solution.py:46
  126.7 12.6 %collective-permute-start.26 = (bf16[512,1024]{1,0:T(8,128)(2,1)S(1)}, bf16[512,1024]{1,0:T(8,128)(2,1)S(1)}, u32[]{:S(2)}, u32[]{:S(2)}) collective-permute-start(bf16[512,1024]{1,0:T(8,128)(2,1)S(1)} %get-tuple-element.114), channel_id=1, source_target_pairs={{0,1},{1,0},{2,3},{3,2},{4,5},{5,4},{6,7},{7,6},{8,9},{9,8},{10,11... | collective-permute-start | bytes 3145736 | tf_op jit(solution)/shard_map/ppermute | solution.py:50
  126.7 12.6 %collective-permute-start.27 = (bf16[512,1024]{1,0:T(8,128)(2,1)S(1)}, bf16[512,1024]{1,0:T(8,128)(2,1)S(1)}, u32[]{:S(2)}, u32[]{:S(2)}) collective-permute-start(bf16[512,1024]{1,0:T(8,128)(2,1)S(1)} %get-tuple-element.115), channel_id=1, source_target_pairs={{0,1},{1,0},{2,3},{3,2},{4,5},{5,4},{6,7},{7,6},{8,9},{9,8},{10,11... | collective-permute-start | bytes 3145736 | tf_op jit(solution)/shard_map/ppermute | solution.py:50
  127.4 11.0 %collective-permute-start.31 = (bf16[3,8,8,1024]{3,2,1,0:T(8,128)(2,1)S(1)}, bf16[3,8,8,1024]{3,2,1,0:T(8,128)(2,1)S(1)}, u32[]{:S(2)}, u32[]{:S(2)}) collective-permute-start(bf16[3,8,8,1024]{3,2,1,0:T(8,128)(2,1)S(1)} %fusion.2), channel_id=1, source_target_pairs={{0,8},{1,25},{2,10},{3,27},{4,12},{5,29},{6,14},{7,31},{8,0},{9,17... | collective-permute-start | bytes 1179656 | tf_op jit(solution)/shard_map/ppermute | solution.py:46
  132.6 11.8 %collective-permute-start.35 = (bf16[3,8,8,1024]{3,2,1,0:T(8,128)(2,1)S(1)}, bf16[3,8,8,1024]{3,2,1,0:T(8,128)(2,1)S(1)}, u32[]{:S(2)}, u32[]{:S(2)}) collective-permute-start(bf16[3,8,8,1024]{3,2,1,0:T(8,128)(2,1)S(1)} %fusion.1), channel_id=1, source_target_pairs={{0,2},{1,7},{2,0},{3,5},{4,6},{5,3},{6,4},{7,1},{8,10},{9,15},{10,... | collective-permute-start | bytes 1179656 | tf_op jit(solution)/shard_map/ppermute | solution.py:46
  138.3 10.7 %collective-permute-start.41 = (bf16[3,8,8,1024]{3,2,1,0:T(8,128)(2,1)S(1)}, bf16[3,8,8,1024]{3,2,1,0:T(8,128)(2,1)S(1)}, u32[]{:S(2)}, u32[]{:S(2)}) collective-permute-start(bf16[3,8,8,1024]{3,2,1,0:T(8,128)(2,1)S(1)} %fusion), channel_id=1, source_target_pairs={{0,32},{1,97},{2,34},{3,99},{4,36},{5,101},{6,38},{7,103},{8,40},{... | collective-permute-start | bytes 1179656 | tf_op jit(solution)/shard_map/ppermute | solution.py:46
  139.3 12.7 %collective-permute-start.32 = (bf16[2,3,2,8,1024]{4,3,2,1,0:T(8,128)(2,1)S(1)}, bf16[2,3,2,8,1024]{4,3,2,1,0:T(8,128)(2,1)S(1)}, u32[]{:S(2)}, u32[]{:S(2)}) collective-permute-start(bf16[2,3,2,8,1024]{4,3,2,1,0:T(8,128)(2,1)S(1)} %get-tuple-element.125), channel_id=1, source_target_pairs={{0,6},{1,3},{2,4},{3,1},{4,2},{5,7},{6,0},{7,5},{8,14},{9,11},{10,... | collective-permute-start | bytes 589832 | tf_op jit(solution)/shard_map/ppermute | solution.py:46
  145.2 8.0 %collective-permute-start.36 = (bf16[2,3,2,8,1024]{4,3,2,1,0:T(8,128)(2,1)S(1)}, bf16[2,3,2,8,1024]{4,3,2,1,0:T(8,128)(2,1)S(1)}, u32[]{:S(2)}, u32[]{:S(2)}) collective-permute-start(bf16[2,3,2,8,1024]{4,3,2,1,0:T(8,128)(2,1)S(1)} %get-tuple-element.134), channel_id=1, source_target_pairs={{0,96},{1,33},{2,98},{3,35},{4,100},{5,37},{6,102},{7,39},{8,104},... | collective-permute-start | bytes 589832 | tf_op jit(solution)/shard_map/ppermute | solution.py:46
  149.9 14.0 %copy-start.3 = (f32[8,3,6,1024]{3,0,2,1:T(8,128)S(1)}, f32[8,3,6,1024]{3,0,2,1:T(8,128)}, u32[]{:S(2)}) copy-start(f32[8,3,6,1024]{3,0,2,1:T(8,128)} %param.13) | copy-start | bytes 1769476
  149.9 14.0 %copy-start.4 = (f32[8,3,6,1024]{3,0,2,1:T(8,128)S(1)}, f32[8,3,6,1024]{3,0,2,1:T(8,128)}, u32[]{:S(2)}) copy-start(f32[8,3,6,1024]{3,0,2,1:T(8,128)} %param.14) | copy-start | bytes 1769476
  149.9 14.0 %copy-start.5 = (f32[8,3,6,1024]{3,0,2,1:T(8,128)S(1)}, f32[8,3,6,1024]{3,0,2,1:T(8,128)}, u32[]{:S(2)}) copy-start(f32[8,3,6,1024]{3,0,2,1:T(8,128)} %param.15) | copy-start | bytes 1769476
  149.9 7.0 %collective-permute-start.42 = (bf16[2,3,2,8,1024]{4,3,2,1,0:T(8,128)(2,1)S(1)}, bf16[2,3,2,8,1024]{4,3,2,1,0:T(8,128)(2,1)S(1)}, u32[]{:S(2)}, u32[]{:S(2)}) collective-permute-start(bf16[2,3,2,8,1024]{4,3,2,1,0:T(8,128)(2,1)S(1)} %get-tuple-element.143), channel_id=1, source_target_pairs={{0,24},{1,9},{2,26},{3,11},{4,28},{5,13},{6,30},{7,15},{8,16},{9,1... | collective-permute-start | bytes 589832 | tf_op jit(solution)/shard_map/ppermute | solution.py:46
  152.0 9.2 %collective-permute-start.33 = (bf16[3,2,8,1024]{3,2,1,0:T(8,128)(2,1)S(1)}, bf16[3,2,8,1024]{3,2,1,0:T(8,128)(2,1)S(1)}, u32[]{:S(2)}, u32[]{:S(2)}) collective-permute-start(bf16[3,2,8,1024]{3,2,1,0:T(8,128)(2,1)S(1)} %fusion.7), channel_id=1, source_target_pairs={{0,2},{1,7},{2,0},{3,5},{4,6},{5,3},{6,4},{7,1},{8,10},{9,15},{10,... | collective-permute-start | bytes 294920 | tf_op jit(solution)/shard_map/ppermute | solution.py:46
  153.3 7.9 %collective-permute-start.37 = (bf16[3,2,8,1024]{3,2,1,0:T(8,128)(2,1)S(1)}, bf16[3,2,8,1024]{3,2,1,0:T(8,128)(2,1)S(1)}, u32[]{:S(2)}, u32[]{:S(2)}) collective-permute-start(bf16[3,2,8,1024]{3,2,1,0:T(8,128)(2,1)S(1)} %fusion.5), channel_id=1, source_target_pairs={{0,32},{1,97},{2,34},{3,99},{4,36},{5,101},{6,38},{7,103},{8,40},{... | collective-permute-start | bytes 294920 | tf_op jit(solution)/shard_map/ppermute | solution.py:46
  157.0 6.8 %collective-permute-start.43 = (bf16[3,2,8,1024]{3,2,1,0:T(8,128)(2,1)S(1)}, bf16[3,2,8,1024]{3,2,1,0:T(8,128)(2,1)S(1)}, u32[]{:S(2)}, u32[]{:S(2)}) collective-permute-start(bf16[3,2,8,1024]{3,2,1,0:T(8,128)(2,1)S(1)} %fusion.3), channel_id=1, source_target_pairs={{0,8},{1,25},{2,10},{3,27},{4,12},{5,29},{6,14},{7,31},{8,0},{9,17... | collective-permute-start | bytes 294920 | tf_op jit(solution)/shard_map/ppermute | solution.py:46
  (3 other events, 8.8 us)

commit v2 on v1

--- a/solution.py
+++ b/solution.py
@@ -274,19 +274,25 @@
 
 def rows_kernel(start, table_ref, *refs):
     hidden, pair, weights = refs[0:3], refs[3:6], refs[6:9]
-    added, (layer_out, grad_out) = refs[9:-2], refs[-2:]
     columns = weights[0].shape[-1]
-    rows = slice(start, start + layer_out.shape[0])
+    count = hidden[0].shape[0] // 2
+    rows = slice(start, start + count)
     step = 512
-    if added:
+    copies = []
+    if start:
+        outs = refs[9:]
+        ready = outs
+    else:
+        got, outs, (ready, sems) = refs[9:11], refs[11:13], refs[13:]
         core = table_ref[8]
         near = pl.multiple_of(core * columns, columns)
         far = pl.ds(pl.multiple_of((1 - core) * columns, columns), columns)
-        layer_out[:, far] = added[0][...]
-        grad_out[:, far] = added[1][...]
+        for i in range(2):
+            copies.append(pltpu.make_async_copy(got[i], outs[i].at[:, far], sems.at[i]))
+            copies[-1].start()
+        ready = [ready.at[i] for i in range(2)]
     for c in range(0, columns, step):
         part = slice(c, c + step)
-        cols = pl.ds(near + c, step) if added else part
         layer = 0.0
         grad = 0.0
         for chain in range(CHAINS):
@@ -296,18 +302,28 @@
             for k in range(2):
                 both = w[k, 0:2, :, :, part].reshape(256, step)
                 grad = grad + matmul(pair[chain][rows, 256 * k : 256 * k + 256], both)
-        layer_out[:, cols] = layer.astype(jnp.bfloat16)
-        grad_out[:, cols] = grad.astype(jnp.bfloat16)
+        ready[0][:, part] = layer.astype(jnp.bfloat16)
+        ready[1][:, part] = grad.astype(jnp.bfloat16)
+        if not start:
+            for i in range(2):
+                target = outs[i].at[:, pl.ds(near + c, step)]
+                sem = sems.at[len(copies)]
+                copies.append(pltpu.make_async_copy(ready[i].at[:, part], target, sem))
+                copies[-1].start()
+    for copy in copies:
+        copy.wait()
 
 
 def rows_out(table, hidden, pair, weights, added, start):
     columns = weights[0].shape[-1]
     rows = hidden[0].shape[0] // 2
+    scratch = [pltpu.VMEM((2, rows, columns), jnp.bfloat16), pltpu.SemaphoreType.DMA((6,))]
     return pl.pallas_call(
         functools.partial(rows_kernel, start),
-        out_shape=[shape_of(rows, 2 * columns if added else columns)] * 2,
+        out_shape=[shape_of(rows, columns if start else 2 * columns)] * 2,
         in_specs=[SMEM] + [VMEM] * (9 + len(added)),
-        out_specs=[VMEM] * 2,
+        out_specs=[VMEM if start else pl.BlockSpec(memory_space=pl.ANY)] * 2,
+        scratch_shapes=[] if start else scratch,
         compiler_params=pltpu.CompilerParams(vmem_limit_bytes=24 * 1024 * 1024),
         name="rows_out",
     )(table, *hidden, *pair, *weights, *added)
@@ -347,6 +363,24 @@
     columns = master.shape[3]
     rows = tokens.shape[0]
 
+    near = [axes[0] for axes in AXES]
+    mid = [axes[1] for axes in AXES]
+    last = [axes[2] for axes in AXES]
+    each = range(CHAINS)
+    blocks = split(master.transpose(1, 2, 0, 3))
+    ones = [hop(blocks[c], near[c], ONE) for c in each]
+    both = [jnp.stack([blocks[c], ones[c]], 0) for c in each]
+    rests = [hop(both[c], near[c], BACK) for c in each]
+    cores = jnp.full((9,), core)
+    lines = [weave(cores, blocks[c], ones[c], rests[c]) for c in each]
+
+    def other_rows(*rows):
+        far = (1 - core) * columns
+        return [lax.dynamic_slice_in_dim(v, far, columns, 1) for v in rows]
+
+    lines[0], tokens, cotangent, row_slot, placement = lax.optimization_barrier(
+        (lines[0], tokens, cotangent, row_slot, placement)
+    )
     steps = np.array(
         [[[step[c] << SHIFTS[axes[2]] for step in STEPS] for axes in AXES] for c in range(2)], np.int32
     ).reshape(2, -1)
@@ -356,23 +390,6 @@
     pairs = pairs.reshape(CHAINS, 2 * SIDE)
     table = jnp.concatenate([pairs, jnp.full((CHAINS, 1), core)], 1)
 
-    near = [axes[0] for axes in AXES]
-    mid = [axes[1] for axes in AXES]
-    last = [axes[2] for axes in AXES]
-    each = range(CHAINS)
-    blocks = split(master.transpose(1, 2, 0, 3))
-    ones = [hop(blocks[c], near[c], ONE) for c in each]
-    both = [jnp.stack([blocks[c], ones[c]], 0) for c in each]
-    rests = [hop(both[c], near[c], BACK) for c in each]
-    lines = [weave(table[c], blocks[c], ones[c], rests[c]) for c in each]
-
-    def other_rows(*rows):
-        far = (1 - core) * columns
-        return [lax.dynamic_slice_in_dim(v, far, columns, 1) for v in rows]
-
-    lines[2], tokens, cotangent, row_slot = lax.optimization_barrier(
-        (lines[2], tokens, cotangent, row_slot)
-    )
     far_tokens, far_cotangent = other_rows(tokens, cotangent)
     rows_in = [tokens, swap(far_tokens), cotangent, swap(far_cotangent)]
     slots = jnp.concatenate([row_slot, swap(row_slot)], 0)

time: 166 us -> 166 us (level)
  waiting for transfers between devices: 58.8 us -> 47.7 us
  Pallas kernels: 34.4 us -> 40 us
  local copies, waits for them, and re-layouts: 1.71 us -> 6.71 us
  starting transfers between devices: 64.7 us -> 61.9 us
  other arithmetic: 4.46 us -> 6.63 us
    ppermute x36, waiting for transfers between devices: 58 us -> 47.7 us  [hop(): return lax.ppermute(value, BOTH, step_pairs(axis, offsets))]
    ppermute x36, starting transfers between devices: 62.2 us -> 58.2 us  [hop(): return lax.ppermute(value, BOTH, step_pairs(axis, offsets))]
    unnamed x14 -> x58, local copies, waits for them, and re-layouts: 1.09 us -> 4.14 us
    another operation x3, other arithmetic: 0.22 us -> 3 us  [shards(): both = [jnp.stack([lines[c], ones[c]], 0) for c in each]]
    pallas_call x3, Pallas kernels: 7.38 us -> 9.47 us  [first(): pl.pallas_call(first_kernel, out_shape=[jax.ShapeDtypeStruct((3, rows, 12...]
    pallas_call x3, Pallas kernels: 8.4 us -> 10.4 us  [second(): pl.pallas_call(second_kernel, out_shape=[shape_of(*lead, 2, 3, 32, column...]
    dynamic_slice x2, local copies, waits for them, and re-layouts: 0.19 us -> 2.14 us  [other_rows(): return [lax.dynamic_slice_in_dim(v, far, columns, 1) for v in rows]]
    pallas_call x3, Pallas kernels: 1.96 us -> 3.87 us  [pick(): pl.pallas_call(pick_kernel, out_shape=[shape_of(*lead, 2, 3, 4, 8, column...]
  transfers between devices with their start and end apart: 44 -> 44, of which waited for: 18 -> 17; matrix products, arithmetic and copies ran while one was open for 2% -> 5% of each run, Pallas kernels for 21% -> 24%
where the time goes in v2:
time: 166 us; the launch traced here: 164 us
  starting transfers between devices  61.9 us (37%)
  waiting for transfers between devices  47.7 us (29%)
  Pallas kernels  40 us (24%)
  local copies, waits for them, and re-layouts  6.71 us (4%)
  other arithmetic  6.63 us (4%)
    ppermute x36, starting transfers between devices, hop(): return lax.ppermute(value, BOTH, step_pairs(axis, offsets))  58.2 us
    ppermute x36, waiting for transfers between devices, hop(): return lax.ppermute(value, BOTH, step_pairs(axis, offsets))  47.7 us
    pallas_call x3, Pallas kernels, second(): pl.pallas_call(second_kernel, out_shape=[shape_of(*lead, 2, 3, 32, column...  10.4 us
    pallas_call x3, Pallas kernels, first(): pl.pallas_call(first_kernel, out_shape=[jax.ShapeDtypeStruct((3, rows, 12...  9.47 us
    pallas_call x2, Pallas kernels, rows_out(): pl.pallas_call(functools.partial(rows_kernel, start), out_shape=[shape_of...  7.73 us
    unnamed x58, local copies, waits for them, and re-layouts  4.14 us
    pallas_call x3, Pallas kernels, pick(): pl.pallas_call(pick_kernel, out_shape=[shape_of(*lead, 2, 3, 4, 8, column...  3.87 us
    ppermute x8, starting transfers between devices, swap(): return lax.ppermute(value, BOTH, CORE_PAIRS)  3.78 us
  transfers between devices with their start and end apart: 44, of which 17 were waited for; matrix products, arithmetic and copies ran while one was open for 5% of the time, Pallas kernels for 24%

profile of v2, /device:TPU:0, one launch (start us, length us, event | category | flops | bytes accessed | tf_op | source)
XLA Modules:
  0.0 164.4 jit_solution(8732481725031745953)
XLA Ops:
  0.7 1.2 copy-done.7
  1.9 1.7 %collective-permute-start = (bf16[3,2,8,1024]{3,2,1,0:T(8,128)(2,1)S(1)}, bf16[3,2,8,1024]{3,2,1,0:T(8,128)(2,1)S(1)}, u32[]{:S(2)}, u32[]{:S(2)}) collective-permute-start(bf16[3,2,8,1024]{3,2,1,0:T(8,128)(2,1)S(1)} %get-tuple-element.76.own), channel_id=1, source_target_pairs={{0,2},{1,7},{2,0},{3,5},{4,6},{5,3},{6,4},{7,1},{8,10},{9,15},{10,... | collective-permute-start | bytes 294920 | tf_op jit(solution)/shard_map/ppermute | solution.py:46
  3.6 1.6 collective-permute-start.17
  5.1 1.9 %collective-permute-start.10 = (bf16[3,2,8,1024]{3,2,1,0:T(8,128)(2,1)S(1)}, bf16[3,2,8,1024]{3,2,1,0:T(8,128)(2,1)S(1)}, u32[]{:S(2)}, u32[]{:S(2)}) collective-permute-start(bf16[3,2,8,1024]{3,2,1,0:T(8,128)(2,1)S(1)} %get-tuple-element.93.own), channel_id=1, source_target_pairs={{0,32},{1,97},{2,34},{3,99},{4,36},{5,101},{6,38},{7,103},{8,40},{... | collective-permute-start | bytes 294920 | tf_op jit(solution)/shard_map/ppermute | solution.py:46
  7.1 2.5 %collective-permute-start.1 = (bf16[2,3,2,8,1024]{4,3,2,1,0:T(8,128)(2,1)S(1)}, bf16[2,3,2,8,1024]{4,3,2,1,0:T(8,128)(2,1)S(1)}, u32[]{:S(2)}, u32[]{:S(2)}) collective-permute-start(bf16[2,3,2,8,1024]{4,3,2,1,0:T(8,128)(2,1)S(1)} %pad_maximum_fusion.10), channel_id=1, source_target_pairs={{0,6},{1,3},{2,4},{3,1},{4,2},{5,7},{6,0},{7,5},{8,14},{9,11},{10,... | collective-permute-start | bytes 589832 | tf_op jit(solution)/shard_map/ppermute | solution.py:46
  9.8 4.1 %collective-permute-start.11 = (bf16[2,3,2,8,1024]{4,3,2,1,0:T(8,128)(2,1)S(1)}, bf16[2,3,2,8,1024]{4,3,2,1,0:T(8,128)(2,1)S(1)}, u32[]{:S(2)}, u32[]{:S(2)}) collective-permute-start(bf16[2,3,2,8,1024]{4,3,2,1,0:T(8,128)(2,1)S(1)} %pad_maximum_fusion.11), channel_id=1, source_target_pairs={{0,96},{1,33},{2,98},{3,35},{4,100},{5,37},{6,102},{7,39},{8,104},... | collective-permute-start | bytes 589832 | tf_op jit(solution)/shard_map/ppermute | solution.py:46
  13.9 2.9 %collective-permute-start.18 = (bf16[2,3,2,8,1024]{4,3,2,1,0:T(8,128)(2,1)S(1)}, bf16[2,3,2,8,1024]{4,3,2,1,0:T(8,128)(2,1)S(1)}, u32[]{:S(2)}, u32[]{:S(2)}) collective-permute-start(bf16[2,3,2,8,1024]{4,3,2,1,0:T(8,128)(2,1)S(1)} %pad_maximum_fusion.12), channel_id=1, source_target_pairs={{0,24},{1,9},{2,26},{3,11},{4,28},{5,13},{6,30},{7,15},{8,16},{9,1... | collective-permute-start | bytes 589832 | tf_op jit(solution)/shard_map/ppermute | solution.py:46
  23.2 1.7 %collective-permute-start.5 = (bf16[512,1024]{1,0:T(8,128)(2,1)}, bf16[512,1024]{1,0:T(8,128)(2,1)}, u32[]{:S(2)}, u32[]{:S(2)}) collective-permute-start(bf16[512,1024]{1,0:T(8,128)(2,1)} %constant_dynamic-slice_fusion), channel_id=1, source_target_pairs={{0,1},{1,0},{2,3},{3,2},{4,5},{5,4},{6,7},{7,6},{8,9},{9,8},{10,11... | collective-permute-start | bytes 3145736 | tf_op jit(solution)/shard_map/ppermute | solution.py:50
  27.9 2.2 %collective-permute-start.3 = (bf16[2,3,8,8,1024]{4,3,2,1,0:T(8,128)(2,1)}, bf16[2,3,8,8,1024]{4,3,2,1,0:T(8,128)(2,1)}, u32[]{:S(2)}, u32[]{:S(2)}) collective-permute-start(bf16[2,3,8,8,1024]{4,3,2,1,0:T(8,128)(2,1)} %pad_maximum_fusion), channel_id=1, source_target_pairs={{0,24},{1,9},{2,26},{3,11},{4,28},{5,13},{6,30},{7,15},{8,16},{9,1... | collective-permute-start | bytes 2359304 | tf_op jit(solution)/shard_map/ppermute | solution.py:46
  31.1 1.4 collective-permute-start.13
  35.3 3.0 %collective-permute-start.20 = (bf16[2,3,8,8,1024]{4,3,2,1,0:T(8,128)(2,1)}, bf16[2,3,8,8,1024]{4,3,2,1,0:T(8,128)(2,1)}, u32[]{:S(2)}, u32[]{:S(2)}) collective-permute-start(bf16[2,3,8,8,1024]{4,3,2,1,0:T(8,128)(2,1)} %pad_maximum_fusion.4), channel_id=1, source_target_pairs={{0,96},{1,33},{2,98},{3,35},{4,100},{5,37},{6,102},{7,39},{8,104},... | collective-permute-start | bytes 2359304 | tf_op jit(solution)/shard_map/ppermute | solution.py:46
  39.5 2.0 %collective-permute-done.3.rest = bf16[2,3,8,8,1024]{4,3,2,1,0:T(8,128)(2,1)} collective-permute-done((bf16[2,3,8,8,1024]{4,3,2,1,0:T(8,128)(2,1)}, bf16[2,3,8,8,1024]{4,3,2,1,0:T(8,128)(2,1)}, u32[]{:S(2)}, u32[]{:S(2)}) %collective-permute-start.3) | collective-permute-done | bytes 786464 | tf_op jit(solution)/shard_map/ppermute | solution.py:46
  42.6 1.4 pick.3
  45.2 1.3 pick.4
  47.3 4.6 %collective-permute-done.20.rest = bf16[2,3,8,8,1024]{4,3,2,1,0:T(8,128)(2,1)} collective-permute-done((bf16[2,3,8,8,1024]{4,3,2,1,0:T(8,128)(2,1)}, bf16[2,3,8,8,1024]{4,3,2,1,0:T(8,128)(2,1)}, u32[]{:S(2)}, u32[]{:S(2)}) %collective-permute-start.20) | collective-permute-done | bytes 786464 | tf_op jit(solution)/shard_map/ppermute | solution.py:46
  51.9 1.3 pick.5
  53.2 2.8 %collective-permute-done.7 = bf16[2,2,3,4,8,1024]{5,4,3,2,1,0:T(8,128)(2,1)S(1)} collective-permute-done((bf16[2,2,3,4,8,1024]{5,4,3,2,1,0:T(8,128)(2,1)S(1)}, bf16[2,2,3,4,8,1024]{5,4,3,2,1,0:T(8,128)(2,1)S(1)}, u32[]{:S(2)}, u32[]{:S(2)}) %collective-permute-start.7) | collective-permute-done | bytes 786464 | tf_op jit(solution)/shard_map/ppermute | solution.py:46
  56.2 2.6 %collective-permute-start.8 = (bf16[2,2,3,4,8,1024]{5,4,3,2,1,0:T(8,128)(2,1)S(1)}, bf16[2,2,3,4,8,1024]{5,4,3,2,1,0:T(8,128)(2,1)S(1)}, u32[]{:S(2)}, u32[]{:S(2)}) collective-permute-start(bf16[2,2,3,4,8,1024]{5,4,3,2,1,0:T(8,128)(2,1)S(1)} %pad_maximum_fusion.1), channel_id=1, source_target_pairs={{0,96},{1,33},{2,98},{3,35},{4,100},{5,37},{6,102},{7,39},{8,104},... | collective-permute-start | bytes 2359304 | tf_op jit(solution)/shard_map/ppermute | solution.py:46
  58.9 2.3 %collective-permute-start.15 = (bf16[2,2,3,4,8,1024]{5,4,3,2,1,0:T(8,128)(2,1)S(1)}, bf16[2,2,3,4,8,1024]{5,4,3,2,1,0:T(8,128)(2,1)S(1)}, u32[]{:S(2)}, u32[]{:S(2)}) collective-permute-start(bf16[2,2,3,4,8,1024]{5,4,3,2,1,0:T(8,128)(2,1)S(1)} %pad_maximum_fusion.3), channel_id=1, source_target_pairs={{0,24},{1,9},{2,26},{3,11},{4,28},{5,13},{6,30},{7,15},{8,16},{9,1... | collective-permute-start | bytes 2359304 | tf_op jit(solution)/shard_map/ppermute | solution.py:46
  61.2 5.8 %collective-permute-done.21 = bf16[2,2,3,4,8,1024]{5,4,3,2,1,0:T(8,128)(2,1)S(1)} collective-permute-done((bf16[2,2,3,4,8,1024]{5,4,3,2,1,0:T(8,128)(2,1)S(1)}, bf16[2,2,3,4,8,1024]{5,4,3,2,1,0:T(8,128)(2,1)S(1)}, u32[]{:S(2)}, u32[]{:S(2)}) %collective-permute-start.21) | collective-permute-done | bytes 786464 | tf_op jit(solution)/shard_map/ppermute | solution.py:46
  67.5 2.0 %collective-permute-done.8 = bf16[2,2,3,4,8,1024]{5,4,3,2,1,0:T(8,128)(2,1)S(1)} collective-permute-done((bf16[2,2,3,4,8,1024]{5,4,3,2,1,0:T(8,128)(2,1)S(1)}, bf16[2,2,3,4,8,1024]{5,4,3,2,1,0:T(8,128)(2,1)S(1)}, u32[]{:S(2)}, u32[]{:S(2)}) %collective-permute-start.8) | collective-permute-done | bytes 786464 | tf_op jit(solution)/shard_map/ppermute | solution.py:46
  69.5 3.2 %first.3 = (f32[3,1024,128]{2,1,0:T(8,128)S(1)}, bf16[2,3,4,32,1024]{4,3,2,1,0:T(8,128)(2,1)S(1)}) custom-call(s32[9]{0:T(128)S(1)} %get-tuple-element.152.table_ref, bf16[512,2048]{1,0:T(8,128)(2,1)S(1)} %copy-done, bf16[512,1024]{1,0:T(8,128)(2,1)S(1)} %collective-permute-done.4.tok1, bf16[512,2048]{1,0:T(8,128)(2,1)S(1)} %copy-done.2, ...), custom_call_target="tpu_custom_call" | custom-call | tf_op jit(solution)/shard_map/first/pallas_call | solution.py:198
  72.9 3.2 %first.4 = (f32[3,1024,128]{2,1,0:T(8,128)S(1)}, bf16[2,3,4,32,1024]{4,3,2,1,0:T(8,128)(2,1)S(1)}) custom-call(s32[9]{0:T(128)S(1)} %get-tuple-element.151.table_ref, bf16[512,2048]{1,0:T(8,128)(2,1)S(1)} %copy-done, bf16[512,1024]{1,0:T(8,128)(2,1)S(1)} %collective-permute-done.4.tok1, bf16[512,2048]{1,0:T(8,128)(2,1)S(1)} %copy-done.2, ...), custom_call_target="tpu_custom_call" | custom-call | tf_op jit(solution)/shard_map/first/pallas_call | solution.py:198
  76.6 3.7 %collective-permute-done.22 = bf16[2,2,3,4,8,1024]{5,4,3,2,1,0:T(8,128)(2,1)S(1)} collective-permute-done((bf16[2,2,3,4,8,1024]{5,4,3,2,1,0:T(8,128)(2,1)S(1)}, bf16[2,2,3,4,8,1024]{5,4,3,2,1,0:T(8,128)(2,1)S(1)}, u32[]{:S(2)}, u32[]{:S(2)}) %collective-permute-start.22) | collective-permute-done | bytes 786464 | tf_op jit(solution)/shard_map/ppermute | solution.py:46
  80.4 3.2 %first.5 = (f32[3,1024,128]{2,1,0:T(8,128)S(1)}, bf16[2,3,4,32,1024]{4,3,2,1,0:T(8,128)(2,1)S(1)}) custom-call(s32[9]{0:T(128)S(1)} %get-tuple-element.150.table_ref, bf16[512,2048]{1,0:T(8,128)(2,1)S(1)} %copy-done, bf16[512,1024]{1,0:T(8,128)(2,1)S(1)} %collective-permute-done.4.tok1, bf16[512,2048]{1,0:T(8,128)(2,1)S(1)} %copy-done.2, ...), custom_call_target="tpu_custom_call" | custom-call | tf_op jit(solution)/shard_map/first/pallas_call | solution.py:198
  83.6 3.5 %second.3 = (bf16[2,3,32,1024]{3,2,1,0:T(8,128)(2,1)S(1)}, bf16[2,2,3,32,1024]{4,3,2,1,0:T(8,128)(2,1)S(1)}, bf16[2,3,32,1024]{3,2,1,0:T(8,128)(2,1)S(1)}, bf16[...) custom-call(s32[9]{0:T(128)S(1)} %get-tuple-element.152.table_ref, bf16[512,2048]{1,0:T(8,128)(2,1)S(1)} %copy-done, ...), custom_call_target="tpu_custom_call" | custom-call | tf_op jit(solution)/shard_map/second/pallas_call | solution.py:263
  87.2 3.5 %second.4 = (bf16[2,3,32,1024]{3,2,1,0:T(8,128)(2,1)S(1)}, bf16[2,2,3,32,1024]{4,3,2,1,0:T(8,128)(2,1)S(1)}, bf16[2,3,32,1024]{3,2,1,0:T(8,128)(2,1)S(1)}, bf16[...) custom-call(s32[9]{0:T(128)S(1)} %get-tuple-element.151.table_ref, bf16[512,2048]{1,0:T(8,128)(2,1)S(1)} %copy-done, ...), custom_call_target="tpu_custom_call" | custom-call | tf_op jit(solution)/shard_map/second/pallas_call | solution.py:263
  90.8 3.5 %second.5 = (bf16[2,3,32,1024]{3,2,1,0:T(8,128)(2,1)S(1)}, bf16[2,2,3,32,1024]{4,3,2,1,0:T(8,128)(2,1)S(1)}, bf16[2,3,32,1024]{3,2,1,0:T(8,128)(2,1)S(1)}, bf16[...) custom-call(s32[9]{0:T(128)S(1)} %get-tuple-element.150.table_ref, bf16[512,2048]{1,0:T(8,128)(2,1)S(1)} %copy-done, ...), custom_call_target="tpu_custom_call" | custom-call | tf_op jit(solution)/shard_map/second/pallas_call | solution.py:263
  94.4 4.8 %collective-permute-done.28 = bf16[2,2,3,32,1024]{4,3,2,1,0:T(8,128)(2,1)S(1)} collective-permute-done((bf16[2,2,3,32,1024]{4,3,2,1,0:T(8,128)(2,1)S(1)}, bf16[2,2,3,32,1024]{4,3,2,1,0:T(8,128)(2,1)S(1)}, u32[]{:S(2)}, u32[]{:S(2)}) %collective-permute-start.28) | collective-permute-done | bytes 786464 | tf_op jit(solution)/shard_map/ppermute | solution.py:46
  99.3 4.2 %collective-permute-start.29 = (bf16[2,2,3,32,1024]{4,3,2,1,0:T(8,128)(2,1)S(1)}, bf16[2,2,3,32,1024]{4,3,2,1,0:T(8,128)(2,1)S(1)}, u32[]{:S(2)}, u32[]{:S(2)}) collective-permute-start(bf16[2,2,3,32,1024]{4,3,2,1,0:T(8,128)(2,1)S(1)} %pad_maximum_fusion.7), channel_id=1, source_target_pairs={{0,96},{1,33},{2,98},{3,35},{4,100},{5,37},{6,102},{7,39},{8,104},... | collective-permute-start | bytes 2359304 | tf_op jit(solution)/shard_map/ppermute | solution.py:46
  103.7 2.3 %collective-permute-start.25 = (bf16[2,2,3,32,1024]{4,3,2,1,0:T(8,128)(2,1)S(1)}, bf16[2,2,3,32,1024]{4,3,2,1,0:T(8,128)(2,1)S(1)}, u32[]{:S(2)}, u32[]{:S(2)}) collective-permute-start(bf16[2,2,3,32,1024]{4,3,2,1,0:T(8,128)(2,1)S(1)} %pad_maximum_fusion.6), channel_id=1, source_target_pairs={{0,24},{1,9},{2,26},{3,11},{4,28},{5,13},{6,30},{7,15},{8,16},{9,1... | collective-permute-start | bytes 2359304 | tf_op jit(solution)/shard_map/ppermute | solution.py:46
  106.5 2.3 %collective-permute-start.39 = (bf16[2,2,3,32,1024]{4,3,2,1,0:T(8,128)(2,1)S(1)}, bf16[2,2,3,32,1024]{4,3,2,1,0:T(8,128)(2,1)S(1)}, u32[]{:S(2)}, u32[]{:S(2)}) collective-permute-start(bf16[2,2,3,32,1024]{4,3,2,1,0:T(8,128)(2,1)S(1)} %pad_maximum_fusion.8), channel_id=1, source_target_pairs={{0,6},{1,3},{2,4},{3,1},{4,2},{5,7},{6,0},{7,5},{8,14},{9,11},{10,... | collective-permute-start | bytes 2359304 | tf_op jit(solution)/shard_map/ppermute | solution.py:46
  108.7 4.8 %collective-permute-done.29 = bf16[2,2,3,32,1024]{4,3,2,1,0:T(8,128)(2,1)S(1)} collective-permute-done((bf16[2,2,3,32,1024]{4,3,2,1,0:T(8,128)(2,1)S(1)}, bf16[2,2,3,32,1024]{4,3,2,1,0:T(8,128)(2,1)S(1)}, u32[]{:S(2)}, u32[]{:S(2)}) %collective-permute-start.29) | collective-permute-done | bytes 786464 | tf_op jit(solution)/shard_map/ppermute | solution.py:46
  114.7 2.3 %collective-permute-start.30 = (bf16[2,3,8,8,1024]{4,3,2,1,0:T(8,128)(2,1)S(1)}, bf16[2,3,8,8,1024]{4,3,2,1,0:T(8,128)(2,1)S(1)}, u32[]{:S(2)}, u32[]{:S(2)}) collective-permute-start(bf16[2,3,8,8,1024]{4,3,2,1,0:T(8,128)(2,1)S(1)} %get-tuple-element.124), channel_id=1, source_target_pairs={{0,24},{1,9},{2,26},{3,11},{4,28},{5,13},{6,30},{7,15},{8,16},{9,1... | collective-permute-start | bytes 2359304 | tf_op jit(solution)/shard_map/ppermute | solution.py:46
  117.1 3.1 %rows_out.2 = (bf16[512,1024]{1,0:T(8,128)(2,1)S(1)}, bf16[512,1024]{1,0:T(8,128)(2,1)S(1)}) custom-call(s32[9]{0:T(128)S(1)} %get-tuple-element.152.table_ref, bf16[1024,256]{1,0:T(8,128)(2,1)S(1)} %get-tuple-element.92.refs_0_, bf16[1024,256]{1,0:T(8,128)(2,1)S(1)} %get-tuple-element.98.refs_1_, bf16[1024,256]{1,0:T(8,128)(2,1)S(1)} %get-tuple-element.104.refs_2_, ...), custom_call_target="tpu_custom_call" | custom-call | tf_op jit(solution)/shard_map/rows_out/pallas_call | solution.py:321
  123.7 3.3 %collective-permute-start.40 = (bf16[2,3,8,8,1024]{4,3,2,1,0:T(8,128)(2,1)S(1)}, bf16[2,3,8,8,1024]{4,3,2,1,0:T(8,128)(2,1)S(1)}, u32[]{:S(2)}, u32[]{:S(2)}) collective-permute-start(bf16[2,3,8,8,1024]{4,3,2,1,0:T(8,128)(2,1)S(1)} %get-tuple-element.142), channel_id=1, source_target_pairs={{0,96},{1,33},{2,98},{3,35},{4,100},{5,37},{6,102},{7,39},{8,104},... | collective-permute-start | bytes 2359304 | tf_op jit(solution)/shard_map/ppermute | solution.py:46
  128.2 6.5 %collective-permute-done.34.came = bf16[2,3,8,8,1024]{4,3,2,1,0:T(8,128)(2,1)S(1)} collective-permute-done((bf16[2,3,8,8,1024]{4,3,2,1,0:T(8,128)(2,1)S(1)}, bf16[2,3,8,8,1024]{4,3,2,1,0:T(8,128)(2,1)S(1)}, u32[]{:S(2)}, u32[]{:S(2)}) %collective-permute-start.34) | collective-permute-done | bytes 786464 | tf_op jit(solution)/shard_map/ppermute | solution.py:46
  134.9 2.1 %collective-permute-done.40.came = bf16[2,3,8,8,1024]{4,3,2,1,0:T(8,128)(2,1)S(1)} collective-permute-done((bf16[2,3,8,8,1024]{4,3,2,1,0:T(8,128)(2,1)S(1)}, bf16[2,3,8,8,1024]{4,3,2,1,0:T(8,128)(2,1)S(1)}, u32[]{:S(2)}, u32[]{:S(2)}) %collective-permute-start.40) | collective-permute-done | bytes 786464 | tf_op jit(solution)/shard_map/ppermute | solution.py:46
  138.1 2.3 %collective-permute-start.32 = (bf16[2,3,2,8,1024]{4,3,2,1,0:T(8,128)(2,1)S(1)}, bf16[2,3,2,8,1024]{4,3,2,1,0:T(8,128)(2,1)S(1)}, u32[]{:S(2)}, u32[]{:S(2)}) collective-permute-start(bf16[2,3,2,8,1024]{4,3,2,1,0:T(8,128)(2,1)S(1)} %get-tuple-element.127), channel_id=1, source_target_pairs={{0,6},{1,3},{2,4},{3,1},{4,2},{5,7},{6,0},{7,5},{8,14},{9,11},{10,... | collective-permute-start | bytes 589832 | tf_op jit(solution)/shard_map/ppermute | solution.py:46
  140.4 4.6 %rows_out.3 = (bf16[512,2048]{1,0:T(8,128)(2,1)}, bf16[512,2048]{1,0:T(8,128)(2,1)}) custom-call(s32[9]{0:T(128)S(1)} %get-tuple-element.152.table_ref, bf16[1024,256]{1,0:T(8,128)(2,1)S(1)} %get-tuple-element.92.refs_0_, bf16[1024,256]{1,0:T(8,128)(2,1)S(1)} %get-tuple-element.98.refs_1_, bf16[1024,256]{1,0:T(8,128)(2,1)S(1)} %get-tuple-element.104.refs_2_, ...), custom_call_target="tpu_custom_call" | custom-call | tf_op jit(solution)/shard_map/rows_out/pallas_call | solution.py:321
  145.8 3.3 %collective-permute-start.36 = (bf16[2,3,2,8,1024]{4,3,2,1,0:T(8,128)(2,1)S(1)}, bf16[2,3,2,8,1024]{4,3,2,1,0:T(8,128)(2,1)S(1)}, u32[]{:S(2)}, u32[]{:S(2)}) collective-permute-start(bf16[2,3,2,8,1024]{4,3,2,1,0:T(8,128)(2,1)S(1)} %get-tuple-element.136), channel_id=1, source_target_pairs={{0,96},{1,33},{2,98},{3,35},{4,100},{5,37},{6,102},{7,39},{8,104},... | collective-permute-start | bytes 589832 | tf_op jit(solution)/shard_map/ppermute | solution.py:46
  150.0 1.3 collective-permute-start.42
  151.5 1.3 collective-permute-done.36
  152.8 2.5 %collective-permute-start.37 = (bf16[3,2,8,1024]{3,2,1,0:T(8,128)(2,1)S(1)}, bf16[3,2,8,1024]{3,2,1,0:T(8,128)(2,1)S(1)}, u32[]{:S(2)}, u32[]{:S(2)}) collective-permute-start(bf16[3,2,8,1024]{3,2,1,0:T(8,128)(2,1)S(1)} %fusion.5), channel_id=1, source_target_pairs={{0,32},{1,97},{2,34},{3,99},{4,36},{5,101},{6,38},{7,103},{8,40},{... | collective-permute-start | bytes 294920 | tf_op jit(solution)/shard_map/ppermute | solution.py:46
  155.3 2.7 %collective-permute-done.42 = bf16[2,3,2,8,1024]{4,3,2,1,0:T(8,128)(2,1)S(1)} collective-permute-done((bf16[2,3,2,8,1024]{4,3,2,1,0:T(8,128)(2,1)S(1)}, bf16[2,3,2,8,1024]{4,3,2,1,0:T(8,128)(2,1)S(1)}, u32[]{:S(2)}, u32[]{:S(2)}) %collective-permute-start.42) | collective-permute-done | bytes 196640 | tf_op jit(solution)/shard_map/ppermute | solution.py:46
  158.1 2.2 %collective-permute-start.43 = (bf16[3,2,8,1024]{3,2,1,0:T(8,128)(2,1)S(1)}, bf16[3,2,8,1024]{3,2,1,0:T(8,128)(2,1)S(1)}, u32[]{:S(2)}, u32[]{:S(2)}) collective-permute-start(bf16[3,2,8,1024]{3,2,1,0:T(8,128)(2,1)S(1)} %fusion.3), channel_id=1, source_target_pairs={{0,8},{1,25},{2,10},{3,27},{4,12},{5,29},{6,14},{7,31},{8,0},{9,17... | collective-permute-start | bytes 294920 | tf_op jit(solution)/shard_map/ppermute | solution.py:46
  160.3 2.5 %collective-permute-done.43 = bf16[3,2,8,1024]{3,2,1,0:T(8,128)(2,1)S(1)} collective-permute-done((bf16[3,2,8,1024]{3,2,1,0:T(8,128)(2,1)S(1)}, bf16[3,2,8,1024]{3,2,1,0:T(8,128)(2,1)S(1)}, u32[]{:S(2)}, u32[]{:S(2)}) %collective-permute-start.43) | collective-permute-done | bytes 98336 | tf_op jit(solution)/shard_map/ppermute | solution.py:46
  162.9 1.5 divide_subtract_fusion
  (157 shorter events, 29.4 us)
Async XLA Ops:
  0.6 17.3 %copy-start = (bf16[512,2048]{1,0:T(8,128)(2,1)S(1)}, bf16[512,2048]{1,0:T(8,128)(2,1)}, u32[]{:S(2)}) copy-start(bf16[512,2048]{1,0:T(8,128)(2,1)} %tok0.5) | copy-start | bytes 6291460
  1.9 16.0 %copy-start.15 = (bf16[3,2,8,1024]{3,2,1,0:T(8,128)(2,1)}, bf16[3,2,8,1024]{3,2,1,0:T(8,128)(2,1)S(1)}, u32[]{:S(2)}) copy-start(bf16[3,2,8,1024]{3,2,1,0:T(8,128)(2,1)S(1)} %get-tuple-element.99.own) | copy-start | bytes 294916
  1.9 16.0 %copy-start.19 = (bf16[3,2,8,1024]{3,2,1,0:T(8,128)(2,1)}, bf16[3,2,8,1024]{3,2,1,0:T(8,128)(2,1)S(1)}, u32[]{:S(2)}) copy-start(bf16[3,2,8,1024]{3,2,1,0:T(8,128)(2,1)S(1)} %get-tuple-element.93.own) | copy-start | bytes 294916
  1.9 5.2 %collective-permute-start = (bf16[3,2,8,1024]{3,2,1,0:T(8,128)(2,1)S(1)}, bf16[3,2,8,1024]{3,2,1,0:T(8,128)(2,1)S(1)}, u32[]{:S(2)}, u32[]{:S(2)}) collective-permute-start(bf16[3,2,8,1024]{3,2,1,0:T(8,128)(2,1)S(1)} %get-tuple-element.76.own), channel_id=1, source_target_pairs={{0,2},{1,7},{2,0},{3,5},{4,6},{5,3},{6,4},{7,1},{8,10},{9,15},{10,... | collective-permute-start | bytes 294920 | tf_op jit(solution)/shard_map/ppermute | solution.py:46
  3.6 10.3 %collective-permute-start.17 = (bf16[3,2,8,1024]{3,2,1,0:T(8,128)(2,1)S(1)}, bf16[3,2,8,1024]{3,2,1,0:T(8,128)(2,1)S(1)}, u32[]{:S(2)}, u32[]{:S(2)}) collective-permute-start(bf16[3,2,8,1024]{3,2,1,0:T(8,128)(2,1)S(1)} %get-tuple-element.99.own), channel_id=1, source_target_pairs={{0,8},{1,25},{2,10},{3,27},{4,12},{5,29},{6,14},{7,31},{8,0},{9,17... | collective-permute-start | bytes 294920 | tf_op jit(solution)/shard_map/ppermute | solution.py:46
  5.1 4.6 %collective-permute-start.10 = (bf16[3,2,8,1024]{3,2,1,0:T(8,128)(2,1)S(1)}, bf16[3,2,8,1024]{3,2,1,0:T(8,128)(2,1)S(1)}, u32[]{:S(2)}, u32[]{:S(2)}) collective-permute-start(bf16[3,2,8,1024]{3,2,1,0:T(8,128)(2,1)S(1)} %get-tuple-element.93.own), channel_id=1, source_target_pairs={{0,32},{1,97},{2,34},{3,99},{4,36},{5,101},{6,38},{7,103},{8,40},{... | collective-permute-start | bytes 294920 | tf_op jit(solution)/shard_map/ppermute | solution.py:46
  7.1 9.7 %collective-permute-start.1 = (bf16[2,3,2,8,1024]{4,3,2,1,0:T(8,128)(2,1)S(1)}, bf16[2,3,2,8,1024]{4,3,2,1,0:T(8,128)(2,1)S(1)}, u32[]{:S(2)}, u32[]{:S(2)}) collective-permute-start(bf16[2,3,2,8,1024]{4,3,2,1,0:T(8,128)(2,1)S(1)} %pad_maximum_fusion.10), channel_id=1, source_target_pairs={{0,6},{1,3},{2,4},{3,1},{4,2},{5,7},{6,0},{7,5},{8,14},{9,11},{10,... | collective-permute-start | bytes 589832 | tf_op jit(solution)/shard_map/ppermute | solution.py:46
  9.8 9.2 %collective-permute-start.11 = (bf16[2,3,2,8,1024]{4,3,2,1,0:T(8,128)(2,1)S(1)}, bf16[2,3,2,8,1024]{4,3,2,1,0:T(8,128)(2,1)S(1)}, u32[]{:S(2)}, u32[]{:S(2)}) collective-permute-start(bf16[2,3,2,8,1024]{4,3,2,1,0:T(8,128)(2,1)S(1)} %pad_maximum_fusion.11), channel_id=1, source_target_pairs={{0,96},{1,33},{2,98},{3,35},{4,100},{5,37},{6,102},{7,39},{8,104},... | collective-permute-start | bytes 589832 | tf_op jit(solution)/shard_map/ppermute | solution.py:46
  13.9 11.1 %collective-permute-start.18 = (bf16[2,3,2,8,1024]{4,3,2,1,0:T(8,128)(2,1)S(1)}, bf16[2,3,2,8,1024]{4,3,2,1,0:T(8,128)(2,1)S(1)}, u32[]{:S(2)}, u32[]{:S(2)}) collective-permute-start(bf16[2,3,2,8,1024]{4,3,2,1,0:T(8,128)(2,1)S(1)} %pad_maximum_fusion.12), channel_id=1, source_target_pairs={{0,24},{1,9},{2,26},{3,11},{4,28},{5,13},{6,30},{7,15},{8,16},{9,1... | collective-permute-start | bytes 589832 | tf_op jit(solution)/shard_map/ppermute | solution.py:46
  17.7 9.2 %collective-permute-start.2 = (bf16[3,8,8,1024]{3,2,1,0:T(8,128)(2,1)S(1)}, bf16[3,8,8,1024]{3,2,1,0:T(8,128)(2,1)S(1)}, u32[]{:S(2)}, u32[]{:S(2)}) collective-permute-start(bf16[3,8,8,1024]{3,2,1,0:T(8,128)(2,1)S(1)} %weave.3.kept), channel_id=1, source_target_pairs={{0,8},{1,25},{2,10},{3,27},{4,12},{5,29},{6,14},{7,31},{8,0},{9,17... | collective-permute-start | bytes 1179656 | tf_op jit(solution)/shard_map/ppermute | solution.py:46
  19.0 20.5 %collective-permute-start.4 = (bf16[512,1024]{1,0:T(8,128)(2,1)}, bf16[512,1024]{1,0:T(8,128)(2,1)S(1)}, u32[]{:S(2)}, u32[]{:S(2)}) collective-permute-start(bf16[512,1024]{1,0:T(8,128)(2,1)} %constant_dynamic-slice_fusion.1), channel_id=1, source_target_pairs={{0,1},{1,0},{2,3},{3,2},{4,5},{5,4},{6,7},{7,6},{8,9},{9,8},{10,11... | collective-permute-start | bytes 3145736 | tf_op jit(solution)/shard_map/ppermute | solution.py:50
  21.7 8.5 %collective-permute-start.12 = (bf16[3,8,8,1024]{3,2,1,0:T(8,128)(2,1)S(1)}, bf16[3,8,8,1024]{3,2,1,0:T(8,128)(2,1)S(1)}, u32[]{:S(2)}, u32[]{:S(2)}) collective-permute-start(bf16[3,8,8,1024]{3,2,1,0:T(8,128)(2,1)S(1)} %weave.4.kept), channel_id=1, source_target_pairs={{0,2},{1,7},{2,0},{3,5},{4,6},{5,3},{6,4},{7,1},{8,10},{9,15},{10,... | collective-permute-start | bytes 1179656 | tf_op jit(solution)/shard_map/ppermute | solution.py:46
  23.2 16.2 %collective-permute-start.5 = (bf16[512,1024]{1,0:T(8,128)(2,1)}, bf16[512,1024]{1,0:T(8,128)(2,1)}, u32[]{:S(2)}, u32[]{:S(2)}) collective-permute-start(bf16[512,1024]{1,0:T(8,128)(2,1)} %constant_dynamic-slice_fusion), channel_id=1, source_target_pairs={{0,1},{1,0},{2,3},{3,2},{4,5},{5,4},{6,7},{7,6},{8,9},{9,8},{10,11... | collective-permute-start | bytes 3145736 | tf_op jit(solution)/shard_map/ppermute | solution.py:50
  25.9 7.9 %collective-permute-start.19 = (bf16[3,8,8,1024]{3,2,1,0:T(8,128)(2,1)S(1)}, bf16[3,8,8,1024]{3,2,1,0:T(8,128)(2,1)S(1)}, u32[]{:S(2)}, u32[]{:S(2)}) collective-permute-start(bf16[3,8,8,1024]{3,2,1,0:T(8,128)(2,1)S(1)} %weave.5.kept), channel_id=1, source_target_pairs={{0,32},{1,97},{2,34},{3,99},{4,36},{5,101},{6,38},{7,103},{8,40},{... | collective-permute-start | bytes 1179656 | tf_op jit(solution)/shard_map/ppermute | solution.py:46
  27.9 13.5 %collective-permute-start.3 = (bf16[2,3,8,8,1024]{4,3,2,1,0:T(8,128)(2,1)}, bf16[2,3,8,8,1024]{4,3,2,1,0:T(8,128)(2,1)}, u32[]{:S(2)}, u32[]{:S(2)}) collective-permute-start(bf16[2,3,8,8,1024]{4,3,2,1,0:T(8,128)(2,1)} %pad_maximum_fusion), channel_id=1, source_target_pairs={{0,24},{1,9},{2,26},{3,11},{4,28},{5,13},{6,30},{7,15},{8,16},{9,1... | collective-permute-start | bytes 2359304 | tf_op jit(solution)/shard_map/ppermute | solution.py:46
  31.1 14.0 %collective-permute-start.13 = (bf16[2,3,8,8,1024]{4,3,2,1,0:T(8,128)(2,1)}, bf16[2,3,8,8,1024]{4,3,2,1,0:T(8,128)(2,1)}, u32[]{:S(2)}, u32[]{:S(2)}) collective-permute-start(bf16[2,3,8,8,1024]{4,3,2,1,0:T(8,128)(2,1)} %pad_maximum_fusion.2), channel_id=1, source_target_pairs={{0,6},{1,3},{2,4},{3,1},{4,2},{5,7},{6,0},{7,5},{8,14},{9,11},{10,... | collective-permute-start | bytes 2359304 | tf_op jit(solution)/shard_map/ppermute | solution.py:46
  33.7 1.6 collective-permute-start.6
  35.3 16.6 %collective-permute-start.20 = (bf16[2,3,8,8,1024]{4,3,2,1,0:T(8,128)(2,1)}, bf16[2,3,8,8,1024]{4,3,2,1,0:T(8,128)(2,1)}, u32[]{:S(2)}, u32[]{:S(2)}) collective-permute-start(bf16[2,3,8,8,1024]{4,3,2,1,0:T(8,128)(2,1)} %pad_maximum_fusion.4), channel_id=1, source_target_pairs={{0,96},{1,33},{2,98},{3,35},{4,100},{5,37},{6,102},{7,39},{8,104},... | collective-permute-start | bytes 2359304 | tf_op jit(solution)/shard_map/ppermute | solution.py:46
  44.0 12.1 %collective-permute-start.7 = (bf16[2,2,3,4,8,1024]{5,4,3,2,1,0:T(8,128)(2,1)S(1)}, bf16[2,2,3,4,8,1024]{5,4,3,2,1,0:T(8,128)(2,1)S(1)}, u32[]{:S(2)}, u32[]{:S(2)}) collective-permute-start(bf16[2,2,3,4,8,1024]{5,4,3,2,1,0:T(8,128)(2,1)S(1)} %get-tuple-element.89), channel_id=1, source_target_pairs={{0,32},{1,97},{2,34},{3,99},{4,36},{5,101},{6,38},{7,103},{8,40},{... | collective-permute-start | bytes 2359304 | tf_op jit(solution)/shard_map/ppermute | solution.py:46
  46.4 12.4 %collective-permute-start.14 = (bf16[2,2,3,4,8,1024]{5,4,3,2,1,0:T(8,128)(2,1)S(1)}, bf16[2,2,3,4,8,1024]{5,4,3,2,1,0:T(8,128)(2,1)S(1)}, u32[]{:S(2)}, u32[]{:S(2)}) collective-permute-start(bf16[2,2,3,4,8,1024]{5,4,3,2,1,0:T(8,128)(2,1)S(1)} %get-tuple-element.95), channel_id=1, source_target_pairs={{0,8},{1,25},{2,10},{3,27},{4,12},{5,29},{6,14},{7,31},{8,0},{9,17... | collective-permute-start | bytes 2359304 | tf_op jit(solution)/shard_map/ppermute | solution.py:46
  53.1 13.8 %collective-permute-start.21 = (bf16[2,2,3,4,8,1024]{5,4,3,2,1,0:T(8,128)(2,1)S(1)}, bf16[2,2,3,4,8,1024]{5,4,3,2,1,0:T(8,128)(2,1)S(1)}, u32[]{:S(2)}, u32[]{:S(2)}) collective-permute-start(bf16[2,2,3,4,8,1024]{5,4,3,2,1,0:T(8,128)(2,1)S(1)} %get-tuple-element.101), channel_id=1, source_target_pairs={{0,2},{1,7},{2,0},{3,5},{4,6},{5,3},{6,4},{7,1},{8,10},{9,15},{10,... | collective-permute-start | bytes 2359304 | tf_op jit(solution)/shard_map/ppermute | solution.py:46
  56.2 13.3 %collective-permute-start.8 = (bf16[2,2,3,4,8,1024]{5,4,3,2,1,0:T(8,128)(2,1)S(1)}, bf16[2,2,3,4,8,1024]{5,4,3,2,1,0:T(8,128)(2,1)S(1)}, u32[]{:S(2)}, u32[]{:S(2)}) collective-permute-start(bf16[2,2,3,4,8,1024]{5,4,3,2,1,0:T(8,128)(2,1)S(1)} %pad_maximum_fusion.1), channel_id=1, source_target_pairs={{0,96},{1,33},{2,98},{3,35},{4,100},{5,37},{6,102},{7,39},{8,104},... | collective-permute-start | bytes 2359304 | tf_op jit(solution)/shard_map/ppermute | solution.py:46
  58.9 14.0 %collective-permute-start.15 = (bf16[2,2,3,4,8,1024]{5,4,3,2,1,0:T(8,128)(2,1)S(1)}, bf16[2,2,3,4,8,1024]{5,4,3,2,1,0:T(8,128)(2,1)S(1)}, u32[]{:S(2)}, u32[]{:S(2)}) collective-permute-start(bf16[2,2,3,4,8,1024]{5,4,3,2,1,0:T(8,128)(2,1)S(1)} %pad_maximum_fusion.3), channel_id=1, source_target_pairs={{0,24},{1,9},{2,26},{3,11},{4,28},{5,13},{6,30},{7,15},{8,16},{9,1... | collective-permute-start | bytes 2359304 | tf_op jit(solution)/shard_map/ppermute | solution.py:46
  67.1 13.3 %collective-permute-start.22 = (bf16[2,2,3,4,8,1024]{5,4,3,2,1,0:T(8,128)(2,1)S(1)}, bf16[2,2,3,4,8,1024]{5,4,3,2,1,0:T(8,128)(2,1)S(1)}, u32[]{:S(2)}, u32[]{:S(2)}) collective-permute-start(bf16[2,2,3,4,8,1024]{5,4,3,2,1,0:T(8,128)(2,1)S(1)} %pad_maximum_fusion.5), channel_id=1, source_target_pairs={{0,6},{1,3},{2,4},{3,1},{4,2},{5,7},{6,0},{7,5},{8,14},{9,11},{10,... | collective-permute-start | bytes 2359304 | tf_op jit(solution)/shard_map/ppermute | solution.py:46
  72.6 11.0 %collective-permute-start.9 = (f32[3,1024,128]{2,1,0:T(8,128)S(1)}, f32[3,1024,128]{2,1,0:T(8,128)S(1)}, u32[]{:S(2)}, u32[]{:S(2)}) collective-permute-start(f32[3,1024,128]{2,1,0:T(8,128)S(1)} %get-tuple-element.91.sums), channel_id=1, source_target_pairs={{0,1},{1,0},{2,3},{3,2},{4,5},{5,4},{6,7},{7,6},{8,9},{9,8},{10,11... | collective-permute-start | bytes 4718600 | tf_op jit(solution)/shard_map/ppermute | solution.py:50
  76.1 11.1 %collective-permute-start.16 = (f32[3,1024,128]{2,1,0:T(8,128)S(1)}, f32[3,1024,128]{2,1,0:T(8,128)S(1)}, u32[]{:S(2)}, u32[]{:S(2)}) collective-permute-start(f32[3,1024,128]{2,1,0:T(8,128)S(1)} %get-tuple-element.97.sums), channel_id=1, source_target_pairs={{0,1},{1,0},{2,3},{3,2},{4,5},{5,4},{6,7},{7,6},{8,9},{9,8},{10,11... | collective-permute-start | bytes 4718600 | tf_op jit(solution)/shard_map/ppermute | solution.py:50
  83.5 7.3 %collective-permute-start.23 = (f32[3,1024,128]{2,1,0:T(8,128)S(1)}, f32[3,1024,128]{2,1,0:T(8,128)S(1)}, u32[]{:S(2)}, u32[]{:S(2)}) collective-permute-start(f32[3,1024,128]{2,1,0:T(8,128)S(1)} %get-tuple-element.103.sums), channel_id=1, source_target_pairs={{0,1},{1,0},{2,3},{3,2},{4,5},{5,4},{6,7},{7,6},{8,9},{9,8},{10,11... | collective-permute-start | bytes 4718600 | tf_op jit(solution)/shard_map/ppermute | solution.py:50
  87.1 12.1 %collective-permute-start.28 = (bf16[2,2,3,32,1024]{4,3,2,1,0:T(8,128)(2,1)S(1)}, bf16[2,2,3,32,1024]{4,3,2,1,0:T(8,128)(2,1)S(1)}, u32[]{:S(2)}, u32[]{:S(2)}) collective-permute-start(bf16[2,2,3,32,1024]{4,3,2,1,0:T(8,128)(2,1)S(1)} %get-tuple-element.121), channel_id=1, source_target_pairs={{0,32},{1,97},{2,34},{3,99},{4,36},{5,101},{6,38},{7,103},{8,40},{... | collective-permute-start | bytes 2359304 | tf_op jit(solution)/shard_map/ppermute | solution.py:46
  90.7 12.9 %collective-permute-start.24 = (bf16[2,2,3,32,1024]{4,3,2,1,0:T(8,128)(2,1)S(1)}, bf16[2,2,3,32,1024]{4,3,2,1,0:T(8,128)(2,1)S(1)}, u32[]{:S(2)}, u32[]{:S(2)}) collective-permute-start(bf16[2,2,3,32,1024]{4,3,2,1,0:T(8,128)(2,1)S(1)} %get-tuple-element.112), channel_id=1, source_target_pairs={{0,8},{1,25},{2,10},{3,27},{4,12},{5,29},{6,14},{7,31},{8,0},{9,17... | collective-permute-start | bytes 2359304 | tf_op jit(solution)/shard_map/ppermute | solution.py:46
  94.3 12.1 %collective-permute-start.38 = (bf16[2,2,3,32,1024]{4,3,2,1,0:T(8,128)(2,1)S(1)}, bf16[2,2,3,32,1024]{4,3,2,1,0:T(8,128)(2,1)S(1)}, u32[]{:S(2)}, u32[]{:S(2)}) collective-permute-start(bf16[2,2,3,32,1024]{4,3,2,1,0:T(8,128)(2,1)S(1)} %get-tuple-element.139), channel_id=1, source_target_pairs={{0,2},{1,7},{2,0},{3,5},{4,6},{5,3},{6,4},{7,1},{8,10},{9,15},{10,... | collective-permute-start | bytes 2359304 | tf_op jit(solution)/shard_map/ppermute | solution.py:46
  99.3 14.2 %collective-permute-start.29 = (bf16[2,2,3,32,1024]{4,3,2,1,0:T(8,128)(2,1)S(1)}, bf16[2,2,3,32,1024]{4,3,2,1,0:T(8,128)(2,1)S(1)}, u32[]{:S(2)}, u32[]{:S(2)}) collective-permute-start(bf16[2,2,3,32,1024]{4,3,2,1,0:T(8,128)(2,1)S(1)} %pad_maximum_fusion.7), channel_id=1, source_target_pairs={{0,96},{1,33},{2,98},{3,35},{4,100},{5,37},{6,102},{7,39},{8,104},... | collective-permute-start | bytes 2359304 | tf_op jit(solution)/shard_map/ppermute | solution.py:46
  103.7 16.5 %collective-permute-start.25 = (bf16[2,2,3,32,1024]{4,3,2,1,0:T(8,128)(2,1)S(1)}, bf16[2,2,3,32,1024]{4,3,2,1,0:T(8,128)(2,1)S(1)}, u32[]{:S(2)}, u32[]{:S(2)}) collective-permute-start(bf16[2,2,3,32,1024]{4,3,2,1,0:T(8,128)(2,1)S(1)} %pad_maximum_fusion.6), channel_id=1, source_target_pairs={{0,24},{1,9},{2,26},{3,11},{4,28},{5,13},{6,30},{7,15},{8,16},{9,1... | collective-permute-start | bytes 2359304 | tf_op jit(solution)/shard_map/ppermute | solution.py:46
  106.5 16.0 %collective-permute-start.39 = (bf16[2,2,3,32,1024]{4,3,2,1,0:T(8,128)(2,1)S(1)}, bf16[2,2,3,32,1024]{4,3,2,1,0:T(8,128)(2,1)S(1)}, u32[]{:S(2)}, u32[]{:S(2)}) collective-permute-start(bf16[2,2,3,32,1024]{4,3,2,1,0:T(8,128)(2,1)S(1)} %pad_maximum_fusion.8), channel_id=1, source_target_pairs={{0,6},{1,3},{2,4},{3,1},{4,2},{5,7},{6,0},{7,5},{8,14},{9,11},{10,... | collective-permute-start | bytes 2359304 | tf_op jit(solution)/shard_map/ppermute | solution.py:46
  114.7 13.3 %collective-permute-start.30 = (bf16[2,3,8,8,1024]{4,3,2,1,0:T(8,128)(2,1)S(1)}, bf16[2,3,8,8,1024]{4,3,2,1,0:T(8,128)(2,1)S(1)}, u32[]{:S(2)}, u32[]{:S(2)}) collective-permute-start(bf16[2,3,8,8,1024]{4,3,2,1,0:T(8,128)(2,1)S(1)} %get-tuple-element.124), channel_id=1, source_target_pairs={{0,24},{1,9},{2,26},{3,11},{4,28},{5,13},{6,30},{7,15},{8,16},{9,1... | collective-permute-start | bytes 2359304 | tf_op jit(solution)/shard_map/ppermute | solution.py:46
  121.4 13.3 %collective-permute-start.34 = (bf16[2,3,8,8,1024]{4,3,2,1,0:T(8,128)(2,1)S(1)}, bf16[2,3,8,8,1024]{4,3,2,1,0:T(8,128)(2,1)S(1)}, u32[]{:S(2)}, u32[]{:S(2)}) collective-permute-start(bf16[2,3,8,8,1024]{4,3,2,1,0:T(8,128)(2,1)S(1)} %get-tuple-element.133), channel_id=1, source_target_pairs={{0,6},{1,3},{2,4},{3,1},{4,2},{5,7},{6,0},{7,5},{8,14},{9,11},{10,... | collective-permute-start | bytes 2359304 | tf_op jit(solution)/shard_map/ppermute | solution.py:46
  123.7 13.3 %collective-permute-start.40 = (bf16[2,3,8,8,1024]{4,3,2,1,0:T(8,128)(2,1)S(1)}, bf16[2,3,8,8,1024]{4,3,2,1,0:T(8,128)(2,1)S(1)}, u32[]{:S(2)}, u32[]{:S(2)}) collective-permute-start(bf16[2,3,8,8,1024]{4,3,2,1,0:T(8,128)(2,1)S(1)} %get-tuple-element.142), channel_id=1, source_target_pairs={{0,96},{1,33},{2,98},{3,35},{4,100},{5,37},{6,102},{7,39},{8,104},... | collective-permute-start | bytes 2359304 | tf_op jit(solution)/shard_map/ppermute | solution.py:46
  127.0 13.4 %collective-permute-start.26 = (bf16[512,1024]{1,0:T(8,128)(2,1)S(1)}, bf16[512,1024]{1,0:T(8,128)(2,1)S(1)}, u32[]{:S(2)}, u32[]{:S(2)}) collective-permute-start(bf16[512,1024]{1,0:T(8,128)(2,1)S(1)} %get-tuple-element.116), channel_id=1, source_target_pairs={{0,1},{1,0},{2,3},{3,2},{4,5},{5,4},{6,7},{7,6},{8,9},{9,8},{10,11... | collective-permute-start | bytes 3145736 | tf_op jit(solution)/shard_map/ppermute | solution.py:50
  127.2 13.1 %collective-permute-start.27 = (bf16[512,1024]{1,0:T(8,128)(2,1)S(1)}, bf16[512,1024]{1,0:T(8,128)(2,1)S(1)}, u32[]{:S(2)}, u32[]{:S(2)}) collective-permute-start(bf16[512,1024]{1,0:T(8,128)(2,1)S(1)} %get-tuple-element.117), channel_id=1, source_target_pairs={{0,1},{1,0},{2,3},{3,2},{4,5},{5,4},{6,7},{7,6},{8,9},{9,8},{10,11... | collective-permute-start | bytes 3145736 | tf_op jit(solution)/shard_map/ppermute | solution.py:50
  128.1 9.1 %collective-permute-start.31 = (bf16[3,8,8,1024]{3,2,1,0:T(8,128)(2,1)S(1)}, bf16[3,8,8,1024]{3,2,1,0:T(8,128)(2,1)S(1)}, u32[]{:S(2)}, u32[]{:S(2)}) collective-permute-start(bf16[3,8,8,1024]{3,2,1,0:T(8,128)(2,1)S(1)} %fusion.2), channel_id=1, source_target_pairs={{0,8},{1,25},{2,10},{3,27},{4,12},{5,29},{6,14},{7,31},{8,0},{9,17... | collective-permute-start | bytes 1179656 | tf_op jit(solution)/shard_map/ppermute | solution.py:46
  134.8 10.1 %collective-permute-start.35 = (bf16[3,8,8,1024]{3,2,1,0:T(8,128)(2,1)S(1)}, bf16[3,8,8,1024]{3,2,1,0:T(8,128)(2,1)S(1)}, u32[]{:S(2)}, u32[]{:S(2)}) collective-permute-start(bf16[3,8,8,1024]{3,2,1,0:T(8,128)(2,1)S(1)} %fusion.1), channel_id=1, source_target_pairs={{0,2},{1,7},{2,0},{3,5},{4,6},{5,3},{6,4},{7,1},{8,10},{9,15},{10,... | collective-permute-start | bytes 1179656 | tf_op jit(solution)/shard_map/ppermute | solution.py:46
  137.1 12.0 %collective-permute-start.41 = (bf16[3,8,8,1024]{3,2,1,0:T(8,128)(2,1)S(1)}, bf16[3,8,8,1024]{3,2,1,0:T(8,128)(2,1)S(1)}, u32[]{:S(2)}, u32[]{:S(2)}) collective-permute-start(bf16[3,8,8,1024]{3,2,1,0:T(8,128)(2,1)S(1)} %fusion), channel_id=1, source_target_pairs={{0,32},{1,97},{2,34},{3,99},{4,36},{5,101},{6,38},{7,103},{8,40},{... | collective-permute-start | bytes 1179656 | tf_op jit(solution)/shard_map/ppermute | solution.py:46
  138.1 13.3 %collective-permute-start.32 = (bf16[2,3,2,8,1024]{4,3,2,1,0:T(8,128)(2,1)S(1)}, bf16[2,3,2,8,1024]{4,3,2,1,0:T(8,128)(2,1)S(1)}, u32[]{:S(2)}, u32[]{:S(2)}) collective-permute-start(bf16[2,3,2,8,1024]{4,3,2,1,0:T(8,128)(2,1)S(1)} %get-tuple-element.127), channel_id=1, source_target_pairs={{0,6},{1,3},{2,4},{3,1},{4,2},{5,7},{6,0},{7,5},{8,14},{9,11},{10,... | collective-permute-start | bytes 589832 | tf_op jit(solution)/shard_map/ppermute | solution.py:46
  145.8 7.0 %collective-permute-start.36 = (bf16[2,3,2,8,1024]{4,3,2,1,0:T(8,128)(2,1)S(1)}, bf16[2,3,2,8,1024]{4,3,2,1,0:T(8,128)(2,1)S(1)}, u32[]{:S(2)}, u32[]{:S(2)}) collective-permute-start(bf16[2,3,2,8,1024]{4,3,2,1,0:T(8,128)(2,1)S(1)} %get-tuple-element.136), channel_id=1, source_target_pairs={{0,96},{1,33},{2,98},{3,35},{4,100},{5,37},{6,102},{7,39},{8,104},... | collective-permute-start | bytes 589832 | tf_op jit(solution)/shard_map/ppermute | solution.py:46
  150.0 12.9 %copy-start.8 = (f32[8,3,6,1024]{3,0,2,1:T(8,128)S(1)}, f32[8,3,6,1024]{3,0,2,1:T(8,128)}, u32[]{:S(2)}) copy-start(f32[8,3,6,1024]{3,0,2,1:T(8,128)} %param.13) | copy-start | bytes 1769476
  150.0 8.0 %collective-permute-start.42 = (bf16[2,3,2,8,1024]{4,3,2,1,0:T(8,128)(2,1)S(1)}, bf16[2,3,2,8,1024]{4,3,2,1,0:T(8,128)(2,1)S(1)}, u32[]{:S(2)}, u32[]{:S(2)}) collective-permute-start(bf16[2,3,2,8,1024]{4,3,2,1,0:T(8,128)(2,1)S(1)} %get-tuple-element.145), channel_id=1, source_target_pairs={{0,24},{1,9},{2,26},{3,11},{4,28},{5,13},{6,30},{7,15},{8,16},{9,1... | collective-permute-start | bytes 589832 | tf_op jit(solution)/shard_map/ppermute | solution.py:46
  151.4 8.9 %collective-permute-start.33 = (bf16[3,2,8,1024]{3,2,1,0:T(8,128)(2,1)S(1)}, bf16[3,2,8,1024]{3,2,1,0:T(8,128)(2,1)S(1)}, u32[]{:S(2)}, u32[]{:S(2)}) collective-permute-start(bf16[3,2,8,1024]{3,2,1,0:T(8,128)(2,1)S(1)} %fusion.7), channel_id=1, source_target_pairs={{0,2},{1,7},{2,0},{3,5},{4,6},{5,3},{6,4},{7,1},{8,10},{9,15},{10,... | collective-permute-start | bytes 294920 | tf_op jit(solution)/shard_map/ppermute | solution.py:46
  152.8 7.5 %collective-permute-start.37 = (bf16[3,2,8,1024]{3,2,1,0:T(8,128)(2,1)S(1)}, bf16[3,2,8,1024]{3,2,1,0:T(8,128)(2,1)S(1)}, u32[]{:S(2)}, u32[]{:S(2)}) collective-permute-start(bf16[3,2,8,1024]{3,2,1,0:T(8,128)(2,1)S(1)} %fusion.5), channel_id=1, source_target_pairs={{0,32},{1,97},{2,34},{3,99},{4,36},{5,101},{6,38},{7,103},{8,40},{... | collective-permute-start | bytes 294920 | tf_op jit(solution)/shard_map/ppermute | solution.py:46
  158.1 4.8 %collective-permute-start.43 = (bf16[3,2,8,1024]{3,2,1,0:T(8,128)(2,1)S(1)}, bf16[3,2,8,1024]{3,2,1,0:T(8,128)(2,1)S(1)}, u32[]{:S(2)}, u32[]{:S(2)}) collective-permute-start(bf16[3,2,8,1024]{3,2,1,0:T(8,128)(2,1)S(1)} %fusion.3), channel_id=1, source_target_pairs={{0,8},{1,25},{2,10},{3,27},{4,12},{5,29},{6,14},{7,31},{8,0},{9,17... | collective-permute-start | bytes 294920 | tf_op jit(solution)/shard_map/ppermute | solution.py:46
  (25 other events, 150.8 us)

commit v3 on v2

--- a/solution.py
+++ b/solution.py
@@ -363,6 +363,15 @@
     columns = master.shape[3]
     rows = tokens.shape[0]
 
+    steps = np.array(
+        [[[step[c] << SHIFTS[axes[2]] for step in STEPS] for axes in AXES] for c in range(2)], np.int32
+    ).reshape(2, -1)
+    there = group ^ jnp.where(core == 0, jnp.asarray(steps[0]), jnp.asarray(steps[1]))
+    seen = there[:, None] == jnp.arange(SIDE**3)[None]
+    pairs = jnp.sum(jnp.where(seen[:, :, None], placement[None], 0), 1)
+    pairs = pairs.reshape(CHAINS, 2 * SIDE)
+    table = jnp.concatenate([pairs, jnp.full((CHAINS, 1), core)], 1)
+
     near = [axes[0] for axes in AXES]
     mid = [axes[1] for axes in AXES]
     last = [axes[2] for axes in AXES]
@@ -371,25 +380,15 @@
     ones = [hop(blocks[c], near[c], ONE) for c in each]
     both = [jnp.stack([blocks[c], ones[c]], 0) for c in each]
     rests = [hop(both[c], near[c], BACK) for c in each]
-    cores = jnp.full((9,), core)
-    lines = [weave(cores, blocks[c], ones[c], rests[c]) for c in each]
+    lines = [weave(table[c], blocks[c], ones[c], rests[c]) for c in each]
 
     def other_rows(*rows):
         far = (1 - core) * columns
         return [lax.dynamic_slice_in_dim(v, far, columns, 1) for v in rows]
 
-    lines[0], tokens, cotangent, row_slot, placement = lax.optimization_barrier(
-        (lines[0], tokens, cotangent, row_slot, placement)
-    )
-    steps = np.array(
-        [[[step[c] << SHIFTS[axes[2]] for step in STEPS] for axes in AXES] for c in range(2)], np.int32
-    ).reshape(2, -1)
-    there = group ^ jnp.where(core == 0, jnp.asarray(steps[0]), jnp.asarray(steps[1]))
-    seen = there[:, None] == jnp.arange(SIDE**3)[None]
-    pairs = jnp.sum(jnp.where(seen[:, :, None], placement[None], 0), 1)
-    pairs = pairs.reshape(CHAINS, 2 * SIDE)
-    table = jnp.concatenate([pairs, jnp.full((CHAINS, 1), core)], 1)
-
+    lines[2], tokens, cotangent, row_slot = lax.optimization_barrier(
+        (lines[2], tokens, cotangent, row_slot)
+    )
     far_tokens, far_cotangent = other_rows(tokens, cotangent)
     rows_in = [tokens, swap(far_tokens), cotangent, swap(far_cotangent)]
     slots = jnp.concatenate([row_slot, swap(row_slot)], 0)
@@ -401,8 +400,10 @@
     rests[0], rows_in, chosen = lax.optimization_barrier((rests[0], rows_in, chosen))
     packed = [pick(table[c], lines[c], ones[c], rests[c]) for c in each]
 
-    def exchange(packed):
+    def exchange(packed, also=None):
         came = [hop(packed[c][1], last[c], ONE) for c in each]
+        if also is not None:
+            came[2], _ = lax.optimization_barrier((came[2], also))
         both = [jnp.stack([packed[c][2], came[c][1]], 0) for c in each]
         return [(packed[c][0], came[c], hop(both[c], last[c], BACK)) for c in each]
 
@@ -417,9 +418,8 @@
     weights = [f[1] for f in firsts]
     hidden = [v[3] for v in seconds]
     pair = [v[4] for v in seconds]
-    sent = exchange(seconds)
     far_rows = rows_out(table[0], hidden, pair, weights, [], rows)
-    sent[1], far_rows = lax.optimization_barrier((sent[1], far_rows))
+    sent = exchange(seconds, far_rows)
     merged = [merge(table[c], sent[c], experts) for c in each]
 
     def add(one, came):

time: 166 us -> 163 us (0.982)
  waiting for transfers between devices: 47.7 us -> 58.7 us
  Pallas kernels: 40 us -> 34 us
  local copies, waits for them, and re-layouts: 6.71 us -> 1.71 us
  other arithmetic: 6.63 us -> 4.46 us
    ppermute x36, waiting for transfers between devices: 47.7 us -> 57.9 us  [hop(): return lax.ppermute(value, BOTH, step_pairs(axis, offsets))]
    unnamed x58 -> x14, local copies, waits for them, and re-layouts: 4.14 us -> 1.09 us
    another operation x3, other arithmetic: 3 us -> 0.22 us  [shards(): both = [jnp.stack([lines[c], ones[c]], 0) for c in each]]
    ppermute x36, starting transfers between devices: 58.2 us -> 60.4 us  [hop(): return lax.ppermute(value, BOTH, step_pairs(axis, offsets))]
    pallas_call x3, Pallas kernels: 9.47 us -> 7.38 us  [first(): pl.pallas_call(first_kernel, out_shape=[jax.ShapeDtypeStruct((3, rows, 12...]
    pallas_call x3, Pallas kernels: 10.4 us -> 8.4 us  [second(): pl.pallas_call(second_kernel, out_shape=[shape_of(*lead, 2, 3, 32, column...]
    dynamic_slice x2, local copies, waits for them, and re-layouts: 2.14 us -> 0.19 us  [other_rows(): return [lax.dynamic_slice_in_dim(v, far, columns, 1) for v in rows]]
    pallas_call x3, Pallas kernels: 3.87 us -> 1.96 us  [pick(): pl.pallas_call(pick_kernel, out_shape=[shape_of(*lead, 2, 3, 4, 8, column...]
  transfers between devices with their start and end apart: 44 -> 44, of which waited for: 17 -> 21; matrix products, arithmetic and copies ran while one was open for 5% -> 2% of each run, Pallas kernels for 24% -> 21%
where the time goes in v3:
time: 163 us
  starting transfers between devices  62.9 us (39%)
  waiting for transfers between devices  58.7 us (36%)
  Pallas kernels  34 us (21%)
  other arithmetic  4.46 us (3%)
  local copies, waits for them, and re-layouts  1.71 us (1%)
    ppermute x36, starting transfers between devices, hop(): return lax.ppermute(value, BOTH, step_pairs(axis, offsets))  60.4 us
    ppermute x36, waiting for transfers between devices, hop(): return lax.ppermute(value, BOTH, step_pairs(axis, offsets))  57.9 us
    pallas_call x3, Pallas kernels, second(): pl.pallas_call(second_kernel, out_shape=[shape_of(*lead, 2, 3, 32, column...  8.4 us
    pallas_call x2, Pallas kernels, rows_out(): pl.pallas_call(functools.partial(rows_kernel, start), out_shape=[shape_of...  7.73 us
    pallas_call x3, Pallas kernels, first(): pl.pallas_call(first_kernel, out_shape=[jax.ShapeDtypeStruct((3, rows, 12...  7.38 us
    pallas_call x3, Pallas kernels, merge(): pl.pallas_call(merge_kernel, out_shape=[shape_of(*lead, 3, experts, 8, co...  3.54 us
  transfers between devices with their start and end apart: 44, of which 21 were waited for; matrix products, arithmetic and copies ran while one was open for 2% of the time, Pallas kernels for 21%

profile of v3, /device:TPU:0, one launch (start us, length us, event | category | flops | bytes accessed | tf_op | source)
XLA Modules:
  0.0 163.0 jit_solution(8243033235940396751)
XLA Ops:
  1.7 1.7 %collective-permute-start = (bf16[3,2,8,1024]{3,2,1,0:T(8,128)(2,1)S(1)}, bf16[3,2,8,1024]{3,2,1,0:T(8,128)(2,1)S(1)}, u32[]{:S(2)}, u32[]{:S(2)}) collective-permute-start(bf16[3,2,8,1024]{3,2,1,0:T(8,128)(2,1)S(1)} %get-tuple-element.71.own), channel_id=1, source_target_pairs={{0,2},{1,7},{2,0},{3,5},{4,6},{5,3},{6,4},{7,1},{8,10},{9,15},{10,... | collective-permute-start | bytes 294920 | tf_op jit(solution)/shard_map/ppermute | solution.py:46
  3.4 1.6 collective-permute-start.4
  5.0 1.9 %collective-permute-start.12 = (bf16[3,2,8,1024]{3,2,1,0:T(8,128)(2,1)S(1)}, bf16[3,2,8,1024]{3,2,1,0:T(8,128)(2,1)S(1)}, u32[]{:S(2)}, u32[]{:S(2)}) collective-permute-start(bf16[3,2,8,1024]{3,2,1,0:T(8,128)(2,1)S(1)} %get-tuple-element.87.own), channel_id=1, source_target_pairs={{0,32},{1,97},{2,34},{3,99},{4,36},{5,101},{6,38},{7,103},{8,40},{... | collective-permute-start | bytes 294920 | tf_op jit(solution)/shard_map/ppermute | solution.py:46
  8.7 2.2 %collective-permute-start.1 = (bf16[2,3,2,8,1024]{4,3,2,1,0:T(8,128)(2,1)S(1)}, bf16[2,3,2,8,1024]{4,3,2,1,0:T(8,128)(2,1)S(1)}, u32[]{:S(2)}, u32[]{:S(2)}) collective-permute-start(bf16[2,3,2,8,1024]{4,3,2,1,0:T(8,128)(2,1)S(1)} %pad_maximum_fusion.10), channel_id=1, source_target_pairs={{0,6},{1,3},{2,4},{3,1},{4,2},{5,7},{6,0},{7,5},{8,14},{9,11},{10,... | collective-permute-start | bytes 589832 | tf_op jit(solution)/shard_map/ppermute | solution.py:46
  10.9 2.3 %collective-permute-start.5 = (bf16[2,3,2,8,1024]{4,3,2,1,0:T(8,128)(2,1)S(1)}, bf16[2,3,2,8,1024]{4,3,2,1,0:T(8,128)(2,1)S(1)}, u32[]{:S(2)}, u32[]{:S(2)}) collective-permute-start(bf16[2,3,2,8,1024]{4,3,2,1,0:T(8,128)(2,1)S(1)} %pad_maximum_fusion.11), channel_id=1, source_target_pairs={{0,24},{1,9},{2,26},{3,11},{4,28},{5,13},{6,30},{7,15},{8,16},{9,1... | collective-permute-start | bytes 589832 | tf_op jit(solution)/shard_map/ppermute | solution.py:46
  13.2 3.5 %collective-permute-start.13 = (bf16[2,3,2,8,1024]{4,3,2,1,0:T(8,128)(2,1)S(1)}, bf16[2,3,2,8,1024]{4,3,2,1,0:T(8,128)(2,1)S(1)}, u32[]{:S(2)}, u32[]{:S(2)}) collective-permute-start(bf16[2,3,2,8,1024]{4,3,2,1,0:T(8,128)(2,1)S(1)} %pad_maximum_fusion.12), channel_id=1, source_target_pairs={{0,96},{1,33},{2,98},{3,35},{4,100},{5,37},{6,102},{7,39},{8,104},... | collective-permute-start | bytes 589832 | tf_op jit(solution)/shard_map/ppermute | solution.py:46
  23.0 2.4 %collective-permute-done.2.one = bf16[3,8,8,1024]{3,2,1,0:T(8,128)(2,1)S(1)} collective-permute-done((bf16[3,8,8,1024]{3,2,1,0:T(8,128)(2,1)S(1)}, bf16[3,8,8,1024]{3,2,1,0:T(8,128)(2,1)S(1)}, u32[]{:S(2)}, u32[]{:S(2)}) %collective-permute-start.2) | collective-permute-done | bytes 393248 | tf_op jit(solution)/shard_map/ppermute | solution.py:46
  25.4 1.3 collective-permute-start.3
  26.7 2.3 %collective-permute-done.14.one = bf16[3,8,8,1024]{3,2,1,0:T(8,128)(2,1)S(1)} collective-permute-done((bf16[3,8,8,1024]{3,2,1,0:T(8,128)(2,1)S(1)}, bf16[3,8,8,1024]{3,2,1,0:T(8,128)(2,1)S(1)}, u32[]{:S(2)}, u32[]{:S(2)}) %collective-permute-start.14) | collective-permute-done | bytes 393248 | tf_op jit(solution)/shard_map/ppermute | solution.py:46
  31.3 3.0 %collective-permute-start.20 = (bf16[2,3,8,8,1024]{4,3,2,1,0:T(8,128)(2,1)S(1)}, bf16[2,3,8,8,1024]{4,3,2,1,0:T(8,128)(2,1)S(1)}, u32[]{:S(2)}, u32[]{:S(2)}) collective-permute-start(bf16[2,3,8,8,1024]{4,3,2,1,0:T(8,128)(2,1)S(1)} %pad_maximum_fusion.4), channel_id=1, source_target_pairs={{0,96},{1,33},{2,98},{3,35},{4,100},{5,37},{6,102},{7,39},{8,104},... | collective-permute-start | bytes 2359304 | tf_op jit(solution)/shard_map/ppermute | solution.py:46
  34.3 4.4 %collective-permute-done.3.rest = bf16[2,3,8,8,1024]{4,3,2,1,0:T(8,128)(2,1)S(1)} collective-permute-done((bf16[2,3,8,8,1024]{4,3,2,1,0:T(8,128)(2,1)S(1)}, bf16[2,3,8,8,1024]{4,3,2,1,0:T(8,128)(2,1)S(1)}, u32[]{:S(2)}, u32[]{:S(2)}) %collective-permute-start.3) | collective-permute-done | bytes 786464 | tf_op jit(solution)/shard_map/ppermute | solution.py:46
  39.8 2.5 %collective-permute-done.15.rest = bf16[2,3,8,8,1024]{4,3,2,1,0:T(8,128)(2,1)S(1)} collective-permute-done((bf16[2,3,8,8,1024]{4,3,2,1,0:T(8,128)(2,1)S(1)}, bf16[2,3,8,8,1024]{4,3,2,1,0:T(8,128)(2,1)S(1)}, u32[]{:S(2)}, u32[]{:S(2)}) %collective-permute-start.15) | collective-permute-done | bytes 786464 | tf_op jit(solution)/shard_map/ppermute | solution.py:46
  43.6 5.2 %collective-permute-done.20.rest = bf16[2,3,8,8,1024]{4,3,2,1,0:T(8,128)(2,1)S(1)} collective-permute-done((bf16[2,3,8,8,1024]{4,3,2,1,0:T(8,128)(2,1)S(1)}, bf16[2,3,8,8,1024]{4,3,2,1,0:T(8,128)(2,1)S(1)}, u32[]{:S(2)}, u32[]{:S(2)}) %collective-permute-start.20) | collective-permute-done | bytes 786464 | tf_op jit(solution)/shard_map/ppermute | solution.py:46
  49.4 3.0 %collective-permute-start.21 = (bf16[2,2,3,4,8,1024]{5,4,3,2,1,0:T(8,128)(2,1)S(1)}, bf16[2,2,3,4,8,1024]{5,4,3,2,1,0:T(8,128)(2,1)S(1)}, u32[]{:S(2)}, u32[]{:S(2)}) collective-permute-start(bf16[2,2,3,4,8,1024]{5,4,3,2,1,0:T(8,128)(2,1)S(1)} %get-tuple-element.95), channel_id=1, source_target_pairs={{0,2},{1,7},{2,0},{3,5},{4,6},{5,3},{6,4},{7,1},{8,10},{9,15},{10,... | collective-permute-start | bytes 2359304 | tf_op jit(solution)/shard_map/ppermute | solution.py:46
  52.5 3.8 %collective-permute-start.10 = (bf16[2,2,3,4,8,1024]{5,4,3,2,1,0:T(8,128)(2,1)S(1)}, bf16[2,2,3,4,8,1024]{5,4,3,2,1,0:T(8,128)(2,1)S(1)}, u32[]{:S(2)}, u32[]{:S(2)}) collective-permute-start(bf16[2,2,3,4,8,1024]{5,4,3,2,1,0:T(8,128)(2,1)S(1)} %pad_maximum_fusion.1), channel_id=1, source_target_pairs={{0,96},{1,33},{2,98},{3,35},{4,100},{5,37},{6,102},{7,39},{8,104},... | collective-permute-start | bytes 2359304 | tf_op jit(solution)/shard_map/ppermute | solution.py:46
  56.4 1.4 collective-permute-start.17
  57.8 8.3 %collective-permute-done.21 = bf16[2,2,3,4,8,1024]{5,4,3,2,1,0:T(8,128)(2,1)S(1)} collective-permute-done((bf16[2,2,3,4,8,1024]{5,4,3,2,1,0:T(8,128)(2,1)S(1)}, bf16[2,2,3,4,8,1024]{5,4,3,2,1,0:T(8,128)(2,1)S(1)}, u32[]{:S(2)}, u32[]{:S(2)}) %collective-permute-start.21) | collective-permute-done | bytes 786464 | tf_op jit(solution)/shard_map/ppermute | solution.py:46
  66.2 4.8 %collective-permute-start.22 = (bf16[2,2,3,4,8,1024]{5,4,3,2,1,0:T(8,128)(2,1)S(1)}, bf16[2,2,3,4,8,1024]{5,4,3,2,1,0:T(8,128)(2,1)S(1)}, u32[]{:S(2)}, u32[]{:S(2)}) collective-permute-start(bf16[2,2,3,4,8,1024]{5,4,3,2,1,0:T(8,128)(2,1)S(1)} %pad_maximum_fusion.5), channel_id=1, source_target_pairs={{0,6},{1,3},{2,4},{3,1},{4,2},{5,7},{6,0},{7,5},{8,14},{9,11},{10,... | collective-permute-start | bytes 2359304 | tf_op jit(solution)/shard_map/ppermute | solution.py:46
  70.9 2.5 %first.3 = (f32[3,1024,128]{2,1,0:T(8,128)S(1)}, bf16[2,3,4,32,1024]{4,3,2,1,0:T(8,128)(2,1)S(1)}) custom-call(s32[9]{0:T(128)S(1)} %get-tuple-element.142.table_ref, bf16[512,2048]{1,0:T(8,128)(2,1)S(1)} %copy-done, bf16[512,1024]{1,0:T(8,128)(2,1)S(1)} %collective-permute-done.6.tok1, bf16[512,2048]{1,0:T(8,128)(2,1)S(1)} %copy-done.1, ...), custom_call_target="tpu_custom_call" | custom-call | tf_op jit(solution)/shard_map/first/pallas_call | solution.py:198
  73.5 2.5 %first.4 = (f32[3,1024,128]{2,1,0:T(8,128)S(1)}, bf16[2,3,4,32,1024]{4,3,2,1,0:T(8,128)(2,1)S(1)}) custom-call(s32[9]{0:T(128)S(1)} %get-tuple-element.140.table_ref, bf16[512,2048]{1,0:T(8,128)(2,1)S(1)} %copy-done, bf16[512,1024]{1,0:T(8,128)(2,1)S(1)} %collective-permute-done.6.tok1, bf16[512,2048]{1,0:T(8,128)(2,1)S(1)} %copy-done.1, ...), custom_call_target="tpu_custom_call" | custom-call | tf_op jit(solution)/shard_map/first/pallas_call | solution.py:198
  76.7 4.2 %collective-permute-done.22 = bf16[2,2,3,4,8,1024]{5,4,3,2,1,0:T(8,128)(2,1)S(1)} collective-permute-done((bf16[2,2,3,4,8,1024]{5,4,3,2,1,0:T(8,128)(2,1)S(1)}, bf16[2,2,3,4,8,1024]{5,4,3,2,1,0:T(8,128)(2,1)S(1)}, u32[]{:S(2)}, u32[]{:S(2)}) %collective-permute-start.22) | collective-permute-done | bytes 786464 | tf_op jit(solution)/shard_map/ppermute | solution.py:46
  80.9 2.5 %first.5 = (f32[3,1024,128]{2,1,0:T(8,128)S(1)}, bf16[2,3,4,32,1024]{4,3,2,1,0:T(8,128)(2,1)S(1)}) custom-call(s32[9]{0:T(128)S(1)} %get-tuple-element.141.table_ref, bf16[512,2048]{1,0:T(8,128)(2,1)S(1)} %copy-done, bf16[512,1024]{1,0:T(8,128)(2,1)S(1)} %collective-permute-done.6.tok1, bf16[512,2048]{1,0:T(8,128)(2,1)S(1)} %copy-done.1, ...), custom_call_target="tpu_custom_call" | custom-call | tf_op jit(solution)/shard_map/first/pallas_call | solution.py:198
  83.5 2.8 %second.3 = (bf16[2,3,32,1024]{3,2,1,0:T(8,128)(2,1)S(1)}, bf16[2,2,3,32,1024]{4,3,2,1,0:T(8,128)(2,1)S(1)}, bf16[2,3,32,1024]{3,2,1,0:T(8,128)(2,1)S(1)}, bf16[...) custom-call(s32[9]{0:T(128)S(1)} %get-tuple-element.142.table_ref, bf16[512,2048]{1,0:T(8,128)(2,1)S(1)} %copy-done, ...), custom_call_target="tpu_custom_call" | custom-call | tf_op jit(solution)/shard_map/second/pallas_call | solution.py:263
  86.4 2.8 %second.4 = (bf16[2,3,32,1024]{3,2,1,0:T(8,128)(2,1)S(1)}, bf16[2,2,3,32,1024]{4,3,2,1,0:T(8,128)(2,1)S(1)}, bf16[2,3,32,1024]{3,2,1,0:T(8,128)(2,1)S(1)}, bf16[...) custom-call(s32[9]{0:T(128)S(1)} %get-tuple-element.140.table_ref, bf16[512,2048]{1,0:T(8,128)(2,1)S(1)} %copy-done, ...), custom_call_target="tpu_custom_call" | custom-call | tf_op jit(solution)/shard_map/second/pallas_call | solution.py:263
  89.3 2.8 %second.5 = (bf16[2,3,32,1024]{3,2,1,0:T(8,128)(2,1)S(1)}, bf16[2,2,3,32,1024]{4,3,2,1,0:T(8,128)(2,1)S(1)}, bf16[2,3,32,1024]{3,2,1,0:T(8,128)(2,1)S(1)}, bf16[...) custom-call(s32[9]{0:T(128)S(1)} %get-tuple-element.141.table_ref, bf16[512,2048]{1,0:T(8,128)(2,1)S(1)} %copy-done, ...), custom_call_target="tpu_custom_call" | custom-call | tf_op jit(solution)/shard_map/second/pallas_call | solution.py:263
  92.2 6.2 %collective-permute-done.26 = bf16[2,2,3,32,1024]{4,3,2,1,0:T(8,128)(2,1)S(1)} collective-permute-done((bf16[2,2,3,32,1024]{4,3,2,1,0:T(8,128)(2,1)S(1)}, bf16[2,2,3,32,1024]{4,3,2,1,0:T(8,128)(2,1)S(1)}, u32[]{:S(2)}, u32[]{:S(2)}) %collective-permute-start.26) | collective-permute-done | bytes 786464 | tf_op jit(solution)/shard_map/ppermute | solution.py:46
  98.5 3.5 %collective-permute-start.27 = (bf16[2,2,3,32,1024]{4,3,2,1,0:T(8,128)(2,1)S(1)}, bf16[2,2,3,32,1024]{4,3,2,1,0:T(8,128)(2,1)S(1)}, u32[]{:S(2)}, u32[]{:S(2)}) collective-permute-start(bf16[2,2,3,32,1024]{4,3,2,1,0:T(8,128)(2,1)S(1)} %pad_maximum_fusion.6), channel_id=1, source_target_pairs={{0,96},{1,33},{2,98},{3,35},{4,100},{5,37},{6,102},{7,39},{8,104},... | collective-permute-start | bytes 2359304 | tf_op jit(solution)/shard_map/ppermute | solution.py:46
  102.1 1.5 collective-permute-start.33
  103.6 3.1 %rows_out.2 = (bf16[512,1024]{1,0:T(8,128)(2,1)S(1)}, bf16[512,1024]{1,0:T(8,128)(2,1)S(1)}) custom-call(s32[9]{0:T(128)S(1)} %get-tuple-element.142.table_ref, bf16[1024,256]{1,0:T(8,128)(2,1)S(1)} %get-tuple-element.86.refs_0_, bf16[1024,256]{1,0:T(8,128)(2,1)S(1)} %get-tuple-element.92.refs_1_, bf16[1024,256]{1,0:T(8,128)(2,1)S(1)} %get-tuple-element.98.refs_2_, ...), custom_call_target="tpu_custom_call" | custom-call | tf_op jit(solution)/shard_map/rows_out/pallas_call | solution.py:321
  106.9 3.0 %collective-permute-start.39 = (bf16[2,2,3,32,1024]{4,3,2,1,0:T(8,128)(2,1)S(1)}, bf16[2,2,3,32,1024]{4,3,2,1,0:T(8,128)(2,1)S(1)}, u32[]{:S(2)}, u32[]{:S(2)}) collective-permute-start(bf16[2,2,3,32,1024]{4,3,2,1,0:T(8,128)(2,1)S(1)} %pad_maximum_fusion.8), channel_id=1, source_target_pairs={{0,6},{1,3},{2,4},{3,1},{4,2},{5,7},{6,0},{7,5},{8,14},{9,11},{10,... | collective-permute-start | bytes 2359304 | tf_op jit(solution)/shard_map/ppermute | solution.py:46
  109.9 2.1 %collective-permute-done.27 = bf16[2,2,3,32,1024]{4,3,2,1,0:T(8,128)(2,1)S(1)} collective-permute-done((bf16[2,2,3,32,1024]{4,3,2,1,0:T(8,128)(2,1)S(1)}, bf16[2,2,3,32,1024]{4,3,2,1,0:T(8,128)(2,1)S(1)}, u32[]{:S(2)}, u32[]{:S(2)}) %collective-permute-start.27) | collective-permute-done | bytes 786464 | tf_op jit(solution)/shard_map/ppermute | solution.py:46
  112.0 1.2 merge.3
  113.2 1.7 %collective-permute-start.28 = (bf16[2,3,8,8,1024]{4,3,2,1,0:T(8,128)(2,1)S(1)}, bf16[2,3,8,8,1024]{4,3,2,1,0:T(8,128)(2,1)S(1)}, u32[]{:S(2)}, u32[]{:S(2)}) collective-permute-start(bf16[2,3,8,8,1024]{4,3,2,1,0:T(8,128)(2,1)S(1)} %get-tuple-element.113), channel_id=1, source_target_pairs={{0,24},{1,9},{2,26},{3,11},{4,28},{5,13},{6,30},{7,15},{8,16},{9,1... | collective-permute-start | bytes 2359304 | tf_op jit(solution)/shard_map/ppermute | solution.py:46
  115.4 1.2 merge.4
  116.6 3.3 %collective-permute-start.34 = (bf16[2,3,8,8,1024]{4,3,2,1,0:T(8,128)(2,1)S(1)}, bf16[2,3,8,8,1024]{4,3,2,1,0:T(8,128)(2,1)S(1)}, u32[]{:S(2)}, u32[]{:S(2)}) collective-permute-start(bf16[2,3,8,8,1024]{4,3,2,1,0:T(8,128)(2,1)S(1)} %get-tuple-element.122), channel_id=1, source_target_pairs={{0,6},{1,3},{2,4},{3,1},{4,2},{5,7},{6,0},{7,5},{8,14},{9,11},{10,... | collective-permute-start | bytes 2359304 | tf_op jit(solution)/shard_map/ppermute | solution.py:46
  121.4 2.8 %collective-permute-start.40 = (bf16[2,3,8,8,1024]{4,3,2,1,0:T(8,128)(2,1)S(1)}, bf16[2,3,8,8,1024]{4,3,2,1,0:T(8,128)(2,1)S(1)}, u32[]{:S(2)}, u32[]{:S(2)}) collective-permute-start(bf16[2,3,8,8,1024]{4,3,2,1,0:T(8,128)(2,1)S(1)} %get-tuple-element.132), channel_id=1, source_target_pairs={{0,96},{1,33},{2,98},{3,35},{4,100},{5,37},{6,102},{7,39},{8,104},... | collective-permute-start | bytes 2359304 | tf_op jit(solution)/shard_map/ppermute | solution.py:46
  124.7 2.0 %collective-permute-done.28.came = bf16[2,3,8,8,1024]{4,3,2,1,0:T(8,128)(2,1)S(1)} collective-permute-done((bf16[2,3,8,8,1024]{4,3,2,1,0:T(8,128)(2,1)S(1)}, bf16[2,3,8,8,1024]{4,3,2,1,0:T(8,128)(2,1)S(1)}, u32[]{:S(2)}, u32[]{:S(2)}) %collective-permute-start.28) | collective-permute-done | bytes 786464 | tf_op jit(solution)/shard_map/ppermute | solution.py:46
  126.9 3.0 %collective-permute-done.34.came = bf16[2,3,8,8,1024]{4,3,2,1,0:T(8,128)(2,1)S(1)} collective-permute-done((bf16[2,3,8,8,1024]{4,3,2,1,0:T(8,128)(2,1)S(1)}, bf16[2,3,8,8,1024]{4,3,2,1,0:T(8,128)(2,1)S(1)}, u32[]{:S(2)}, u32[]{:S(2)}) %collective-permute-start.34) | collective-permute-done | bytes 786464 | tf_op jit(solution)/shard_map/ppermute | solution.py:46
  130.1 4.5 %collective-permute-done.40.came = bf16[2,3,8,8,1024]{4,3,2,1,0:T(8,128)(2,1)S(1)} collective-permute-done((bf16[2,3,8,8,1024]{4,3,2,1,0:T(8,128)(2,1)S(1)}, bf16[2,3,8,8,1024]{4,3,2,1,0:T(8,128)(2,1)S(1)}, u32[]{:S(2)}, u32[]{:S(2)}) %collective-permute-start.40) | collective-permute-done | bytes 786464 | tf_op jit(solution)/shard_map/ppermute | solution.py:46
  134.8 1.6 collective-permute-start.41
  137.2 3.0 %collective-permute-start.30 = (bf16[2,3,2,8,1024]{4,3,2,1,0:T(8,128)(2,1)S(1)}, bf16[2,3,2,8,1024]{4,3,2,1,0:T(8,128)(2,1)S(1)}, u32[]{:S(2)}, u32[]{:S(2)}) collective-permute-start(bf16[2,3,2,8,1024]{4,3,2,1,0:T(8,128)(2,1)S(1)} %get-tuple-element.116), channel_id=1, source_target_pairs={{0,6},{1,3},{2,4},{3,1},{4,2},{5,7},{6,0},{7,5},{8,14},{9,11},{10,... | collective-permute-start | bytes 589832 | tf_op jit(solution)/shard_map/ppermute | solution.py:46
  140.2 4.6 %rows_out.3 = (bf16[512,2048]{1,0:T(8,128)(2,1)}, bf16[512,2048]{1,0:T(8,128)(2,1)}) custom-call(s32[9]{0:T(128)S(1)} %get-tuple-element.142.table_ref, bf16[1024,256]{1,0:T(8,128)(2,1)S(1)} %get-tuple-element.86.refs_0_, bf16[1024,256]{1,0:T(8,128)(2,1)S(1)} %get-tuple-element.92.refs_1_, bf16[1024,256]{1,0:T(8,128)(2,1)S(1)} %get-tuple-element.98.refs_2_, ...), custom_call_target="tpu_custom_call" | custom-call | tf_op jit(solution)/shard_map/rows_out/pallas_call | solution.py:321
  145.7 3.2 %collective-permute-start.36 = (bf16[2,3,2,8,1024]{4,3,2,1,0:T(8,128)(2,1)S(1)}, bf16[2,3,2,8,1024]{4,3,2,1,0:T(8,128)(2,1)S(1)}, u32[]{:S(2)}, u32[]{:S(2)}) collective-permute-start(bf16[2,3,2,8,1024]{4,3,2,1,0:T(8,128)(2,1)S(1)} %get-tuple-element.125), channel_id=1, source_target_pairs={{0,96},{1,33},{2,98},{3,35},{4,100},{5,37},{6,102},{7,39},{8,104},... | collective-permute-start | bytes 589832 | tf_op jit(solution)/shard_map/ppermute | solution.py:46
  149.7 2.2 %collective-permute-start.42 = (bf16[2,3,2,8,1024]{4,3,2,1,0:T(8,128)(2,1)S(1)}, bf16[2,3,2,8,1024]{4,3,2,1,0:T(8,128)(2,1)S(1)}, u32[]{:S(2)}, u32[]{:S(2)}) collective-permute-start(bf16[2,3,2,8,1024]{4,3,2,1,0:T(8,128)(2,1)S(1)} %get-tuple-element.135), channel_id=1, source_target_pairs={{0,24},{1,9},{2,26},{3,11},{4,28},{5,13},{6,30},{7,15},{8,16},{9,1... | collective-permute-start | bytes 589832 | tf_op jit(solution)/shard_map/ppermute | solution.py:46
  152.1 1.2 collective-permute-done.36
  153.4 3.3 %collective-permute-done.42 = bf16[2,3,2,8,1024]{4,3,2,1,0:T(8,128)(2,1)S(1)} collective-permute-done((bf16[2,3,2,8,1024]{4,3,2,1,0:T(8,128)(2,1)S(1)}, bf16[2,3,2,8,1024]{4,3,2,1,0:T(8,128)(2,1)S(1)}, u32[]{:S(2)}, u32[]{:S(2)}) %collective-permute-start.42) | collective-permute-done | bytes 196640 | tf_op jit(solution)/shard_map/ppermute | solution.py:46
  158.0 3.4 %collective-permute-done.43 = bf16[3,2,8,1024]{3,2,1,0:T(8,128)(2,1)S(1)} collective-permute-done((bf16[3,2,8,1024]{3,2,1,0:T(8,128)(2,1)S(1)}, bf16[3,2,8,1024]{3,2,1,0:T(8,128)(2,1)S(1)}, u32[]{:S(2)}, u32[]{:S(2)}) %collective-permute-start.43) | collective-permute-done | bytes 98336 | tf_op jit(solution)/shard_map/ppermute | solution.py:46
  161.5 1.5 divide_subtract_fusion
  (112 shorter events, 23.6 us)
Async XLA Ops:
  1.7 17.0 %copy-start = (bf16[512,2048]{1,0:T(8,128)(2,1)S(1)}, bf16[512,2048]{1,0:T(8,128)(2,1)}, u32[]{:S(2)}) copy-start(bf16[512,2048]{1,0:T(8,128)(2,1)} %tok0.5) | copy-start | bytes 6291460
  1.7 6.9 %collective-permute-start = (bf16[3,2,8,1024]{3,2,1,0:T(8,128)(2,1)S(1)}, bf16[3,2,8,1024]{3,2,1,0:T(8,128)(2,1)S(1)}, u32[]{:S(2)}, u32[]{:S(2)}) collective-permute-start(bf16[3,2,8,1024]{3,2,1,0:T(8,128)(2,1)S(1)} %get-tuple-element.71.own), channel_id=1, source_target_pairs={{0,2},{1,7},{2,0},{3,5},{4,6},{5,3},{6,4},{7,1},{8,10},{9,15},{10,... | collective-permute-start | bytes 294920 | tf_op jit(solution)/shard_map/ppermute | solution.py:46
  3.4 7.5 %collective-permute-start.4 = (bf16[3,2,8,1024]{3,2,1,0:T(8,128)(2,1)S(1)}, bf16[3,2,8,1024]{3,2,1,0:T(8,128)(2,1)S(1)}, u32[]{:S(2)}, u32[]{:S(2)}) collective-permute-start(bf16[3,2,8,1024]{3,2,1,0:T(8,128)(2,1)S(1)} %get-tuple-element.72.own), channel_id=1, source_target_pairs={{0,8},{1,25},{2,10},{3,27},{4,12},{5,29},{6,14},{7,31},{8,0},{9,17... | collective-permute-start | bytes 294920 | tf_op jit(solution)/shard_map/ppermute | solution.py:46
  5.0 8.2 %collective-permute-start.12 = (bf16[3,2,8,1024]{3,2,1,0:T(8,128)(2,1)S(1)}, bf16[3,2,8,1024]{3,2,1,0:T(8,128)(2,1)S(1)}, u32[]{:S(2)}, u32[]{:S(2)}) collective-permute-start(bf16[3,2,8,1024]{3,2,1,0:T(8,128)(2,1)S(1)} %get-tuple-element.87.own), channel_id=1, source_target_pairs={{0,32},{1,97},{2,34},{3,99},{4,36},{5,101},{6,38},{7,103},{8,40},{... | collective-permute-start | bytes 294920 | tf_op jit(solution)/shard_map/ppermute | solution.py:46
  8.7 8.0 %collective-permute-start.1 = (bf16[2,3,2,8,1024]{4,3,2,1,0:T(8,128)(2,1)S(1)}, bf16[2,3,2,8,1024]{4,3,2,1,0:T(8,128)(2,1)S(1)}, u32[]{:S(2)}, u32[]{:S(2)}) collective-permute-start(bf16[2,3,2,8,1024]{4,3,2,1,0:T(8,128)(2,1)S(1)} %pad_maximum_fusion.10), channel_id=1, source_target_pairs={{0,6},{1,3},{2,4},{3,1},{4,2},{5,7},{6,0},{7,5},{8,14},{9,11},{10,... | collective-permute-start | bytes 589832 | tf_op jit(solution)/shard_map/ppermute | solution.py:46
  10.9 7.0 %collective-permute-start.5 = (bf16[2,3,2,8,1024]{4,3,2,1,0:T(8,128)(2,1)S(1)}, bf16[2,3,2,8,1024]{4,3,2,1,0:T(8,128)(2,1)S(1)}, u32[]{:S(2)}, u32[]{:S(2)}) collective-permute-start(bf16[2,3,2,8,1024]{4,3,2,1,0:T(8,128)(2,1)S(1)} %pad_maximum_fusion.11), channel_id=1, source_target_pairs={{0,24},{1,9},{2,26},{3,11},{4,28},{5,13},{6,30},{7,15},{8,16},{9,1... | collective-permute-start | bytes 589832 | tf_op jit(solution)/shard_map/ppermute | solution.py:46
  13.2 7.1 %collective-permute-start.13 = (bf16[2,3,2,8,1024]{4,3,2,1,0:T(8,128)(2,1)S(1)}, bf16[2,3,2,8,1024]{4,3,2,1,0:T(8,128)(2,1)S(1)}, u32[]{:S(2)}, u32[]{:S(2)}) collective-permute-start(bf16[2,3,2,8,1024]{4,3,2,1,0:T(8,128)(2,1)S(1)} %pad_maximum_fusion.12), channel_id=1, source_target_pairs={{0,96},{1,33},{2,98},{3,35},{4,100},{5,37},{6,102},{7,39},{8,104},... | collective-permute-start | bytes 589832 | tf_op jit(solution)/shard_map/ppermute | solution.py:46
  17.5 7.9 %collective-permute-start.2 = (bf16[3,8,8,1024]{3,2,1,0:T(8,128)(2,1)S(1)}, bf16[3,8,8,1024]{3,2,1,0:T(8,128)(2,1)S(1)}, u32[]{:S(2)}, u32[]{:S(2)}) collective-permute-start(bf16[3,8,8,1024]{3,2,1,0:T(8,128)(2,1)S(1)} %weave.3.kept), channel_id=1, source_target_pairs={{0,8},{1,25},{2,10},{3,27},{4,12},{5,29},{6,14},{7,31},{8,0},{9,17... | collective-permute-start | bytes 1179656 | tf_op jit(solution)/shard_map/ppermute | solution.py:46
  18.8 15.5 %collective-permute-start.6 = (bf16[512,1024]{1,0:T(8,128)(2,1)S(1)}, bf16[512,1024]{1,0:T(8,128)(2,1)S(1)}, u32[]{:S(2)}, u32[]{:S(2)}) collective-permute-start(bf16[512,1024]{1,0:T(8,128)(2,1)S(1)} %constant_dynamic-slice_fusion.1), channel_id=1, source_target_pairs={{0,1},{1,0},{2,3},{3,2},{4,5},{5,4},{6,7},{7,6},{8,9},{9,8},{10,11... | collective-permute-start | bytes 3145736 | tf_op jit(solution)/shard_map/ppermute | solution.py:50
  21.1 7.9 %collective-permute-start.14 = (bf16[3,8,8,1024]{3,2,1,0:T(8,128)(2,1)S(1)}, bf16[3,8,8,1024]{3,2,1,0:T(8,128)(2,1)S(1)}, u32[]{:S(2)}, u32[]{:S(2)}) collective-permute-start(bf16[3,8,8,1024]{3,2,1,0:T(8,128)(2,1)S(1)} %weave.5.kept), channel_id=1, source_target_pairs={{0,2},{1,7},{2,0},{3,5},{4,6},{5,3},{6,4},{7,1},{8,10},{9,15},{10,... | collective-permute-start | bytes 1179656 | tf_op jit(solution)/shard_map/ppermute | solution.py:46
  21.7 12.6 %collective-permute-start.7 = (bf16[512,1024]{1,0:T(8,128)(2,1)S(1)}, bf16[512,1024]{1,0:T(8,128)(2,1)S(1)}, u32[]{:S(2)}, u32[]{:S(2)}) collective-permute-start(bf16[512,1024]{1,0:T(8,128)(2,1)S(1)} %constant_dynamic-slice_fusion), channel_id=1, source_target_pairs={{0,1},{1,0},{2,3},{3,2},{4,5},{5,4},{6,7},{7,6},{8,9},{9,8},{10,11... | collective-permute-start | bytes 3145736 | tf_op jit(solution)/shard_map/ppermute | solution.py:50
  21.8 8.3 %collective-permute-start.19 = (bf16[3,8,8,1024]{3,2,1,0:T(8,128)(2,1)S(1)}, bf16[3,8,8,1024]{3,2,1,0:T(8,128)(2,1)S(1)}, u32[]{:S(2)}, u32[]{:S(2)}) collective-permute-start(bf16[3,8,8,1024]{3,2,1,0:T(8,128)(2,1)S(1)} %weave.4.kept), channel_id=1, source_target_pairs={{0,32},{1,97},{2,34},{3,99},{4,36},{5,101},{6,38},{7,103},{8,40},{... | collective-permute-start | bytes 1179656 | tf_op jit(solution)/shard_map/ppermute | solution.py:46
  25.4 13.3 %collective-permute-start.3 = (bf16[2,3,8,8,1024]{4,3,2,1,0:T(8,128)(2,1)S(1)}, bf16[2,3,8,8,1024]{4,3,2,1,0:T(8,128)(2,1)S(1)}, u32[]{:S(2)}, u32[]{:S(2)}) collective-permute-start(bf16[2,3,8,8,1024]{4,3,2,1,0:T(8,128)(2,1)S(1)} %pad_maximum_fusion), channel_id=1, source_target_pairs={{0,24},{1,9},{2,26},{3,11},{4,28},{5,13},{6,30},{7,15},{8,16},{9,1... | collective-permute-start | bytes 2359304 | tf_op jit(solution)/shard_map/ppermute | solution.py:46
  29.0 13.3 %collective-permute-start.15 = (bf16[2,3,8,8,1024]{4,3,2,1,0:T(8,128)(2,1)S(1)}, bf16[2,3,8,8,1024]{4,3,2,1,0:T(8,128)(2,1)S(1)}, u32[]{:S(2)}, u32[]{:S(2)}) collective-permute-start(bf16[2,3,8,8,1024]{4,3,2,1,0:T(8,128)(2,1)S(1)} %pad_maximum_fusion.2), channel_id=1, source_target_pairs={{0,6},{1,3},{2,4},{3,1},{4,2},{5,7},{6,0},{7,5},{8,14},{9,11},{10,... | collective-permute-start | bytes 2359304 | tf_op jit(solution)/shard_map/ppermute | solution.py:46
  30.1 1.2 collective-permute-start.8
  31.3 17.4 %collective-permute-start.20 = (bf16[2,3,8,8,1024]{4,3,2,1,0:T(8,128)(2,1)S(1)}, bf16[2,3,8,8,1024]{4,3,2,1,0:T(8,128)(2,1)S(1)}, u32[]{:S(2)}, u32[]{:S(2)}) collective-permute-start(bf16[2,3,8,8,1024]{4,3,2,1,0:T(8,128)(2,1)S(1)} %pad_maximum_fusion.4), channel_id=1, source_target_pairs={{0,96},{1,33},{2,98},{3,35},{4,100},{5,37},{6,102},{7,39},{8,104},... | collective-permute-start | bytes 2359304 | tf_op jit(solution)/shard_map/ppermute | solution.py:46
  39.5 12.8 %collective-permute-start.9 = (bf16[2,2,3,4,8,1024]{5,4,3,2,1,0:T(8,128)(2,1)S(1)}, bf16[2,2,3,4,8,1024]{5,4,3,2,1,0:T(8,128)(2,1)S(1)}, u32[]{:S(2)}, u32[]{:S(2)}) collective-permute-start(bf16[2,2,3,4,8,1024]{5,4,3,2,1,0:T(8,128)(2,1)S(1)} %get-tuple-element.83), channel_id=1, source_target_pairs={{0,32},{1,97},{2,34},{3,99},{4,36},{5,101},{6,38},{7,103},{8,40},{... | collective-permute-start | bytes 2359304 | tf_op jit(solution)/shard_map/ppermute | solution.py:46
  43.0 13.3 %collective-permute-start.16 = (bf16[2,2,3,4,8,1024]{5,4,3,2,1,0:T(8,128)(2,1)S(1)}, bf16[2,2,3,4,8,1024]{5,4,3,2,1,0:T(8,128)(2,1)S(1)}, u32[]{:S(2)}, u32[]{:S(2)}) collective-permute-start(bf16[2,2,3,4,8,1024]{5,4,3,2,1,0:T(8,128)(2,1)S(1)} %get-tuple-element.89), channel_id=1, source_target_pairs={{0,8},{1,25},{2,10},{3,27},{4,12},{5,29},{6,14},{7,31},{8,0},{9,17... | collective-permute-start | bytes 2359304 | tf_op jit(solution)/shard_map/ppermute | solution.py:46
  49.4 16.7 %collective-permute-start.21 = (bf16[2,2,3,4,8,1024]{5,4,3,2,1,0:T(8,128)(2,1)S(1)}, bf16[2,2,3,4,8,1024]{5,4,3,2,1,0:T(8,128)(2,1)S(1)}, u32[]{:S(2)}, u32[]{:S(2)}) collective-permute-start(bf16[2,2,3,4,8,1024]{5,4,3,2,1,0:T(8,128)(2,1)S(1)} %get-tuple-element.95), channel_id=1, source_target_pairs={{0,2},{1,7},{2,0},{3,5},{4,6},{5,3},{6,4},{7,1},{8,10},{9,15},{10,... | collective-permute-start | bytes 2359304 | tf_op jit(solution)/shard_map/ppermute | solution.py:46
  52.5 18.5 %collective-permute-start.10 = (bf16[2,2,3,4,8,1024]{5,4,3,2,1,0:T(8,128)(2,1)S(1)}, bf16[2,2,3,4,8,1024]{5,4,3,2,1,0:T(8,128)(2,1)S(1)}, u32[]{:S(2)}, u32[]{:S(2)}) collective-permute-start(bf16[2,2,3,4,8,1024]{5,4,3,2,1,0:T(8,128)(2,1)S(1)} %pad_maximum_fusion.1), channel_id=1, source_target_pairs={{0,96},{1,33},{2,98},{3,35},{4,100},{5,37},{6,102},{7,39},{8,104},... | collective-permute-start | bytes 2359304 | tf_op jit(solution)/shard_map/ppermute | solution.py:46
  56.4 17.1 %collective-permute-start.17 = (bf16[2,2,3,4,8,1024]{5,4,3,2,1,0:T(8,128)(2,1)S(1)}, bf16[2,2,3,4,8,1024]{5,4,3,2,1,0:T(8,128)(2,1)S(1)}, u32[]{:S(2)}, u32[]{:S(2)}) collective-permute-start(bf16[2,2,3,4,8,1024]{5,4,3,2,1,0:T(8,128)(2,1)S(1)} %pad_maximum_fusion.3), channel_id=1, source_target_pairs={{0,24},{1,9},{2,26},{3,11},{4,28},{5,13},{6,30},{7,15},{8,16},{9,1... | collective-permute-start | bytes 2359304 | tf_op jit(solution)/shard_map/ppermute | solution.py:46
  66.2 14.7 %collective-permute-start.22 = (bf16[2,2,3,4,8,1024]{5,4,3,2,1,0:T(8,128)(2,1)S(1)}, bf16[2,2,3,4,8,1024]{5,4,3,2,1,0:T(8,128)(2,1)S(1)}, u32[]{:S(2)}, u32[]{:S(2)}) collective-permute-start(bf16[2,2,3,4,8,1024]{5,4,3,2,1,0:T(8,128)(2,1)S(1)} %pad_maximum_fusion.5), channel_id=1, source_target_pairs={{0,6},{1,3},{2,4},{3,1},{4,2},{5,7},{6,0},{7,5},{8,14},{9,11},{10,... | collective-permute-start | bytes 2359304 | tf_op jit(solution)/shard_map/ppermute | solution.py:46
  73.4 10.1 %collective-permute-start.11 = (f32[3,1024,128]{2,1,0:T(8,128)S(1)}, f32[3,1024,128]{2,1,0:T(8,128)S(1)}, u32[]{:S(2)}, u32[]{:S(2)}) collective-permute-start(f32[3,1024,128]{2,1,0:T(8,128)S(1)} %get-tuple-element.85.sums), channel_id=1, source_target_pairs={{0,1},{1,0},{2,3},{3,2},{4,5},{5,4},{6,7},{7,6},{8,9},{9,8},{10,11... | collective-permute-start | bytes 4718600 | tf_op jit(solution)/shard_map/ppermute | solution.py:50
  76.0 10.4 %collective-permute-start.18 = (f32[3,1024,128]{2,1,0:T(8,128)S(1)}, f32[3,1024,128]{2,1,0:T(8,128)S(1)}, u32[]{:S(2)}, u32[]{:S(2)}) collective-permute-start(f32[3,1024,128]{2,1,0:T(8,128)S(1)} %get-tuple-element.91.sums), channel_id=1, source_target_pairs={{0,1},{1,0},{2,3},{3,2},{4,5},{5,4},{6,7},{7,6},{8,9},{9,8},{10,11... | collective-permute-start | bytes 4718600 | tf_op jit(solution)/shard_map/ppermute | solution.py:50
  83.4 5.9 %collective-permute-start.23 = (f32[3,1024,128]{2,1,0:T(8,128)S(1)}, f32[3,1024,128]{2,1,0:T(8,128)S(1)}, u32[]{:S(2)}, u32[]{:S(2)}) collective-permute-start(f32[3,1024,128]{2,1,0:T(8,128)S(1)} %get-tuple-element.97.sums), channel_id=1, source_target_pairs={{0,1},{1,0},{2,3},{3,2},{4,5},{5,4},{6,7},{7,6},{8,9},{9,8},{10,11... | collective-permute-start | bytes 4718600 | tf_op jit(solution)/shard_map/ppermute | solution.py:50
  86.3 12.1 %collective-permute-start.26 = (bf16[2,2,3,32,1024]{4,3,2,1,0:T(8,128)(2,1)S(1)}, bf16[2,2,3,32,1024]{4,3,2,1,0:T(8,128)(2,1)S(1)}, u32[]{:S(2)}, u32[]{:S(2)}) collective-permute-start(bf16[2,2,3,32,1024]{4,3,2,1,0:T(8,128)(2,1)S(1)} %get-tuple-element.110), channel_id=1, source_target_pairs={{0,32},{1,97},{2,34},{3,99},{4,36},{5,101},{6,38},{7,103},{8,40},{... | collective-permute-start | bytes 2359304 | tf_op jit(solution)/shard_map/ppermute | solution.py:46
  89.2 12.8 %collective-permute-start.32 = (bf16[2,2,3,32,1024]{4,3,2,1,0:T(8,128)(2,1)S(1)}, bf16[2,2,3,32,1024]{4,3,2,1,0:T(8,128)(2,1)S(1)}, u32[]{:S(2)}, u32[]{:S(2)}) collective-permute-start(bf16[2,2,3,32,1024]{4,3,2,1,0:T(8,128)(2,1)S(1)} %get-tuple-element.119), channel_id=1, source_target_pairs={{0,8},{1,25},{2,10},{3,27},{4,12},{5,29},{6,14},{7,31},{8,0},{9,17... | collective-permute-start | bytes 2359304 | tf_op jit(solution)/shard_map/ppermute | solution.py:46
  92.1 14.7 %collective-permute-start.38 = (bf16[2,2,3,32,1024]{4,3,2,1,0:T(8,128)(2,1)S(1)}, bf16[2,2,3,32,1024]{4,3,2,1,0:T(8,128)(2,1)S(1)}, u32[]{:S(2)}, u32[]{:S(2)}) collective-permute-start(bf16[2,2,3,32,1024]{4,3,2,1,0:T(8,128)(2,1)S(1)} %get-tuple-element.128), channel_id=1, source_target_pairs={{0,2},{1,7},{2,0},{3,5},{4,6},{5,3},{6,4},{7,1},{8,10},{9,15},{10,... | collective-permute-start | bytes 2359304 | tf_op jit(solution)/shard_map/ppermute | solution.py:46
  98.5 13.5 %collective-permute-start.27 = (bf16[2,2,3,32,1024]{4,3,2,1,0:T(8,128)(2,1)S(1)}, bf16[2,2,3,32,1024]{4,3,2,1,0:T(8,128)(2,1)S(1)}, u32[]{:S(2)}, u32[]{:S(2)}) collective-permute-start(bf16[2,2,3,32,1024]{4,3,2,1,0:T(8,128)(2,1)S(1)} %pad_maximum_fusion.6), channel_id=1, source_target_pairs={{0,96},{1,33},{2,98},{3,35},{4,100},{5,37},{6,102},{7,39},{8,104},... | collective-permute-start | bytes 2359304 | tf_op jit(solution)/shard_map/ppermute | solution.py:46
  102.1 13.3 %collective-permute-start.33 = (bf16[2,2,3,32,1024]{4,3,2,1,0:T(8,128)(2,1)S(1)}, bf16[2,2,3,32,1024]{4,3,2,1,0:T(8,128)(2,1)S(1)}, u32[]{:S(2)}, u32[]{:S(2)}) collective-permute-start(bf16[2,2,3,32,1024]{4,3,2,1,0:T(8,128)(2,1)S(1)} %pad_maximum_fusion.7), channel_id=1, source_target_pairs={{0,24},{1,9},{2,26},{3,11},{4,28},{5,13},{6,30},{7,15},{8,16},{9,1... | collective-permute-start | bytes 2359304 | tf_op jit(solution)/shard_map/ppermute | solution.py:46
  106.9 13.3 %collective-permute-start.39 = (bf16[2,2,3,32,1024]{4,3,2,1,0:T(8,128)(2,1)S(1)}, bf16[2,2,3,32,1024]{4,3,2,1,0:T(8,128)(2,1)S(1)}, u32[]{:S(2)}, u32[]{:S(2)}) collective-permute-start(bf16[2,2,3,32,1024]{4,3,2,1,0:T(8,128)(2,1)S(1)} %pad_maximum_fusion.8), channel_id=1, source_target_pairs={{0,6},{1,3},{2,4},{3,1},{4,2},{5,7},{6,0},{7,5},{8,14},{9,11},{10,... | collective-permute-start | bytes 2359304 | tf_op jit(solution)/shard_map/ppermute | solution.py:46
  113.2 13.5 %collective-permute-start.28 = (bf16[2,3,8,8,1024]{4,3,2,1,0:T(8,128)(2,1)S(1)}, bf16[2,3,8,8,1024]{4,3,2,1,0:T(8,128)(2,1)S(1)}, u32[]{:S(2)}, u32[]{:S(2)}) collective-permute-start(bf16[2,3,8,8,1024]{4,3,2,1,0:T(8,128)(2,1)S(1)} %get-tuple-element.113), channel_id=1, source_target_pairs={{0,24},{1,9},{2,26},{3,11},{4,28},{5,13},{6,30},{7,15},{8,16},{9,1... | collective-permute-start | bytes 2359304 | tf_op jit(solution)/shard_map/ppermute | solution.py:46
  116.6 13.3 %collective-permute-start.34 = (bf16[2,3,8,8,1024]{4,3,2,1,0:T(8,128)(2,1)S(1)}, bf16[2,3,8,8,1024]{4,3,2,1,0:T(8,128)(2,1)S(1)}, u32[]{:S(2)}, u32[]{:S(2)}) collective-permute-start(bf16[2,3,8,8,1024]{4,3,2,1,0:T(8,128)(2,1)S(1)} %get-tuple-element.122), channel_id=1, source_target_pairs={{0,6},{1,3},{2,4},{3,1},{4,2},{5,7},{6,0},{7,5},{8,14},{9,11},{10,... | collective-permute-start | bytes 2359304 | tf_op jit(solution)/shard_map/ppermute | solution.py:46
  121.4 13.3 %collective-permute-start.40 = (bf16[2,3,8,8,1024]{4,3,2,1,0:T(8,128)(2,1)S(1)}, bf16[2,3,8,8,1024]{4,3,2,1,0:T(8,128)(2,1)S(1)}, u32[]{:S(2)}, u32[]{:S(2)}) collective-permute-start(bf16[2,3,8,8,1024]{4,3,2,1,0:T(8,128)(2,1)S(1)} %get-tuple-element.132), channel_id=1, source_target_pairs={{0,96},{1,33},{2,98},{3,35},{4,100},{5,37},{6,102},{7,39},{8,104},... | collective-permute-start | bytes 2359304 | tf_op jit(solution)/shard_map/ppermute | solution.py:46
  124.2 16.1 %collective-permute-start.24 = (bf16[512,1024]{1,0:T(8,128)(2,1)S(1)}, bf16[512,1024]{1,0:T(8,128)(2,1)S(1)}, u32[]{:S(2)}, u32[]{:S(2)}) collective-permute-start(bf16[512,1024]{1,0:T(8,128)(2,1)S(1)} %get-tuple-element.105), channel_id=1, source_target_pairs={{0,1},{1,0},{2,3},{3,2},{4,5},{5,4},{6,7},{7,6},{8,9},{9,8},{10,11... | collective-permute-start | bytes 3145736 | tf_op jit(solution)/shard_map/ppermute | solution.py:50
  124.2 16.1 %collective-permute-start.25 = (bf16[512,1024]{1,0:T(8,128)(2,1)S(1)}, bf16[512,1024]{1,0:T(8,128)(2,1)S(1)}, u32[]{:S(2)}, u32[]{:S(2)}) collective-permute-start(bf16[512,1024]{1,0:T(8,128)(2,1)S(1)} %get-tuple-element.106), channel_id=1, source_target_pairs={{0,1},{1,0},{2,3},{3,2},{4,5},{5,4},{6,7},{7,6},{8,9},{9,8},{10,11... | collective-permute-start | bytes 3145736 | tf_op jit(solution)/shard_map/ppermute | solution.py:50
  126.8 9.5 %collective-permute-start.29 = (bf16[3,8,8,1024]{3,2,1,0:T(8,128)(2,1)S(1)}, bf16[3,8,8,1024]{3,2,1,0:T(8,128)(2,1)S(1)}, u32[]{:S(2)}, u32[]{:S(2)}) collective-permute-start(bf16[3,8,8,1024]{3,2,1,0:T(8,128)(2,1)S(1)} %fusion.2), channel_id=1, source_target_pairs={{0,8},{1,25},{2,10},{3,27},{4,12},{5,29},{6,14},{7,31},{8,0},{9,17... | collective-permute-start | bytes 1179656 | tf_op jit(solution)/shard_map/ppermute | solution.py:46
  130.0 14.8 %collective-permute-start.35 = (bf16[3,8,8,1024]{3,2,1,0:T(8,128)(2,1)S(1)}, bf16[3,8,8,1024]{3,2,1,0:T(8,128)(2,1)S(1)}, u32[]{:S(2)}, u32[]{:S(2)}) collective-permute-start(bf16[3,8,8,1024]{3,2,1,0:T(8,128)(2,1)S(1)} %fusion.1), channel_id=1, source_target_pairs={{0,2},{1,7},{2,0},{3,5},{4,6},{5,3},{6,4},{7,1},{8,10},{9,15},{10,... | collective-permute-start | bytes 1179656 | tf_op jit(solution)/shard_map/ppermute | solution.py:46
  134.8 14.1 %collective-permute-start.41 = (bf16[3,8,8,1024]{3,2,1,0:T(8,128)(2,1)S(1)}, bf16[3,8,8,1024]{3,2,1,0:T(8,128)(2,1)S(1)}, u32[]{:S(2)}, u32[]{:S(2)}) collective-permute-start(bf16[3,8,8,1024]{3,2,1,0:T(8,128)(2,1)S(1)} %fusion), channel_id=1, source_target_pairs={{0,32},{1,97},{2,34},{3,99},{4,36},{5,101},{6,38},{7,103},{8,40},{... | collective-permute-start | bytes 1179656 | tf_op jit(solution)/shard_map/ppermute | solution.py:46
  137.2 14.7 %collective-permute-start.30 = (bf16[2,3,2,8,1024]{4,3,2,1,0:T(8,128)(2,1)S(1)}, bf16[2,3,2,8,1024]{4,3,2,1,0:T(8,128)(2,1)S(1)}, u32[]{:S(2)}, u32[]{:S(2)}) collective-permute-start(bf16[2,3,2,8,1024]{4,3,2,1,0:T(8,128)(2,1)S(1)} %get-tuple-element.116), channel_id=1, source_target_pairs={{0,6},{1,3},{2,4},{3,1},{4,2},{5,7},{6,0},{7,5},{8,14},{9,11},{10,... | collective-permute-start | bytes 589832 | tf_op jit(solution)/shard_map/ppermute | solution.py:46
  145.7 7.6 %collective-permute-start.36 = (bf16[2,3,2,8,1024]{4,3,2,1,0:T(8,128)(2,1)S(1)}, bf16[2,3,2,8,1024]{4,3,2,1,0:T(8,128)(2,1)S(1)}, u32[]{:S(2)}, u32[]{:S(2)}) collective-permute-start(bf16[2,3,2,8,1024]{4,3,2,1,0:T(8,128)(2,1)S(1)} %get-tuple-element.125), channel_id=1, source_target_pairs={{0,96},{1,33},{2,98},{3,35},{4,100},{5,37},{6,102},{7,39},{8,104},... | collective-permute-start | bytes 589832 | tf_op jit(solution)/shard_map/ppermute | solution.py:46
  149.7 11.8 %copy-start.3 = (f32[8,3,6,1024]{3,0,2,1:T(8,128)S(1)}, f32[8,3,6,1024]{3,0,2,1:T(8,128)}, u32[]{:S(2)}) copy-start(f32[8,3,6,1024]{3,0,2,1:T(8,128)} %param.13) | copy-start | bytes 1769476
  149.7 11.8 %copy-start.4 = (f32[8,3,6,1024]{3,0,2,1:T(8,128)S(1)}, f32[8,3,6,1024]{3,0,2,1:T(8,128)}, u32[]{:S(2)}) copy-start(f32[8,3,6,1024]{3,0,2,1:T(8,128)} %param.14) | copy-start | bytes 1769476
  149.7 11.8 %copy-start.5 = (f32[8,3,6,1024]{3,0,2,1:T(8,128)S(1)}, f32[8,3,6,1024]{3,0,2,1:T(8,128)}, u32[]{:S(2)}) copy-start(f32[8,3,6,1024]{3,0,2,1:T(8,128)} %param.15) | copy-start | bytes 1769476
  149.7 7.0 %collective-permute-start.42 = (bf16[2,3,2,8,1024]{4,3,2,1,0:T(8,128)(2,1)S(1)}, bf16[2,3,2,8,1024]{4,3,2,1,0:T(8,128)(2,1)S(1)}, u32[]{:S(2)}, u32[]{:S(2)}) collective-permute-start(bf16[2,3,2,8,1024]{4,3,2,1,0:T(8,128)(2,1)S(1)} %get-tuple-element.135), channel_id=1, source_target_pairs={{0,24},{1,9},{2,26},{3,11},{4,28},{5,13},{6,30},{7,15},{8,16},{9,1... | collective-permute-start | bytes 589832 | tf_op jit(solution)/shard_map/ppermute | solution.py:46
  152.0 4.9 %collective-permute-start.31 = (bf16[3,2,8,1024]{3,2,1,0:T(8,128)(2,1)S(1)}, bf16[3,2,8,1024]{3,2,1,0:T(8,128)(2,1)S(1)}, u32[]{:S(2)}, u32[]{:S(2)}) collective-permute-start(bf16[3,2,8,1024]{3,2,1,0:T(8,128)(2,1)S(1)} %fusion.7), channel_id=1, source_target_pairs={{0,2},{1,7},{2,0},{3,5},{4,6},{5,3},{6,4},{7,1},{8,10},{9,15},{10,... | collective-permute-start | bytes 294920 | tf_op jit(solution)/shard_map/ppermute | solution.py:46
  153.3 4.7 %collective-permute-start.37 = (bf16[3,2,8,1024]{3,2,1,0:T(8,128)(2,1)S(1)}, bf16[3,2,8,1024]{3,2,1,0:T(8,128)(2,1)S(1)}, u32[]{:S(2)}, u32[]{:S(2)}) collective-permute-start(bf16[3,2,8,1024]{3,2,1,0:T(8,128)(2,1)S(1)} %fusion.5), channel_id=1, source_target_pairs={{0,32},{1,97},{2,34},{3,99},{4,36},{5,101},{6,38},{7,103},{8,40},{... | collective-permute-start | bytes 294920 | tf_op jit(solution)/shard_map/ppermute | solution.py:46
  156.7 4.7 %collective-permute-start.43 = (bf16[3,2,8,1024]{3,2,1,0:T(8,128)(2,1)S(1)}, bf16[3,2,8,1024]{3,2,1,0:T(8,128)(2,1)S(1)}, u32[]{:S(2)}, u32[]{:S(2)}) collective-permute-start(bf16[3,2,8,1024]{3,2,1,0:T(8,128)(2,1)S(1)} %fusion.3), channel_id=1, source_target_pairs={{0,8},{1,25},{2,10},{3,27},{4,12},{5,29},{6,14},{7,31},{8,0},{9,17... | collective-permute-start | bytes 294920 | tf_op jit(solution)/shard_map/ppermute | solution.py:46
  (3 other events, 8.8 us)

commit v4 on v3

--- a/solution.py
+++ b/solution.py
@@ -425,15 +425,17 @@
     def add(one, came):
         return (one.astype(jnp.float32) + came[1].astype(jnp.float32)).astype(jnp.bfloat16)
 
-    def scatter(parts, axes):
+    def scatter(parts, axes, *also):
         came = [hop(parts[c][2], axes[c], BACK) for c in each]
+        if also:
+            came[2], *also = lax.optimization_barrier((came[2], *also))
         ones = [add(parts[c][1], came[c]) for c in each]
         return [(parts[c][0], came[c], hop(ones[c], axes[c], ONE)) for c in each]
 
     layer_out, input_grad = rows_out(
         table[0], hidden, pair, weights, [swap(r) for r in far_rows], 0
     )
-    merged = scatter(merged, mid)
+    merged = scatter(merged, mid, layer_out, input_grad)
     sums = [unweave(table[c], *merged[c]) for c in each]
     parts = [
         own + came[0].astype(jnp.float32) + one.astype(jnp.float32)

time: 163 us -> 160 us (0.982)
  waiting for transfers between devices: 58.7 us -> 55 us
    ppermute x36, waiting for transfers between devices: 57.9 us -> 54.2 us  [hop(): return lax.ppermute(value, BOTH, step_pairs(axis, offsets))]
where the time goes in v4:
time: 160 us
  starting transfers between devices  63.1 us (39%)
  waiting for transfers between devices  55 us (34%)
  Pallas kernels  34 us (21%)
  other arithmetic  4.48 us (3%)
  local copies, waits for them, and re-layouts  1.71 us (1%)
    ppermute x36, starting transfers between devices, hop(): return lax.ppermute(value, BOTH, step_pairs(axis, offsets))  60.7 us
    ppermute x36, waiting for transfers between devices, hop(): return lax.ppermute(value, BOTH, step_pairs(axis, offsets))  54.2 us
    pallas_call x3, Pallas kernels, second(): pl.pallas_call(second_kernel, out_shape=[shape_of(*lead, 2, 3, 32, column...  8.4 us
    pallas_call x2, Pallas kernels, rows_out(): pl.pallas_call(functools.partial(rows_kernel, start), out_shape=[shape_of...  7.73 us
    pallas_call x3, Pallas kernels, first(): pl.pallas_call(first_kernel, out_shape=[jax.ShapeDtypeStruct((3, rows, 12...  7.38 us
    pallas_call x3, Pallas kernels, merge(): pl.pallas_call(merge_kernel, out_shape=[shape_of(*lead, 3, experts, 8, co...  3.54 us
  transfers between devices with their start and end apart: 44, of which 21 were waited for; matrix products, arithmetic and copies ran while one was open for 2% of the time, Pallas kernels for 21%

profile of v4, /device:TPU:0, one launch (start us, length us, event | category | flops | bytes accessed | tf_op | source)
XLA Modules:
  0.0 159.5 jit_solution(2705983447263251060)
XLA Ops:
  1.7 1.7 %collective-permute-start = (bf16[3,2,8,1024]{3,2,1,0:T(8,128)(2,1)S(1)}, bf16[3,2,8,1024]{3,2,1,0:T(8,128)(2,1)S(1)}, u32[]{:S(2)}, u32[]{:S(2)}) collective-permute-start(bf16[3,2,8,1024]{3,2,1,0:T(8,128)(2,1)S(1)} %get-tuple-element.72.own), channel_id=1, source_target_pairs={{0,2},{1,7},{2,0},{3,5},{4,6},{5,3},{6,4},{7,1},{8,10},{9,15},{10,... | collective-permute-start | bytes 294920 | tf_op jit(solution)/shard_map/ppermute | solution.py:46
  3.4 1.6 collective-permute-start.4
  5.0 1.9 %collective-permute-start.12 = (bf16[3,2,8,1024]{3,2,1,0:T(8,128)(2,1)S(1)}, bf16[3,2,8,1024]{3,2,1,0:T(8,128)(2,1)S(1)}, u32[]{:S(2)}, u32[]{:S(2)}) collective-permute-start(bf16[3,2,8,1024]{3,2,1,0:T(8,128)(2,1)S(1)} %get-tuple-element.88.own), channel_id=1, source_target_pairs={{0,32},{1,97},{2,34},{3,99},{4,36},{5,101},{6,38},{7,103},{8,40},{... | collective-permute-start | bytes 294920 | tf_op jit(solution)/shard_map/ppermute | solution.py:46
  8.7 2.2 %collective-permute-start.1 = (bf16[2,3,2,8,1024]{4,3,2,1,0:T(8,128)(2,1)S(1)}, bf16[2,3,2,8,1024]{4,3,2,1,0:T(8,128)(2,1)S(1)}, u32[]{:S(2)}, u32[]{:S(2)}) collective-permute-start(bf16[2,3,2,8,1024]{4,3,2,1,0:T(8,128)(2,1)S(1)} %pad_maximum_fusion.10), channel_id=1, source_target_pairs={{0,6},{1,3},{2,4},{3,1},{4,2},{5,7},{6,0},{7,5},{8,14},{9,11},{10,... | collective-permute-start | bytes 589832 | tf_op jit(solution)/shard_map/ppermute | solution.py:46
  10.9 2.3 %collective-permute-start.5 = (bf16[2,3,2,8,1024]{4,3,2,1,0:T(8,128)(2,1)S(1)}, bf16[2,3,2,8,1024]{4,3,2,1,0:T(8,128)(2,1)S(1)}, u32[]{:S(2)}, u32[]{:S(2)}) collective-permute-start(bf16[2,3,2,8,1024]{4,3,2,1,0:T(8,128)(2,1)S(1)} %pad_maximum_fusion.11), channel_id=1, source_target_pairs={{0,24},{1,9},{2,26},{3,11},{4,28},{5,13},{6,30},{7,15},{8,16},{9,1... | collective-permute-start | bytes 589832 | tf_op jit(solution)/shard_map/ppermute | solution.py:46
  13.2 3.5 %collective-permute-start.13 = (bf16[2,3,2,8,1024]{4,3,2,1,0:T(8,128)(2,1)S(1)}, bf16[2,3,2,8,1024]{4,3,2,1,0:T(8,128)(2,1)S(1)}, u32[]{:S(2)}, u32[]{:S(2)}) collective-permute-start(bf16[2,3,2,8,1024]{4,3,2,1,0:T(8,128)(2,1)S(1)} %pad_maximum_fusion.12), channel_id=1, source_target_pairs={{0,96},{1,33},{2,98},{3,35},{4,100},{5,37},{6,102},{7,39},{8,104},... | collective-permute-start | bytes 589832 | tf_op jit(solution)/shard_map/ppermute | solution.py:46
  21.8 1.1 collective-permute-start.19
  23.0 2.4 %collective-permute-done.2.one = bf16[3,8,8,1024]{3,2,1,0:T(8,128)(2,1)S(1)} collective-permute-done((bf16[3,8,8,1024]{3,2,1,0:T(8,128)(2,1)S(1)}, bf16[3,8,8,1024]{3,2,1,0:T(8,128)(2,1)S(1)}, u32[]{:S(2)}, u32[]{:S(2)}) %collective-permute-start.2) | collective-permute-done | bytes 393248 | tf_op jit(solution)/shard_map/ppermute | solution.py:46
  25.4 1.3 collective-permute-start.3
  26.7 2.3 %collective-permute-done.14.one = bf16[3,8,8,1024]{3,2,1,0:T(8,128)(2,1)S(1)} collective-permute-done((bf16[3,8,8,1024]{3,2,1,0:T(8,128)(2,1)S(1)}, bf16[3,8,8,1024]{3,2,1,0:T(8,128)(2,1)S(1)}, u32[]{:S(2)}, u32[]{:S(2)}) %collective-permute-start.14) | collective-permute-done | bytes 393248 | tf_op jit(solution)/shard_map/ppermute | solution.py:46
  29.0 1.1 collective-permute-start.15
  31.3 3.0 %collective-permute-start.20 = (bf16[2,3,8,8,1024]{4,3,2,1,0:T(8,128)(2,1)S(1)}, bf16[2,3,8,8,1024]{4,3,2,1,0:T(8,128)(2,1)S(1)}, u32[]{:S(2)}, u32[]{:S(2)}) collective-permute-start(bf16[2,3,8,8,1024]{4,3,2,1,0:T(8,128)(2,1)S(1)} %pad_maximum_fusion.4), channel_id=1, source_target_pairs={{0,96},{1,33},{2,98},{3,35},{4,100},{5,37},{6,102},{7,39},{8,104},... | collective-permute-start | bytes 2359304 | tf_op jit(solution)/shard_map/ppermute | solution.py:46
  34.3 4.4 %collective-permute-done.3.rest = bf16[2,3,8,8,1024]{4,3,2,1,0:T(8,128)(2,1)S(1)} collective-permute-done((bf16[2,3,8,8,1024]{4,3,2,1,0:T(8,128)(2,1)S(1)}, bf16[2,3,8,8,1024]{4,3,2,1,0:T(8,128)(2,1)S(1)}, u32[]{:S(2)}, u32[]{:S(2)}) %collective-permute-start.3) | collective-permute-done | bytes 786464 | tf_op jit(solution)/shard_map/ppermute | solution.py:46
  39.8 2.5 %collective-permute-done.15.rest = bf16[2,3,8,8,1024]{4,3,2,1,0:T(8,128)(2,1)S(1)} collective-permute-done((bf16[2,3,8,8,1024]{4,3,2,1,0:T(8,128)(2,1)S(1)}, bf16[2,3,8,8,1024]{4,3,2,1,0:T(8,128)(2,1)S(1)}, u32[]{:S(2)}, u32[]{:S(2)}) %collective-permute-start.15) | collective-permute-done | bytes 786464 | tf_op jit(solution)/shard_map/ppermute | solution.py:46
  43.6 5.2 %collective-permute-done.20.rest = bf16[2,3,8,8,1024]{4,3,2,1,0:T(8,128)(2,1)S(1)} collective-permute-done((bf16[2,3,8,8,1024]{4,3,2,1,0:T(8,128)(2,1)S(1)}, bf16[2,3,8,8,1024]{4,3,2,1,0:T(8,128)(2,1)S(1)}, u32[]{:S(2)}, u32[]{:S(2)}) %collective-permute-start.20) | collective-permute-done | bytes 786464 | tf_op jit(solution)/shard_map/ppermute | solution.py:46
  49.4 3.0 %collective-permute-start.21 = (bf16[2,2,3,4,8,1024]{5,4,3,2,1,0:T(8,128)(2,1)S(1)}, bf16[2,2,3,4,8,1024]{5,4,3,2,1,0:T(8,128)(2,1)S(1)}, u32[]{:S(2)}, u32[]{:S(2)}) collective-permute-start(bf16[2,2,3,4,8,1024]{5,4,3,2,1,0:T(8,128)(2,1)S(1)} %get-tuple-element.96), channel_id=1, source_target_pairs={{0,2},{1,7},{2,0},{3,5},{4,6},{5,3},{6,4},{7,1},{8,10},{9,15},{10,... | collective-permute-start | bytes 2359304 | tf_op jit(solution)/shard_map/ppermute | solution.py:46
  52.5 3.8 %collective-permute-start.10 = (bf16[2,2,3,4,8,1024]{5,4,3,2,1,0:T(8,128)(2,1)S(1)}, bf16[2,2,3,4,8,1024]{5,4,3,2,1,0:T(8,128)(2,1)S(1)}, u32[]{:S(2)}, u32[]{:S(2)}) collective-permute-start(bf16[2,2,3,4,8,1024]{5,4,3,2,1,0:T(8,128)(2,1)S(1)} %pad_maximum_fusion.1), channel_id=1, source_target_pairs={{0,96},{1,33},{2,98},{3,35},{4,100},{5,37},{6,102},{7,39},{8,104},... | collective-permute-start | bytes 2359304 | tf_op jit(solution)/shard_map/ppermute | solution.py:46
  56.4 1.4 collective-permute-start.17
  57.8 8.3 %collective-permute-done.21 = bf16[2,2,3,4,8,1024]{5,4,3,2,1,0:T(8,128)(2,1)S(1)} collective-permute-done((bf16[2,2,3,4,8,1024]{5,4,3,2,1,0:T(8,128)(2,1)S(1)}, bf16[2,2,3,4,8,1024]{5,4,3,2,1,0:T(8,128)(2,1)S(1)}, u32[]{:S(2)}, u32[]{:S(2)}) %collective-permute-start.21) | collective-permute-done | bytes 786464 | tf_op jit(solution)/shard_map/ppermute | solution.py:46
  66.2 4.8 %collective-permute-start.22 = (bf16[2,2,3,4,8,1024]{5,4,3,2,1,0:T(8,128)(2,1)S(1)}, bf16[2,2,3,4,8,1024]{5,4,3,2,1,0:T(8,128)(2,1)S(1)}, u32[]{:S(2)}, u32[]{:S(2)}) collective-permute-start(bf16[2,2,3,4,8,1024]{5,4,3,2,1,0:T(8,128)(2,1)S(1)} %pad_maximum_fusion.5), channel_id=1, source_target_pairs={{0,6},{1,3},{2,4},{3,1},{4,2},{5,7},{6,0},{7,5},{8,14},{9,11},{10,... | collective-permute-start | bytes 2359304 | tf_op jit(solution)/shard_map/ppermute | solution.py:46
  70.9 2.5 %first.3 = (f32[3,1024,128]{2,1,0:T(8,128)S(1)}, bf16[2,3,4,32,1024]{4,3,2,1,0:T(8,128)(2,1)S(1)}) custom-call(s32[9]{0:T(128)S(1)} %get-tuple-element.144.table_ref, bf16[512,2048]{1,0:T(8,128)(2,1)S(1)} %copy-done, bf16[512,1024]{1,0:T(8,128)(2,1)S(1)} %collective-permute-done.6.tok1, bf16[512,2048]{1,0:T(8,128)(2,1)S(1)} %copy-done.1, ...), custom_call_target="tpu_custom_call" | custom-call | tf_op jit(solution)/shard_map/first/pallas_call | solution.py:198
  73.5 2.5 %first.4 = (f32[3,1024,128]{2,1,0:T(8,128)S(1)}, bf16[2,3,4,32,1024]{4,3,2,1,0:T(8,128)(2,1)S(1)}) custom-call(s32[9]{0:T(128)S(1)} %get-tuple-element.142.table_ref, bf16[512,2048]{1,0:T(8,128)(2,1)S(1)} %copy-done, bf16[512,1024]{1,0:T(8,128)(2,1)S(1)} %collective-permute-done.6.tok1, bf16[512,2048]{1,0:T(8,128)(2,1)S(1)} %copy-done.1, ...), custom_call_target="tpu_custom_call" | custom-call | tf_op jit(solution)/shard_map/first/pallas_call | solution.py:198
  76.7 4.2 %collective-permute-done.22 = bf16[2,2,3,4,8,1024]{5,4,3,2,1,0:T(8,128)(2,1)S(1)} collective-permute-done((bf16[2,2,3,4,8,1024]{5,4,3,2,1,0:T(8,128)(2,1)S(1)}, bf16[2,2,3,4,8,1024]{5,4,3,2,1,0:T(8,128)(2,1)S(1)}, u32[]{:S(2)}, u32[]{:S(2)}) %collective-permute-start.22) | collective-permute-done | bytes 786464 | tf_op jit(solution)/shard_map/ppermute | solution.py:46
  80.9 2.5 %first.5 = (f32[3,1024,128]{2,1,0:T(8,128)S(1)}, bf16[2,3,4,32,1024]{4,3,2,1,0:T(8,128)(2,1)S(1)}) custom-call(s32[9]{0:T(128)S(1)} %get-tuple-element.143.table_ref, bf16[512,2048]{1,0:T(8,128)(2,1)S(1)} %copy-done, bf16[512,1024]{1,0:T(8,128)(2,1)S(1)} %collective-permute-done.6.tok1, bf16[512,2048]{1,0:T(8,128)(2,1)S(1)} %copy-done.1, ...), custom_call_target="tpu_custom_call" | custom-call | tf_op jit(solution)/shard_map/first/pallas_call | solution.py:198
  83.5 2.8 %second.3 = (bf16[2,3,32,1024]{3,2,1,0:T(8,128)(2,1)S(1)}, bf16[2,2,3,32,1024]{4,3,2,1,0:T(8,128)(2,1)S(1)}, bf16[2,3,32,1024]{3,2,1,0:T(8,128)(2,1)S(1)}, bf16[...) custom-call(s32[9]{0:T(128)S(1)} %get-tuple-element.144.table_ref, bf16[512,2048]{1,0:T(8,128)(2,1)S(1)} %copy-done, ...), custom_call_target="tpu_custom_call" | custom-call | tf_op jit(solution)/shard_map/second/pallas_call | solution.py:263
  86.4 2.8 %second.4 = (bf16[2,3,32,1024]{3,2,1,0:T(8,128)(2,1)S(1)}, bf16[2,2,3,32,1024]{4,3,2,1,0:T(8,128)(2,1)S(1)}, bf16[2,3,32,1024]{3,2,1,0:T(8,128)(2,1)S(1)}, bf16[...) custom-call(s32[9]{0:T(128)S(1)} %get-tuple-element.142.table_ref, bf16[512,2048]{1,0:T(8,128)(2,1)S(1)} %copy-done, ...), custom_call_target="tpu_custom_call" | custom-call | tf_op jit(solution)/shard_map/second/pallas_call | solution.py:263
  89.3 2.8 %second.5 = (bf16[2,3,32,1024]{3,2,1,0:T(8,128)(2,1)S(1)}, bf16[2,2,3,32,1024]{4,3,2,1,0:T(8,128)(2,1)S(1)}, bf16[2,3,32,1024]{3,2,1,0:T(8,128)(2,1)S(1)}, bf16[...) custom-call(s32[9]{0:T(128)S(1)} %get-tuple-element.143.table_ref, bf16[512,2048]{1,0:T(8,128)(2,1)S(1)} %copy-done, ...), custom_call_target="tpu_custom_call" | custom-call | tf_op jit(solution)/shard_map/second/pallas_call | solution.py:263
  92.2 6.2 %collective-permute-done.26 = bf16[2,2,3,32,1024]{4,3,2,1,0:T(8,128)(2,1)S(1)} collective-permute-done((bf16[2,2,3,32,1024]{4,3,2,1,0:T(8,128)(2,1)S(1)}, bf16[2,2,3,32,1024]{4,3,2,1,0:T(8,128)(2,1)S(1)}, u32[]{:S(2)}, u32[]{:S(2)}) %collective-permute-start.26) | collective-permute-done | bytes 786464 | tf_op jit(solution)/shard_map/ppermute | solution.py:46
  98.5 3.5 %collective-permute-start.27 = (bf16[2,2,3,32,1024]{4,3,2,1,0:T(8,128)(2,1)S(1)}, bf16[2,2,3,32,1024]{4,3,2,1,0:T(8,128)(2,1)S(1)}, u32[]{:S(2)}, u32[]{:S(2)}) collective-permute-start(bf16[2,2,3,32,1024]{4,3,2,1,0:T(8,128)(2,1)S(1)} %pad_maximum_fusion.6), channel_id=1, source_target_pairs={{0,96},{1,33},{2,98},{3,35},{4,100},{5,37},{6,102},{7,39},{8,104},... | collective-permute-start | bytes 2359304 | tf_op jit(solution)/shard_map/ppermute | solution.py:46
  102.1 1.5 collective-permute-start.33
  103.6 3.1 %rows_out.2 = (bf16[512,1024]{1,0:T(8,128)(2,1)S(1)}, bf16[512,1024]{1,0:T(8,128)(2,1)S(1)}) custom-call(s32[9]{0:T(128)S(1)} %get-tuple-element.144.table_ref, bf16[1024,256]{1,0:T(8,128)(2,1)S(1)} %get-tuple-element.87.refs_0_, bf16[1024,256]{1,0:T(8,128)(2,1)S(1)} %get-tuple-element.93.refs_1_, bf16[1024,256]{1,0:T(8,128)(2,1)S(1)} %get-tuple-element.99.refs_2_, ...), custom_call_target="tpu_custom_call" | custom-call | tf_op jit(solution)/shard_map/rows_out/pallas_call | solution.py:321
  106.9 3.0 %collective-permute-start.39 = (bf16[2,2,3,32,1024]{4,3,2,1,0:T(8,128)(2,1)S(1)}, bf16[2,2,3,32,1024]{4,3,2,1,0:T(8,128)(2,1)S(1)}, u32[]{:S(2)}, u32[]{:S(2)}) collective-permute-start(bf16[2,2,3,32,1024]{4,3,2,1,0:T(8,128)(2,1)S(1)} %pad_maximum_fusion.8), channel_id=1, source_target_pairs={{0,6},{1,3},{2,4},{3,1},{4,2},{5,7},{6,0},{7,5},{8,14},{9,11},{10,... | collective-permute-start | bytes 2359304 | tf_op jit(solution)/shard_map/ppermute | solution.py:46
  110.4 1.6 collective-permute-done.27
  112.0 1.2 merge.3
  113.2 1.5 collective-permute-start.28
  115.4 1.2 merge.4
  116.6 3.3 %collective-permute-start.34 = (bf16[2,3,8,8,1024]{4,3,2,1,0:T(8,128)(2,1)S(1)}, bf16[2,3,8,8,1024]{4,3,2,1,0:T(8,128)(2,1)S(1)}, u32[]{:S(2)}, u32[]{:S(2)}) collective-permute-start(bf16[2,3,8,8,1024]{4,3,2,1,0:T(8,128)(2,1)S(1)} %get-tuple-element.123), channel_id=1, source_target_pairs={{0,6},{1,3},{2,4},{3,1},{4,2},{5,7},{6,0},{7,5},{8,14},{9,11},{10,... | collective-permute-start | bytes 2359304 | tf_op jit(solution)/shard_map/ppermute | solution.py:46
  120.2 1.2 merge.5
  121.4 2.8 %collective-permute-start.40 = (bf16[2,3,8,8,1024]{4,3,2,1,0:T(8,128)(2,1)S(1)}, bf16[2,3,8,8,1024]{4,3,2,1,0:T(8,128)(2,1)S(1)}, u32[]{:S(2)}, u32[]{:S(2)}) collective-permute-start(bf16[2,3,8,8,1024]{4,3,2,1,0:T(8,128)(2,1)S(1)} %get-tuple-element.133), channel_id=1, source_target_pairs={{0,96},{1,33},{2,98},{3,35},{4,100},{5,37},{6,102},{7,39},{8,104},... | collective-permute-start | bytes 2359304 | tf_op jit(solution)/shard_map/ppermute | solution.py:46
  124.2 4.6 %rows_out.3 = (bf16[512,2048]{1,0:T(8,128)(2,1)}, bf16[512,2048]{1,0:T(8,128)(2,1)}) custom-call(s32[9]{0:T(128)S(1)} %get-tuple-element.144.table_ref, bf16[1024,256]{1,0:T(8,128)(2,1)S(1)} %get-tuple-element.87.refs_0_, bf16[1024,256]{1,0:T(8,128)(2,1)S(1)} %get-tuple-element.93.refs_1_, bf16[1024,256]{1,0:T(8,128)(2,1)S(1)} %get-tuple-element.99.refs_2_, ...), custom_call_target="tpu_custom_call" | custom-call | tf_op jit(solution)/shard_map/rows_out/pallas_call | solution.py:321
  130.1 4.5 %collective-permute-done.40.came = bf16[2,3,8,8,1024]{4,3,2,1,0:T(8,128)(2,1)S(1)} collective-permute-done((bf16[2,3,8,8,1024]{4,3,2,1,0:T(8,128)(2,1)S(1)}, bf16[2,3,8,8,1024]{4,3,2,1,0:T(8,128)(2,1)S(1)}, u32[]{:S(2)}, u32[]{:S(2)}) %collective-permute-start.40) | collective-permute-done | bytes 786464 | tf_op jit(solution)/shard_map/ppermute | solution.py:46
  134.8 1.6 collective-permute-start.41
  137.6 3.0 %collective-permute-start.30 = (bf16[2,3,2,8,1024]{4,3,2,1,0:T(8,128)(2,1)S(1)}, bf16[2,3,2,8,1024]{4,3,2,1,0:T(8,128)(2,1)S(1)}, u32[]{:S(2)}, u32[]{:S(2)}) collective-permute-start(bf16[2,3,2,8,1024]{4,3,2,1,0:T(8,128)(2,1)S(1)} %get-tuple-element.117), channel_id=1, source_target_pairs={{0,6},{1,3},{2,4},{3,1},{4,2},{5,7},{6,0},{7,5},{8,14},{9,11},{10,... | collective-permute-start | bytes 589832 | tf_op jit(solution)/shard_map/ppermute | solution.py:46
  141.5 2.8 %collective-permute-start.36 = (bf16[2,3,2,8,1024]{4,3,2,1,0:T(8,128)(2,1)S(1)}, bf16[2,3,2,8,1024]{4,3,2,1,0:T(8,128)(2,1)S(1)}, u32[]{:S(2)}, u32[]{:S(2)}) collective-permute-start(bf16[2,3,2,8,1024]{4,3,2,1,0:T(8,128)(2,1)S(1)} %get-tuple-element.126), channel_id=1, source_target_pairs={{0,96},{1,33},{2,98},{3,35},{4,100},{5,37},{6,102},{7,39},{8,104},... | collective-permute-start | bytes 589832 | tf_op jit(solution)/shard_map/ppermute | solution.py:46
  145.2 2.1 %collective-permute-start.42 = (bf16[2,3,2,8,1024]{4,3,2,1,0:T(8,128)(2,1)S(1)}, bf16[2,3,2,8,1024]{4,3,2,1,0:T(8,128)(2,1)S(1)}, u32[]{:S(2)}, u32[]{:S(2)}) collective-permute-start(bf16[2,3,2,8,1024]{4,3,2,1,0:T(8,128)(2,1)S(1)} %get-tuple-element.137), channel_id=1, source_target_pairs={{0,24},{1,9},{2,26},{3,11},{4,28},{5,13},{6,30},{7,15},{8,16},{9,1... | collective-permute-start | bytes 589832 | tf_op jit(solution)/shard_map/ppermute | solution.py:46
  149.4 3.9 %collective-permute-done.42 = bf16[2,3,2,8,1024]{4,3,2,1,0:T(8,128)(2,1)S(1)} collective-permute-done((bf16[2,3,2,8,1024]{4,3,2,1,0:T(8,128)(2,1)S(1)}, bf16[2,3,2,8,1024]{4,3,2,1,0:T(8,128)(2,1)S(1)}, u32[]{:S(2)}, u32[]{:S(2)}) %collective-permute-start.42) | collective-permute-done | bytes 196640 | tf_op jit(solution)/shard_map/ppermute | solution.py:46
  153.5 4.5 %collective-permute-done.43 = bf16[3,2,8,1024]{3,2,1,0:T(8,128)(2,1)S(1)} collective-permute-done((bf16[3,2,8,1024]{3,2,1,0:T(8,128)(2,1)S(1)}, bf16[3,2,8,1024]{3,2,1,0:T(8,128)(2,1)S(1)}, u32[]{:S(2)}, u32[]{:S(2)}) %collective-permute-start.43) | collective-permute-done | bytes 98336 | tf_op jit(solution)/shard_map/ppermute | solution.py:46
  158.0 1.5 divide_subtract_fusion
  (112 shorter events, 22.6 us)
Async XLA Ops:
  1.7 17.0 %copy-start = (bf16[512,2048]{1,0:T(8,128)(2,1)S(1)}, bf16[512,2048]{1,0:T(8,128)(2,1)}, u32[]{:S(2)}) copy-start(bf16[512,2048]{1,0:T(8,128)(2,1)} %tok0.5) | copy-start | bytes 6291460
  1.7 6.9 %collective-permute-start = (bf16[3,2,8,1024]{3,2,1,0:T(8,128)(2,1)S(1)}, bf16[3,2,8,1024]{3,2,1,0:T(8,128)(2,1)S(1)}, u32[]{:S(2)}, u32[]{:S(2)}) collective-permute-start(bf16[3,2,8,1024]{3,2,1,0:T(8,128)(2,1)S(1)} %get-tuple-element.72.own), channel_id=1, source_target_pairs={{0,2},{1,7},{2,0},{3,5},{4,6},{5,3},{6,4},{7,1},{8,10},{9,15},{10,... | collective-permute-start | bytes 294920 | tf_op jit(solution)/shard_map/ppermute | solution.py:46
  3.4 7.5 %collective-permute-start.4 = (bf16[3,2,8,1024]{3,2,1,0:T(8,128)(2,1)S(1)}, bf16[3,2,8,1024]{3,2,1,0:T(8,128)(2,1)S(1)}, u32[]{:S(2)}, u32[]{:S(2)}) collective-permute-start(bf16[3,2,8,1024]{3,2,1,0:T(8,128)(2,1)S(1)} %get-tuple-element.73.own), channel_id=1, source_target_pairs={{0,8},{1,25},{2,10},{3,27},{4,12},{5,29},{6,14},{7,31},{8,0},{9,17... | collective-permute-start | bytes 294920 | tf_op jit(solution)/shard_map/ppermute | solution.py:46
  5.0 8.2 %collective-permute-start.12 = (bf16[3,2,8,1024]{3,2,1,0:T(8,128)(2,1)S(1)}, bf16[3,2,8,1024]{3,2,1,0:T(8,128)(2,1)S(1)}, u32[]{:S(2)}, u32[]{:S(2)}) collective-permute-start(bf16[3,2,8,1024]{3,2,1,0:T(8,128)(2,1)S(1)} %get-tuple-element.88.own), channel_id=1, source_target_pairs={{0,32},{1,97},{2,34},{3,99},{4,36},{5,101},{6,38},{7,103},{8,40},{... | collective-permute-start | bytes 294920 | tf_op jit(solution)/shard_map/ppermute | solution.py:46
  8.7 8.0 %collective-permute-start.1 = (bf16[2,3,2,8,1024]{4,3,2,1,0:T(8,128)(2,1)S(1)}, bf16[2,3,2,8,1024]{4,3,2,1,0:T(8,128)(2,1)S(1)}, u32[]{:S(2)}, u32[]{:S(2)}) collective-permute-start(bf16[2,3,2,8,1024]{4,3,2,1,0:T(8,128)(2,1)S(1)} %pad_maximum_fusion.10), channel_id=1, source_target_pairs={{0,6},{1,3},{2,4},{3,1},{4,2},{5,7},{6,0},{7,5},{8,14},{9,11},{10,... | collective-permute-start | bytes 589832 | tf_op jit(solution)/shard_map/ppermute | solution.py:46
  10.9 7.0 %collective-permute-start.5 = (bf16[2,3,2,8,1024]{4,3,2,1,0:T(8,128)(2,1)S(1)}, bf16[2,3,2,8,1024]{4,3,2,1,0:T(8,128)(2,1)S(1)}, u32[]{:S(2)}, u32[]{:S(2)}) collective-permute-start(bf16[2,3,2,8,1024]{4,3,2,1,0:T(8,128)(2,1)S(1)} %pad_maximum_fusion.11), channel_id=1, source_target_pairs={{0,24},{1,9},{2,26},{3,11},{4,28},{5,13},{6,30},{7,15},{8,16},{9,1... | collective-permute-start | bytes 589832 | tf_op jit(solution)/shard_map/ppermute | solution.py:46
  13.2 7.1 %collective-permute-start.13 = (bf16[2,3,2,8,1024]{4,3,2,1,0:T(8,128)(2,1)S(1)}, bf16[2,3,2,8,1024]{4,3,2,1,0:T(8,128)(2,1)S(1)}, u32[]{:S(2)}, u32[]{:S(2)}) collective-permute-start(bf16[2,3,2,8,1024]{4,3,2,1,0:T(8,128)(2,1)S(1)} %pad_maximum_fusion.12), channel_id=1, source_target_pairs={{0,96},{1,33},{2,98},{3,35},{4,100},{5,37},{6,102},{7,39},{8,104},... | collective-permute-start | bytes 589832 | tf_op jit(solution)/shard_map/ppermute | solution.py:46
  17.5 7.9 %collective-permute-start.2 = (bf16[3,8,8,1024]{3,2,1,0:T(8,128)(2,1)S(1)}, bf16[3,8,8,1024]{3,2,1,0:T(8,128)(2,1)S(1)}, u32[]{:S(2)}, u32[]{:S(2)}) collective-permute-start(bf16[3,8,8,1024]{3,2,1,0:T(8,128)(2,1)S(1)} %weave.3.kept), channel_id=1, source_target_pairs={{0,8},{1,25},{2,10},{3,27},{4,12},{5,29},{6,14},{7,31},{8,0},{9,17... | collective-permute-start | bytes 1179656 | tf_op jit(solution)/shard_map/ppermute | solution.py:46
  18.8 15.5 %collective-permute-start.6 = (bf16[512,1024]{1,0:T(8,128)(2,1)S(1)}, bf16[512,1024]{1,0:T(8,128)(2,1)S(1)}, u32[]{:S(2)}, u32[]{:S(2)}) collective-permute-start(bf16[512,1024]{1,0:T(8,128)(2,1)S(1)} %constant_dynamic-slice_fusion.1), channel_id=1, source_target_pairs={{0,1},{1,0},{2,3},{3,2},{4,5},{5,4},{6,7},{7,6},{8,9},{9,8},{10,11... | collective-permute-start | bytes 3145736 | tf_op jit(solution)/shard_map/ppermute | solution.py:50
  21.1 7.9 %collective-permute-start.14 = (bf16[3,8,8,1024]{3,2,1,0:T(8,128)(2,1)S(1)}, bf16[3,8,8,1024]{3,2,1,0:T(8,128)(2,1)S(1)}, u32[]{:S(2)}, u32[]{:S(2)}) collective-permute-start(bf16[3,8,8,1024]{3,2,1,0:T(8,128)(2,1)S(1)} %weave.5.kept), channel_id=1, source_target_pairs={{0,2},{1,7},{2,0},{3,5},{4,6},{5,3},{6,4},{7,1},{8,10},{9,15},{10,... | collective-permute-start | bytes 1179656 | tf_op jit(solution)/shard_map/ppermute | solution.py:46
  21.7 12.6 %collective-permute-start.7 = (bf16[512,1024]{1,0:T(8,128)(2,1)S(1)}, bf16[512,1024]{1,0:T(8,128)(2,1)S(1)}, u32[]{:S(2)}, u32[]{:S(2)}) collective-permute-start(bf16[512,1024]{1,0:T(8,128)(2,1)S(1)} %constant_dynamic-slice_fusion), channel_id=1, source_target_pairs={{0,1},{1,0},{2,3},{3,2},{4,5},{5,4},{6,7},{7,6},{8,9},{9,8},{10,11... | collective-permute-start | bytes 3145736 | tf_op jit(solution)/shard_map/ppermute | solution.py:50
  21.8 8.3 %collective-permute-start.19 = (bf16[3,8,8,1024]{3,2,1,0:T(8,128)(2,1)S(1)}, bf16[3,8,8,1024]{3,2,1,0:T(8,128)(2,1)S(1)}, u32[]{:S(2)}, u32[]{:S(2)}) collective-permute-start(bf16[3,8,8,1024]{3,2,1,0:T(8,128)(2,1)S(1)} %weave.4.kept), channel_id=1, source_target_pairs={{0,32},{1,97},{2,34},{3,99},{4,36},{5,101},{6,38},{7,103},{8,40},{... | collective-permute-start | bytes 1179656 | tf_op jit(solution)/shard_map/ppermute | solution.py:46
  25.4 13.3 %collective-permute-start.3 = (bf16[2,3,8,8,1024]{4,3,2,1,0:T(8,128)(2,1)S(1)}, bf16[2,3,8,8,1024]{4,3,2,1,0:T(8,128)(2,1)S(1)}, u32[]{:S(2)}, u32[]{:S(2)}) collective-permute-start(bf16[2,3,8,8,1024]{4,3,2,1,0:T(8,128)(2,1)S(1)} %pad_maximum_fusion), channel_id=1, source_target_pairs={{0,24},{1,9},{2,26},{3,11},{4,28},{5,13},{6,30},{7,15},{8,16},{9,1... | collective-permute-start | bytes 2359304 | tf_op jit(solution)/shard_map/ppermute | solution.py:46
  29.0 13.3 %collective-permute-start.15 = (bf16[2,3,8,8,1024]{4,3,2,1,0:T(8,128)(2,1)S(1)}, bf16[2,3,8,8,1024]{4,3,2,1,0:T(8,128)(2,1)S(1)}, u32[]{:S(2)}, u32[]{:S(2)}) collective-permute-start(bf16[2,3,8,8,1024]{4,3,2,1,0:T(8,128)(2,1)S(1)} %pad_maximum_fusion.2), channel_id=1, source_target_pairs={{0,6},{1,3},{2,4},{3,1},{4,2},{5,7},{6,0},{7,5},{8,14},{9,11},{10,... | collective-permute-start | bytes 2359304 | tf_op jit(solution)/shard_map/ppermute | solution.py:46
  30.1 1.2 collective-permute-start.8
  31.3 17.4 %collective-permute-start.20 = (bf16[2,3,8,8,1024]{4,3,2,1,0:T(8,128)(2,1)S(1)}, bf16[2,3,8,8,1024]{4,3,2,1,0:T(8,128)(2,1)S(1)}, u32[]{:S(2)}, u32[]{:S(2)}) collective-permute-start(bf16[2,3,8,8,1024]{4,3,2,1,0:T(8,128)(2,1)S(1)} %pad_maximum_fusion.4), channel_id=1, source_target_pairs={{0,96},{1,33},{2,98},{3,35},{4,100},{5,37},{6,102},{7,39},{8,104},... | collective-permute-start | bytes 2359304 | tf_op jit(solution)/shard_map/ppermute | solution.py:46
  39.5 12.8 %collective-permute-start.9 = (bf16[2,2,3,4,8,1024]{5,4,3,2,1,0:T(8,128)(2,1)S(1)}, bf16[2,2,3,4,8,1024]{5,4,3,2,1,0:T(8,128)(2,1)S(1)}, u32[]{:S(2)}, u32[]{:S(2)}) collective-permute-start(bf16[2,2,3,4,8,1024]{5,4,3,2,1,0:T(8,128)(2,1)S(1)} %get-tuple-element.84), channel_id=1, source_target_pairs={{0,32},{1,97},{2,34},{3,99},{4,36},{5,101},{6,38},{7,103},{8,40},{... | collective-permute-start | bytes 2359304 | tf_op jit(solution)/shard_map/ppermute | solution.py:46
  43.0 13.3 %collective-permute-start.16 = (bf16[2,2,3,4,8,1024]{5,4,3,2,1,0:T(8,128)(2,1)S(1)}, bf16[2,2,3,4,8,1024]{5,4,3,2,1,0:T(8,128)(2,1)S(1)}, u32[]{:S(2)}, u32[]{:S(2)}) collective-permute-start(bf16[2,2,3,4,8,1024]{5,4,3,2,1,0:T(8,128)(2,1)S(1)} %get-tuple-element.90), channel_id=1, source_target_pairs={{0,8},{1,25},{2,10},{3,27},{4,12},{5,29},{6,14},{7,31},{8,0},{9,17... | collective-permute-start | bytes 2359304 | tf_op jit(solution)/shard_map/ppermute | solution.py:46
  49.4 16.7 %collective-permute-start.21 = (bf16[2,2,3,4,8,1024]{5,4,3,2,1,0:T(8,128)(2,1)S(1)}, bf16[2,2,3,4,8,1024]{5,4,3,2,1,0:T(8,128)(2,1)S(1)}, u32[]{:S(2)}, u32[]{:S(2)}) collective-permute-start(bf16[2,2,3,4,8,1024]{5,4,3,2,1,0:T(8,128)(2,1)S(1)} %get-tuple-element.96), channel_id=1, source_target_pairs={{0,2},{1,7},{2,0},{3,5},{4,6},{5,3},{6,4},{7,1},{8,10},{9,15},{10,... | collective-permute-start | bytes 2359304 | tf_op jit(solution)/shard_map/ppermute | solution.py:46
  52.5 18.5 %collective-permute-start.10 = (bf16[2,2,3,4,8,1024]{5,4,3,2,1,0:T(8,128)(2,1)S(1)}, bf16[2,2,3,4,8,1024]{5,4,3,2,1,0:T(8,128)(2,1)S(1)}, u32[]{:S(2)}, u32[]{:S(2)}) collective-permute-start(bf16[2,2,3,4,8,1024]{5,4,3,2,1,0:T(8,128)(2,1)S(1)} %pad_maximum_fusion.1), channel_id=1, source_target_pairs={{0,96},{1,33},{2,98},{3,35},{4,100},{5,37},{6,102},{7,39},{8,104},... | collective-permute-start | bytes 2359304 | tf_op jit(solution)/shard_map/ppermute | solution.py:46
  56.4 17.1 %collective-permute-start.17 = (bf16[2,2,3,4,8,1024]{5,4,3,2,1,0:T(8,128)(2,1)S(1)}, bf16[2,2,3,4,8,1024]{5,4,3,2,1,0:T(8,128)(2,1)S(1)}, u32[]{:S(2)}, u32[]{:S(2)}) collective-permute-start(bf16[2,2,3,4,8,1024]{5,4,3,2,1,0:T(8,128)(2,1)S(1)} %pad_maximum_fusion.3), channel_id=1, source_target_pairs={{0,24},{1,9},{2,26},{3,11},{4,28},{5,13},{6,30},{7,15},{8,16},{9,1... | collective-permute-start | bytes 2359304 | tf_op jit(solution)/shard_map/ppermute | solution.py:46
  66.2 14.7 %collective-permute-start.22 = (bf16[2,2,3,4,8,1024]{5,4,3,2,1,0:T(8,128)(2,1)S(1)}, bf16[2,2,3,4,8,1024]{5,4,3,2,1,0:T(8,128)(2,1)S(1)}, u32[]{:S(2)}, u32[]{:S(2)}) collective-permute-start(bf16[2,2,3,4,8,1024]{5,4,3,2,1,0:T(8,128)(2,1)S(1)} %pad_maximum_fusion.5), channel_id=1, source_target_pairs={{0,6},{1,3},{2,4},{3,1},{4,2},{5,7},{6,0},{7,5},{8,14},{9,11},{10,... | collective-permute-start | bytes 2359304 | tf_op jit(solution)/shard_map/ppermute | solution.py:46
  73.4 10.1 %collective-permute-start.11 = (f32[3,1024,128]{2,1,0:T(8,128)S(1)}, f32[3,1024,128]{2,1,0:T(8,128)S(1)}, u32[]{:S(2)}, u32[]{:S(2)}) collective-permute-start(f32[3,1024,128]{2,1,0:T(8,128)S(1)} %get-tuple-element.86.sums), channel_id=1, source_target_pairs={{0,1},{1,0},{2,3},{3,2},{4,5},{5,4},{6,7},{7,6},{8,9},{9,8},{10,11... | collective-permute-start | bytes 4718600 | tf_op jit(solution)/shard_map/ppermute | solution.py:50
  76.0 10.4 %collective-permute-start.18 = (f32[3,1024,128]{2,1,0:T(8,128)S(1)}, f32[3,1024,128]{2,1,0:T(8,128)S(1)}, u32[]{:S(2)}, u32[]{:S(2)}) collective-permute-start(f32[3,1024,128]{2,1,0:T(8,128)S(1)} %get-tuple-element.92.sums), channel_id=1, source_target_pairs={{0,1},{1,0},{2,3},{3,2},{4,5},{5,4},{6,7},{7,6},{8,9},{9,8},{10,11... | collective-permute-start | bytes 4718600 | tf_op jit(solution)/shard_map/ppermute | solution.py:50
  83.4 5.9 %collective-permute-start.23 = (f32[3,1024,128]{2,1,0:T(8,128)S(1)}, f32[3,1024,128]{2,1,0:T(8,128)S(1)}, u32[]{:S(2)}, u32[]{:S(2)}) collective-permute-start(f32[3,1024,128]{2,1,0:T(8,128)S(1)} %get-tuple-element.98.sums), channel_id=1, source_target_pairs={{0,1},{1,0},{2,3},{3,2},{4,5},{5,4},{6,7},{7,6},{8,9},{9,8},{10,11... | collective-permute-start | bytes 4718600 | tf_op jit(solution)/shard_map/ppermute | solution.py:50
  86.3 12.1 %collective-permute-start.26 = (bf16[2,2,3,32,1024]{4,3,2,1,0:T(8,128)(2,1)S(1)}, bf16[2,2,3,32,1024]{4,3,2,1,0:T(8,128)(2,1)S(1)}, u32[]{:S(2)}, u32[]{:S(2)}) collective-permute-start(bf16[2,2,3,32,1024]{4,3,2,1,0:T(8,128)(2,1)S(1)} %get-tuple-element.111), channel_id=1, source_target_pairs={{0,32},{1,97},{2,34},{3,99},{4,36},{5,101},{6,38},{7,103},{8,40},{... | collective-permute-start | bytes 2359304 | tf_op jit(solution)/shard_map/ppermute | solution.py:46
  89.2 12.8 %collective-permute-start.32 = (bf16[2,2,3,32,1024]{4,3,2,1,0:T(8,128)(2,1)S(1)}, bf16[2,2,3,32,1024]{4,3,2,1,0:T(8,128)(2,1)S(1)}, u32[]{:S(2)}, u32[]{:S(2)}) collective-permute-start(bf16[2,2,3,32,1024]{4,3,2,1,0:T(8,128)(2,1)S(1)} %get-tuple-element.120), channel_id=1, source_target_pairs={{0,8},{1,25},{2,10},{3,27},{4,12},{5,29},{6,14},{7,31},{8,0},{9,17... | collective-permute-start | bytes 2359304 | tf_op jit(solution)/shard_map/ppermute | solution.py:46
  92.1 14.7 %collective-permute-start.38 = (bf16[2,2,3,32,1024]{4,3,2,1,0:T(8,128)(2,1)S(1)}, bf16[2,2,3,32,1024]{4,3,2,1,0:T(8,128)(2,1)S(1)}, u32[]{:S(2)}, u32[]{:S(2)}) collective-permute-start(bf16[2,2,3,32,1024]{4,3,2,1,0:T(8,128)(2,1)S(1)} %get-tuple-element.129), channel_id=1, source_target_pairs={{0,2},{1,7},{2,0},{3,5},{4,6},{5,3},{6,4},{7,1},{8,10},{9,15},{10,... | collective-permute-start | bytes 2359304 | tf_op jit(solution)/shard_map/ppermute | solution.py:46
  98.5 13.5 %collective-permute-start.27 = (bf16[2,2,3,32,1024]{4,3,2,1,0:T(8,128)(2,1)S(1)}, bf16[2,2,3,32,1024]{4,3,2,1,0:T(8,128)(2,1)S(1)}, u32[]{:S(2)}, u32[]{:S(2)}) collective-permute-start(bf16[2,2,3,32,1024]{4,3,2,1,0:T(8,128)(2,1)S(1)} %pad_maximum_fusion.6), channel_id=1, source_target_pairs={{0,96},{1,33},{2,98},{3,35},{4,100},{5,37},{6,102},{7,39},{8,104},... | collective-permute-start | bytes 2359304 | tf_op jit(solution)/shard_map/ppermute | solution.py:46
  102.1 13.3 %collective-permute-start.33 = (bf16[2,2,3,32,1024]{4,3,2,1,0:T(8,128)(2,1)S(1)}, bf16[2,2,3,32,1024]{4,3,2,1,0:T(8,128)(2,1)S(1)}, u32[]{:S(2)}, u32[]{:S(2)}) collective-permute-start(bf16[2,2,3,32,1024]{4,3,2,1,0:T(8,128)(2,1)S(1)} %pad_maximum_fusion.7), channel_id=1, source_target_pairs={{0,24},{1,9},{2,26},{3,11},{4,28},{5,13},{6,30},{7,15},{8,16},{9,1... | collective-permute-start | bytes 2359304 | tf_op jit(solution)/shard_map/ppermute | solution.py:46
  106.9 13.3 %collective-permute-start.39 = (bf16[2,2,3,32,1024]{4,3,2,1,0:T(8,128)(2,1)S(1)}, bf16[2,2,3,32,1024]{4,3,2,1,0:T(8,128)(2,1)S(1)}, u32[]{:S(2)}, u32[]{:S(2)}) collective-permute-start(bf16[2,2,3,32,1024]{4,3,2,1,0:T(8,128)(2,1)S(1)} %pad_maximum_fusion.8), channel_id=1, source_target_pairs={{0,6},{1,3},{2,4},{3,1},{4,2},{5,7},{6,0},{7,5},{8,14},{9,11},{10,... | collective-permute-start | bytes 2359304 | tf_op jit(solution)/shard_map/ppermute | solution.py:46
  109.9 14.2 %collective-permute-start.24 = (bf16[512,1024]{1,0:T(8,128)(2,1)S(1)}, bf16[512,1024]{1,0:T(8,128)(2,1)S(1)}, u32[]{:S(2)}, u32[]{:S(2)}) collective-permute-start(bf16[512,1024]{1,0:T(8,128)(2,1)S(1)} %get-tuple-element.106), channel_id=1, source_target_pairs={{0,1},{1,0},{2,3},{3,2},{4,5},{5,4},{6,7},{7,6},{8,9},{9,8},{10,11... | collective-permute-start | bytes 3145736 | tf_op jit(solution)/shard_map/ppermute | solution.py:50
  109.9 14.2 %collective-permute-start.25 = (bf16[512,1024]{1,0:T(8,128)(2,1)S(1)}, bf16[512,1024]{1,0:T(8,128)(2,1)S(1)}, u32[]{:S(2)}, u32[]{:S(2)}) collective-permute-start(bf16[512,1024]{1,0:T(8,128)(2,1)S(1)} %get-tuple-element.107), channel_id=1, source_target_pairs={{0,1},{1,0},{2,3},{3,2},{4,5},{5,4},{6,7},{7,6},{8,9},{9,8},{10,11... | collective-permute-start | bytes 3145736 | tf_op jit(solution)/shard_map/ppermute | solution.py:50
  113.2 15.6 %collective-permute-start.28 = (bf16[2,3,8,8,1024]{4,3,2,1,0:T(8,128)(2,1)S(1)}, bf16[2,3,8,8,1024]{4,3,2,1,0:T(8,128)(2,1)S(1)}, u32[]{:S(2)}, u32[]{:S(2)}) collective-permute-start(bf16[2,3,8,8,1024]{4,3,2,1,0:T(8,128)(2,1)S(1)} %get-tuple-element.114), channel_id=1, source_target_pairs={{0,24},{1,9},{2,26},{3,11},{4,28},{5,13},{6,30},{7,15},{8,16},{9,1... | collective-permute-start | bytes 2359304 | tf_op jit(solution)/shard_map/ppermute | solution.py:46
  116.6 13.3 %collective-permute-start.34 = (bf16[2,3,8,8,1024]{4,3,2,1,0:T(8,128)(2,1)S(1)}, bf16[2,3,8,8,1024]{4,3,2,1,0:T(8,128)(2,1)S(1)}, u32[]{:S(2)}, u32[]{:S(2)}) collective-permute-start(bf16[2,3,8,8,1024]{4,3,2,1,0:T(8,128)(2,1)S(1)} %get-tuple-element.123), channel_id=1, source_target_pairs={{0,6},{1,3},{2,4},{3,1},{4,2},{5,7},{6,0},{7,5},{8,14},{9,11},{10,... | collective-permute-start | bytes 2359304 | tf_op jit(solution)/shard_map/ppermute | solution.py:46
  121.4 13.3 %collective-permute-start.40 = (bf16[2,3,8,8,1024]{4,3,2,1,0:T(8,128)(2,1)S(1)}, bf16[2,3,8,8,1024]{4,3,2,1,0:T(8,128)(2,1)S(1)}, u32[]{:S(2)}, u32[]{:S(2)}) collective-permute-start(bf16[2,3,8,8,1024]{4,3,2,1,0:T(8,128)(2,1)S(1)} %get-tuple-element.133), channel_id=1, source_target_pairs={{0,96},{1,33},{2,98},{3,35},{4,100},{5,37},{6,102},{7,39},{8,104},... | collective-permute-start | bytes 2359304 | tf_op jit(solution)/shard_map/ppermute | solution.py:46
  128.9 7.9 %collective-permute-start.29 = (bf16[3,8,8,1024]{3,2,1,0:T(8,128)(2,1)S(1)}, bf16[3,8,8,1024]{3,2,1,0:T(8,128)(2,1)S(1)}, u32[]{:S(2)}, u32[]{:S(2)}) collective-permute-start(bf16[3,8,8,1024]{3,2,1,0:T(8,128)(2,1)S(1)} %fusion.2), channel_id=1, source_target_pairs={{0,8},{1,25},{2,10},{3,27},{4,12},{5,29},{6,14},{7,31},{8,0},{9,17... | collective-permute-start | bytes 1179656 | tf_op jit(solution)/shard_map/ppermute | solution.py:46
  130.0 10.6 %collective-permute-start.35 = (bf16[3,8,8,1024]{3,2,1,0:T(8,128)(2,1)S(1)}, bf16[3,8,8,1024]{3,2,1,0:T(8,128)(2,1)S(1)}, u32[]{:S(2)}, u32[]{:S(2)}) collective-permute-start(bf16[3,8,8,1024]{3,2,1,0:T(8,128)(2,1)S(1)} %fusion.1), channel_id=1, source_target_pairs={{0,2},{1,7},{2,0},{3,5},{4,6},{5,3},{6,4},{7,1},{8,10},{9,15},{10,... | collective-permute-start | bytes 1179656 | tf_op jit(solution)/shard_map/ppermute | solution.py:46
  134.8 9.6 %collective-permute-start.41 = (bf16[3,8,8,1024]{3,2,1,0:T(8,128)(2,1)S(1)}, bf16[3,8,8,1024]{3,2,1,0:T(8,128)(2,1)S(1)}, u32[]{:S(2)}, u32[]{:S(2)}) collective-permute-start(bf16[3,8,8,1024]{3,2,1,0:T(8,128)(2,1)S(1)} %fusion), channel_id=1, source_target_pairs={{0,32},{1,97},{2,34},{3,99},{4,36},{5,101},{6,38},{7,103},{8,40},{... | collective-permute-start | bytes 1179656 | tf_op jit(solution)/shard_map/ppermute | solution.py:46
  137.6 9.7 %collective-permute-start.30 = (bf16[2,3,2,8,1024]{4,3,2,1,0:T(8,128)(2,1)S(1)}, bf16[2,3,2,8,1024]{4,3,2,1,0:T(8,128)(2,1)S(1)}, u32[]{:S(2)}, u32[]{:S(2)}) collective-permute-start(bf16[2,3,2,8,1024]{4,3,2,1,0:T(8,128)(2,1)S(1)} %get-tuple-element.117), channel_id=1, source_target_pairs={{0,6},{1,3},{2,4},{3,1},{4,2},{5,7},{6,0},{7,5},{8,14},{9,11},{10,... | collective-permute-start | bytes 589832 | tf_op jit(solution)/shard_map/ppermute | solution.py:46
  141.5 7.0 %collective-permute-start.36 = (bf16[2,3,2,8,1024]{4,3,2,1,0:T(8,128)(2,1)S(1)}, bf16[2,3,2,8,1024]{4,3,2,1,0:T(8,128)(2,1)S(1)}, u32[]{:S(2)}, u32[]{:S(2)}) collective-permute-start(bf16[2,3,2,8,1024]{4,3,2,1,0:T(8,128)(2,1)S(1)} %get-tuple-element.126), channel_id=1, source_target_pairs={{0,96},{1,33},{2,98},{3,35},{4,100},{5,37},{6,102},{7,39},{8,104},... | collective-permute-start | bytes 589832 | tf_op jit(solution)/shard_map/ppermute | solution.py:46
  145.2 12.8 %copy-start.3 = (f32[8,3,6,1024]{3,0,2,1:T(8,128)S(1)}, f32[8,3,6,1024]{3,0,2,1:T(8,128)}, u32[]{:S(2)}) copy-start(f32[8,3,6,1024]{3,0,2,1:T(8,128)} %param.13) | copy-start | bytes 1769476
  145.2 12.8 %copy-start.4 = (f32[8,3,6,1024]{3,0,2,1:T(8,128)S(1)}, f32[8,3,6,1024]{3,0,2,1:T(8,128)}, u32[]{:S(2)}) copy-start(f32[8,3,6,1024]{3,0,2,1:T(8,128)} %param.14) | copy-start | bytes 1769476
  145.2 12.8 %copy-start.5 = (f32[8,3,6,1024]{3,0,2,1:T(8,128)S(1)}, f32[8,3,6,1024]{3,0,2,1:T(8,128)}, u32[]{:S(2)}) copy-start(f32[8,3,6,1024]{3,0,2,1:T(8,128)} %param.15) | copy-start | bytes 1769476
  145.2 8.0 %collective-permute-start.42 = (bf16[2,3,2,8,1024]{4,3,2,1,0:T(8,128)(2,1)S(1)}, bf16[2,3,2,8,1024]{4,3,2,1,0:T(8,128)(2,1)S(1)}, u32[]{:S(2)}, u32[]{:S(2)}) collective-permute-start(bf16[2,3,2,8,1024]{4,3,2,1,0:T(8,128)(2,1)S(1)} %get-tuple-element.137), channel_id=1, source_target_pairs={{0,24},{1,9},{2,26},{3,11},{4,28},{5,13},{6,30},{7,15},{8,16},{9,1... | collective-permute-start | bytes 589832 | tf_op jit(solution)/shard_map/ppermute | solution.py:46
  147.4 6.0 %collective-permute-start.31 = (bf16[3,2,8,1024]{3,2,1,0:T(8,128)(2,1)S(1)}, bf16[3,2,8,1024]{3,2,1,0:T(8,128)(2,1)S(1)}, u32[]{:S(2)}, u32[]{:S(2)}) collective-permute-start(bf16[3,2,8,1024]{3,2,1,0:T(8,128)(2,1)S(1)} %fusion.7), channel_id=1, source_target_pairs={{0,2},{1,7},{2,0},{3,5},{4,6},{5,3},{6,4},{7,1},{8,10},{9,15},{10,... | collective-permute-start | bytes 294920 | tf_op jit(solution)/shard_map/ppermute | solution.py:46
  148.5 5.0 %collective-permute-start.37 = (bf16[3,2,8,1024]{3,2,1,0:T(8,128)(2,1)S(1)}, bf16[3,2,8,1024]{3,2,1,0:T(8,128)(2,1)S(1)}, u32[]{:S(2)}, u32[]{:S(2)}) collective-permute-start(bf16[3,2,8,1024]{3,2,1,0:T(8,128)(2,1)S(1)} %fusion.5), channel_id=1, source_target_pairs={{0,32},{1,97},{2,34},{3,99},{4,36},{5,101},{6,38},{7,103},{8,40},{... | collective-permute-start | bytes 294920 | tf_op jit(solution)/shard_map/ppermute | solution.py:46
  153.3 4.7 %collective-permute-start.43 = (bf16[3,2,8,1024]{3,2,1,0:T(8,128)(2,1)S(1)}, bf16[3,2,8,1024]{3,2,1,0:T(8,128)(2,1)S(1)}, u32[]{:S(2)}, u32[]{:S(2)}) collective-permute-start(bf16[3,2,8,1024]{3,2,1,0:T(8,128)(2,1)S(1)} %fusion.3), channel_id=1, source_target_pairs={{0,8},{1,25},{2,10},{3,27},{4,12},{5,29},{6,14},{7,31},{8,0},{9,17... | collective-permute-start | bytes 294920 | tf_op jit(solution)/shard_map/ppermute | solution.py:46
  (3 other events, 8.8 us)
